TPU v7x, 32 devices: a whole 2x2x4 slice. The times are simulated.
32 devices in a mesh: dp: 8 (over z, x), rep: 4 (over y, core).
Axes of the slice: x: 2, y: 2, z: 4, core: 2. Of those that a mesh axis runs over, the one named last changes fastest.
Arguments:
- embeddings: bfloat16 [32768, 4096], P(('dp', 'rep'))
- assignment: int32 [32768], P(('dp', 'rep')), may hold values from 0 to 7
- block_mask: int32 [256], P(('dp', 'rep')), may hold values from 0 to 1, as said below
- cluster_cap: int32 [8], replicated, may hold values from 12 to 24, as said below
- adjacent: int32 [8], replicated, may hold values from 0 to 7, as said below
Outputs:
- keep: float32 [32768], P(('dp', 'rep'))
Inputs may be any that keep to these rules, and one draw needn't show every extreme that they name: `cluster_cap`: caps are at most 24; in every draw some cluster has cap 24 and 24 or more active documents in every device block. `adjacent`: one cycle through all clusters: each cluster names another one, and is named by exactly one. `block_mask`: every device block of 1024 documents has an active block.
All inputs are finite; a program needn't handle non-finite values.
Results may differ from a plain program's by a relative error of at most 0.0003.
Values may be sent and summed in bfloat16 or wider, within the bound.
No kernel may reach another device: no remote copies, remote signals or barrier semaphores. Data moves between devices by JAX's collectives and lax.ppermute only.
A program may use at most 128 MiB of HBM per device.

v0:
```python
import jax
import jax.numpy as jnp
from jax import lax
from jax.sharding import PartitionSpec as P

CAPS = 24


slope_gain = 64.0
inner_cut = 0.12
edge_cut = 0.06


def unit_rows(embeddings):
    values = embeddings.astype(jnp.float32)
    squares = jnp.sum(values * values, axis=1)
    return (values * lax.rsqrt(squares + 1e-06)[:, None]).astype(jnp.bfloat16)


def score_tile(query_rows, key_rows, key_valid, threshold):
    cos_tile = jnp.einsum("sd,kd->sk", query_rows, key_rows, preferred_element_type=jnp.float32)
    return jax.nn.sigmoid(slope_gain * (cos_tile - threshold)) * key_valid[None, :]


def send_buffers(normed, index_list, dp_count, width_slots, feature_width):
    send_rows = jnp.zeros((dp_count * width_slots, feature_width), jnp.bfloat16)
    send_flags = jnp.zeros((dp_count * width_slots,), jnp.float32)
    for target_index in index_list:
        send_rows = send_rows.at[target_index].set(normed, mode="drop")
        send_flags = send_flags.at[target_index].set(1.0, mode="drop")
    return (
        send_rows.reshape(dp_count, width_slots, feature_width),
        send_flags.astype(jnp.bfloat16).reshape(dp_count, width_slots),
    )


def local(embeddings, assignment, block_mask, cluster_cap, adjacent):
    dp_count = lax.axis_size("dp")
    rows_dev = embeddings.shape[0]
    feature_width = embeddings.shape[1]
    block_rows = rows_dev // block_mask.shape[0]
    cluster_count = cluster_cap.shape[0]
    slot_count = dp_count * CAPS
    normed = unit_rows(embeddings)
    cluster_ids = jnp.arange(cluster_count, dtype=jnp.int32)
    active = jnp.repeat(block_mask, block_rows) == 1
    select_table = (assignment[:, None] == cluster_ids[None, :]).astype(jnp.int32)
    member = select_table * active[:, None].astype(jnp.int32)
    row_rank = jnp.sum((jnp.cumsum(member, axis=0) - member) * member, axis=1)
    row_cap = jnp.sum(select_table * cluster_cap[None, :], axis=1)
    placed = active & (row_rank < row_cap)
    my_cluster = lax.axis_index("dp")
    next_cluster = jnp.sum(adjacent * (cluster_ids == my_cluster))
    before_cluster = jnp.sum(cluster_ids * (adjacent == my_cluster))
    main_index = jnp.where(placed, assignment * CAPS + row_rank, dp_count * CAPS)
    send_rows, send_flags = send_buffers(normed, (main_index,), dp_count, CAPS, feature_width)
    got_rows, got_flags = (
        lax.all_to_all(send_rows, "dp", split_axis=0, concat_axis=0, tiled=True),
        lax.all_to_all(send_flags, "dp", split_axis=0, concat_axis=0, tiled=True),
    )
    own_rows = got_rows.reshape(slot_count, feature_width)
    own_flags = got_flags.reshape(slot_count)
    chosen = jnp.arange(dp_count, dtype=jnp.int32) == before_cluster
    edge_send = jnp.where(chosen[:, None, None], got_rows[:, 0][None], jnp.zeros((), jnp.bfloat16))
    flag_send = jnp.where(chosen[:, None], got_flags[:, 0][None], jnp.zeros((), jnp.bfloat16))
    edge_got, flag_got = (
        lax.all_to_all(edge_send, "dp", split_axis=0, concat_axis=0, tiled=True),
        lax.all_to_all(flag_send, "dp", split_axis=0, concat_axis=0, tiled=True),
    )
    edge_rows = lax.dynamic_index_in_dim(edge_got, next_cluster, 0, keepdims=False)
    edge_flags = lax.dynamic_index_in_dim(flag_got, next_cluster, 0, keepdims=False)
    edge_sum = jnp.sum(
        score_tile(own_rows, edge_rows, edge_flags.astype(jnp.float32), edge_cut), axis=1
    )
    my_lane = lax.axis_index("rep")
    local_ids = jnp.arange(slot_count, dtype=jnp.int32)
    own_index = my_lane * slot_count + local_ids
    piece_rows = lax.all_gather(own_rows, "rep", axis=0, tiled=True)
    piece_flags = lax.all_gather(own_flags, "rep", axis=0, tiled=True)
    column_ids = jnp.arange(piece_rows.shape[0], dtype=jnp.int32)
    weights = score_tile(own_rows, piece_rows, piece_flags.astype(jnp.float32), inner_cut)
    weights = weights * (column_ids[None, :] != own_index[:, None]).astype(jnp.float32)
    inner_sum = jnp.sum(weights, axis=1)
    keep_slots = (1.0 / (1.0 + (inner_sum + edge_sum))).reshape(dp_count, CAPS)
    keep_got = lax.all_to_all(keep_slots, "dp", split_axis=0, concat_axis=0, tiled=True)
    back_index = jnp.where(placed, assignment * CAPS + row_rank, 0)
    return jnp.where(placed, keep_got.reshape(-1)[back_index], 1.0)


def solution(mesh):
    placed = (P(("dp", "rep"), None), P(("dp", "rep")), P(("dp", "rep")), P(), P())
    return jax.shard_map(
        local, mesh=mesh, in_specs=placed, out_specs=P(("dp", "rep")), check_vma=False
    )
```

profile of v0, /device:TPU:0, one launch (start us, length us, event | category | flops | bytes accessed | tf_op | source)
XLA Modules:
  0.0 154.6 jit_solution(4579782534092499973)
XLA Ops:
  6.5 0.0 all-gather.2.cloned.1.call-start
  6.5 0.7 fusion.31
  7.2 0.8 fusion.24
  8.0 2.3 %reduce-window.6 = s32[8,8,128]{2,1,0:T(8,128)S(1)} reduce-window(s32[8,8,128]{2,1,0:T(8,128)S(1)} %fusion.24, s32[]{:T(128)} %constant.18.clone.1), window={size=1x1x128 pad=0_0x0_0x127_0}, to_apply=%region_0.0 | reduce-window | flops 1040384 | bytes 65540 | tf_op jit(solution)/shard_map/reduce-window
  10.2 0.3 slice_reduce_fusion
  10.5 0.2 reduce-window.9
  10.6 0.1 add_bitcast_fusion
  10.7 0.1 bitcast_convert_fusion
  10.8 0.8 select_reduce_fusion
  11.6 0.8 fusion.25
  12.4 0.7 compare_select_fusion.1
  13.1 5.1 %fusion = f32[1024]{0:T(1024)S(1)} fusion(bf16[1024,4096]{1,0:T(8,128)(2,1)} %param.5), kind=kLoop, calls=%fused_computation.5 | loop fusion | flops 12581888 | bytes 8392704 | tf_op jit(solution)/shard_map/reduce_sum | solution.py:16
  18.1 0.0 copy-start
  18.1 0.0 copy-start.1
  18.2 13.4 %scatter_custom_fusion = bf16[192,4096]{1,0:T(8,128)(2,1)S(1)} fusion(s32[1024]{0:T(1024)S(1)} %compare_select_fusion.1, bf16[1024,4096]{1,0:T(8,128)(2,1)} %param.5, f32[1024]{0:T(1024)S(1)} %add_rsqrt_fusion, bf16[]{:T(256)} %constant.22.clone.1), kind=kCustom, calls=%fused_computation.7 | custom fusion | flops 12582912 | bytes 9965570 | tf_op jit(solution)/shard_map/scatter | solution.py:29
  31.6 44.2 %all_to_all.35 = bf16[8,24,4096]{2,1,0:T(8,128)(2,1)} all-to-all(bf16[8,24,4096]{2,1,0:T(8,128)(2,1)S(1)} %bitcast.37), channel_id=1, replica_groups=mesh['dp'=8,'rep'=4] {'dp'}, dimensions={0} | all-to-all | bytes 3145728 | tf_op jit(solution)/shard_map/all_to_all | solution.py:58
  75.8 0.0 all-gather.2.cloned.1.call-update
  75.8 4.3 %scatter_custom_fusion.1 = f32[192]{0:T(256)S(1)} fusion(s32[1024]{0:T(1024)S(1)} %compare_select_fusion.1, f32[1024]{0:T(1024)S(1)} %broadcast.152, f32[]{:T(128)} %constant.25.clone.1), kind=kCustom, calls=%fused_computation.60 | custom fusion | bytes 772 | tf_op jit(solution)/shard_map/scatter | solution.py:30
  80.1 0.7 all_to_all.29
  80.8 3.6 %all-to-all-start.1 = ((bf16[8,1,24]{2,1,0:T(2,128)(2,1)}), bf16[8,1,24]{2,1,0:T(2,128)(2,1)S(1)}, u32[]{:S(2)}, u32[]{:S(2)}) async-start(bf16[8,1,24]{2,1,0:T(2,128)(2,1)} %all_to_all.29), calls=%async_computation.1 | async-start | bytes 8192 | tf_op jit(solution)/shard_map/all_to_all | solution.py:59
  84.4 0.0 copy-done
  84.4 0.7 fusion.27
  85.1 0.6 iota_compare_fusion.3
  85.7 5.1 %all-to-all-done.1 = bf16[8,1,24]{2,1,0:T(2,128)(2,1)S(1)} async-done(((bf16[8,1,24]{2,1,0:T(2,128)(2,1)}), bf16[8,1,24]{2,1,0:T(2,128)(2,1)S(1)}, u32[]{:S(2)}, u32[]{:S(2)}) %all-to-all-start.1) | async-done | bytes 416 | tf_op jit(solution)/shard_map/all_to_all | solution.py:59
  90.8 0.1 slice_reduce_fusion.1
  90.9 0.7 broadcast_select_fusion.1
  91.6 3.3 %all-to-all-start.3 = ((bf16[8,1,8]{2,1,0:T(2,128)(2,1)}), bf16[8,1,8]{2,1,0:T(2,128)(2,1)S(1)}, u32[]{:S(2)}, u32[]{:S(2)}) async-start(bf16[8,1,8]{2,1,0:T(2,128)(2,1)} %broadcast_select_fusion.1), calls=%async_computation.3 | async-start | bytes 8192 | tf_op jit(solution)/shard_map/all_to_all | solution.py:68
  94.9 1.1 slice.19
  96.0 0.1 copy.15
  96.1 0.9 broadcast_select_fusion
  97.0 4.2 %all-to-all-done.3 = bf16[8,1,8]{2,1,0:T(2,128)(2,1)S(1)} async-done(((bf16[8,1,8]{2,1,0:T(2,128)(2,1)}), bf16[8,1,8]{2,1,0:T(2,128)(2,1)S(1)}, u32[]{:S(2)}, u32[]{:S(2)}) %all-to-all-start.3) | async-done | bytes 160 | tf_op jit(solution)/shard_map/all_to_all | solution.py:68
  101.2 3.5 %all-to-all-start.2 = ((bf16[8,8,4096]{2,1,0:T(8,128)(2,1)}), bf16[8,8,4096]{2,1,0:T(8,128)(2,1)S(1)}, u32[]{:S(2)}, u32[]{:S(2)}) async-start(bf16[8,8,4096]{2,1,0:T(8,128)(2,1)} %broadcast_select_fusion), calls=%async_computation.2 | async-start | bytes 1048576 | tf_op jit(solution)/shard_map/all_to_all | solution.py:67
  106.4 0.0 copy-done.1
  106.4 0.6 dynamic-slice.1
  107.7 0.1 reshape.195
  107.8 0.2 dynamic-update-slice
  108.1 6.3 %all-reduce = bf16[768]{0:T(1024)(128)(2,1)S(1)} all-reduce(bf16[768]{0:T(1024)(128)(2,1)S(1)} %dynamic-update-slice), channel_id=1, replica_groups=mesh['dp'=8,'rep'=4] {'rep'}, use_global_device_ids=true, to_apply=%add | all-reduce | flops 768 | bytes 3072
  114.4 2.1 %all-to-all-done.2 = bf16[8,8,4096]{2,1,0:T(8,128)(2,1)S(1)} async-done(((bf16[8,8,4096]{2,1,0:T(8,128)(2,1)}), bf16[8,8,4096]{2,1,0:T(8,128)(2,1)S(1)}, u32[]{:S(2)}, u32[]{:S(2)}) %all-to-all-start.2) | async-done | bytes 524320 | tf_op jit(solution)/shard_map/all_to_all | solution.py:67
  116.5 1.9 %fusion.19 = f32[192]{0:T(256)S(1)} fusion(bf16[192,4096]{1,0:T(8,128)(2,1)} %bitcast.35, bf16[8,8,4096]{2,1,0:T(8,128)(2,1)S(1)} %all-to-all-done.2, s32[]{:T(128)S(6)} %select_n.42, f32[8]{0:T(128)S(1)} %bitcast_convert_fusion.1), kind=kOutput, calls=%fused_computation.25 | convolution fusion | flops 12593472 | bytes 1639684 | tf_op jit(solution)/shard_map/sd,kd->sk/dot_general | solution.py:21
  118.4 3.1 %all-gather.2.cloned.1.call-done = bf16[768,4096]{1,0:T(8,128)(2,1)} async-done(((bf16[192,4096]{1,0:T(8,128)(2,1)}), bf16[768,4096]{1,0:T(8,128)(2,1)}) %all-gather.2.cloned.1.call-update) | async-done | bytes 6291472 | tf_op jit(solution)/shard_map/all_gather | solution.py:78
  121.5 5.7 %fusion.12 = f32[192]{0:T(256)S(1)} fusion(bf16[192,4096]{1,0:T(8,128)(2,1)} %bitcast.36, bf16[768,4096]{1,0:T(8,128)(2,1)} %all-gather.2.cloned.1.call-done, f32[768]{0:T(1024)S(1)} %convert_element_type.43, s32[192]{0:T(256)S(1)} %iota_add_fusion), kind=kOutput, calls=%fused_computation.17 | convolution fusion | flops 1209286400 | bytes 7868928 | tf_op jit(solution)/shard_map/sd,kd->sk/dot_general | solution.py:21
  127.2 0.1 div.23
  127.3 11.8 %all_to_all.36 = f32[8,1,24]{2,1,0:T(1,128)S(1)} all-to-all(f32[8,1,24]{2,1,0:T(1,128)S(1)} %div.23), channel_id=1, replica_groups=mesh['dp'=8,'rep'=4] {'dp'}, dimensions={0} | all-to-all | bytes 1536 | tf_op jit(solution)/shard_map/all_to_all | solution.py:85
  139.1 0.5 broadcast.184
  139.6 0.7 reduce.8
  140.2 0.1 reshape.166
  140.3 6.9 %gather_fusion = f32[1024]{0:T(1024)S(1)} fusion(f32[192]{0:T(256)S(1)} %reshape.166, s32[1024]{0:T(1024)S(1)} %get-tuple-element.9), kind=kCustom, calls=%fused_computation | custom fusion | bytes 12288 | tf_op jit(solution)/shard_map/gather | solution.py:87
  147.2 0.6 broadcast_select_fusion.2
  (10 shorter events, 0.1 us)
Async XLA Ops:
  6.5 115.0 %all-gather.2.cloned.1.call-start = ((), (), s32[]{:S(2)}) async-start(), calls=%async_computation.5 | async-start | bytes 7864320 | tf_op jit(solution)/shard_map/all_gather | solution.py:78
  18.1 66.3 %copy-start = (s32[8]{0:T(128)S(1)}, s32[8]{0:T(128)}, u32[]{:S(2)}) copy-start(s32[8]{0:T(128)} %param.9) | copy-start | bytes 100
  18.1 88.3 %copy-start.1 = (u32[32]{0:T(128)S(1)}, u32[32]{0:T(128)}, u32[]{:S(2)}) copy-start(u32[32]{0:T(128)} %constant.63) | copy-start | bytes 388
  80.8 10.0 %all-to-all-start.1 = ((bf16[8,1,24]{2,1,0:T(2,128)(2,1)}), bf16[8,1,24]{2,1,0:T(2,128)(2,1)S(1)}, u32[]{:S(2)}, u32[]{:S(2)}) async-start(bf16[8,1,24]{2,1,0:T(2,128)(2,1)} %all_to_all.29), calls=%async_computation.1 | async-start | bytes 8192 | tf_op jit(solution)/shard_map/all_to_all | solution.py:59
  91.6 9.6 %all-to-all-start.3 = ((bf16[8,1,8]{2,1,0:T(2,128)(2,1)}), bf16[8,1,8]{2,1,0:T(2,128)(2,1)S(1)}, u32[]{:S(2)}, u32[]{:S(2)}) async-start(bf16[8,1,8]{2,1,0:T(2,128)(2,1)} %broadcast_select_fusion.1), calls=%async_computation.3 | async-start | bytes 8192 | tf_op jit(solution)/shard_map/all_to_all | solution.py:68
  101.2 15.3 %all-to-all-start.2 = ((bf16[8,8,4096]{2,1,0:T(8,128)(2,1)}), bf16[8,8,4096]{2,1,0:T(8,128)(2,1)S(1)}, u32[]{:S(2)}, u32[]{:S(2)}) async-start(bf16[8,8,4096]{2,1,0:T(8,128)(2,1)} %broadcast_select_fusion), calls=%async_computation.2 | async-start | bytes 1048576 | tf_op jit(solution)/shard_map/all_to_all | solution.py:67
Sparse Core Ops, SparseCore 0:
  75.9 45.5 all-gather.1
where the time goes:
time: 155 us
  blocking collectives  62.3 us (40%)
  other arithmetic  29 us (19%)
  between operations  15.9 us (10%)
  local copies, waits for them, and re-layouts  15.1 us (10%)
  waiting for transfers between devices  14.4 us (9%)
  starting transfers between devices  10.4 us (7%)
  matrix products  7.63 us (5%)
    all_to_all x1, blocking collectives, local(): lax.all_to_all(send_rows, 'dp', split_axis=0, concat_axis=0, tiled=True)  44.2 us
    scatter x1, other arithmetic, send_buffers(): send_rows = send_rows.at[target_index].set(normed, mode='drop')  13.4 us
    all_to_all x1, blocking collectives, local(): lax.all_to_all(keep_slots, 'dp', split_axis=0, concat_axis=0, tiled=True)  11.8 us
    dot_general x2, matrix products, score_tile(): jnp.einsum('sd,kd->sk', query_rows, key_rows, preferred_element_type=jnp....  7.63 us
    gather x1, local copies, waits for them, and re-layouts, local(): return jnp.where(placed, keep_got.reshape(-1)[back_index], 1.0)  6.86 us
    unnamed x1, blocking collectives  6.33 us
    reduce_sum x1, other arithmetic, unit_rows(): squares = jnp.sum(values * values, axis=1)  5.07 us
    all_to_all x1, waiting for transfers between devices, local(): lax.all_to_all(send_flags, 'dp', split_axis=0, concat_axis=0, tiled=True)  5.06 us
  transfers between devices with their start and end apart: 4, of which 4 were waited for; matrix products, arithmetic and copies ran while one was open for 7% of the time, Pallas kernels for 0%

commit v1 on v0

v1 whole, which is shorter than its diff:
```python
import functools

import jax
import jax.numpy as jnp
from jax import lax
from jax.experimental import pallas as pl
from jax.experimental.pallas import tpu as pltpu
from jax.sharding import PartitionSpec as P

CAPS = 24
LANES = 128
ALL = ("dp", "rep")
FEATURE_STEP = 512
EMPTY_MARK = 4.0
PENALTY = -1000.0
VMEM_BYTES = 60 * 1024 * 1024

slope_gain = 64.0
inner_cut = 0.12
edge_cut = 0.06


def each(count, body, limit=8):
    if count <= limit:
        for index in range(count):
            body(index)
    else:

        def step(index, carry):
            body(index)
            return carry

        lax.fori_loop(0, count, step, 0)


def iota(shape, dim):
    return lax.broadcasted_iota(jnp.int32, shape, dim)


def select_kernel(
    clusters, reps, cap, adjacent, mask, assign, rows, out, slots, pick, filled, chosen, squares
):
    step = pl.program_id(0)
    blocks = assign.shape[0]
    depth = chosen.shape[1]
    wide = rows.shape[1]
    count = pick.shape[0]
    base = clusters * CAPS

    @pl.when(step == 0)
    def _():
        table = assign[...]
        sub = iota(table.shape, 0)
        active = jnp.zeros(table.shape, jnp.int32)
        for block in range(blocks):
            active = jnp.where(sub == block, mask[block], active)
        live = jnp.where(active == 1, table, -1)
        members = jnp.concatenate(
            [(live == c).astype(jnp.float32) for c in range(clusters)], axis=0
        ).astype(jnp.bfloat16)
        total = clusters * blocks
        earlier = (iota((LANES, LANES), 0) < iota((LANES, LANES), 1)).astype(jnp.bfloat16)
        within = jnp.dot(members, earlier, preferred_element_type=jnp.float32)
        left, right = iota((total, total), 0), iota((total, total), 1)
        same = (left // blocks == right // blocks) & (right < left)
        sums = jnp.dot(
            same.astype(jnp.bfloat16), members, preferred_element_type=jnp.float32
        ).astype(jnp.bfloat16)
        before = jnp.dot(
            sums, jnp.ones((LANES, LANES), jnp.bfloat16), preferred_element_type=jnp.float32
        )
        rank = (within + before).astype(jnp.int32)
        slot = jnp.full(table.shape, -1, jnp.int32)
        for c in range(clusters):
            own = rank[c * blocks : (c + 1) * blocks]
            slot = jnp.where((live == c) & (own < cap[c]), c * CAPS + own, slot)
        slots[...] = slot
        place = iota((count, LANES), 0)
        target = jnp.where(place < base, place, -7)
        for c in range(clusters):
            target = jnp.where(place == base + c, adjacent[c] * CAPS, target)
        seen = jnp.zeros((count, LANES), jnp.float32)
        for block in range(blocks):
            hit = (target == slot[block : block + 1]).astype(jnp.float32)
            pick[:, block * LANES : (block + 1) * LANES] = hit.astype(jnp.bfloat16)
            seen += hit
        filled[...] = seen
        squares[...] = jnp.zeros_like(squares)

    part = jnp.dot(pick[...], rows[...], preferred_element_type=jnp.float32)
    chosen[:, pl.ds(pl.multiple_of(step * wide, wide), wide)] = part
    power = squares[...]
    for k in range(wide // LANES):
        piece = part[:, k * LANES : (k + 1) * LANES]
        power += piece * piece
    squares[...] = power

    @pl.when(step == pl.num_programs(0) - 1)
    def _():
        scale = lax.rsqrt(jnp.sum(squares[...], axis=1, keepdims=True) + 1e-06)
        squares[...] = jnp.broadcast_to(scale, squares.shape)
        mark = jnp.sum(filled[...], axis=1, keepdims=True) < 0.5
        mark = mark & (iota(filled.shape, 1) == 0)
        filled[...] = jnp.where(mark, EMPTY_MARK, 0.0)
        quarter = depth // reps
        tiles = quarter // LANES
        sub = iota((tiles, LANES), 0)

        def eight(group):
            near = pl.ds(pl.multiple_of(base + group * 8, 8), 8)
            near_gain, near_flag = squares[near, :], filled[near, :]
            for k in range(8):
                at = pl.ds(pl.multiple_of((group * 8 + k) * CAPS, 8), CAPS)
                gain, flag = squares[at, :], filled[at, :]
                for q in range(reps):
                    pieces = []
                    edge = jnp.zeros((tiles, LANES), jnp.float32)
                    for t in range(tiles):
                        cols = slice(q * quarter + t * LANES, q * quarter + (t + 1) * LANES)
                        piece = chosen[at, cols] * gain
                        line = chosen[near, cols] * near_gain
                        if t == 0:
                            piece += flag
                            line += near_flag
                        pieces.append(piece)
                        line = jnp.broadcast_to(line[k : k + 1], edge.shape)
                        edge = jnp.where(sub == t, line, edge)
                    pieces.append(edge)
                    chunk = jnp.concatenate(pieces, axis=0).astype(jnp.bfloat16)
                    out[(group * 8 + k) * reps + q] = chunk

        each(clusters // 8, eight, 1)


def gram_kernel(
    ranks, per_set, got, send_far, send_near, keep_far, keep_near, x, edge_rows, edge_x, hold, sem
):
    sources = got.shape[0]
    count, quarter = x.shape
    tiles = quarter // LANES
    blocks = count // LANES
    reps = 4
    main = tiles * CAPS
    me = lax.axis_index("rep")
    my_core, my_y = me % 2, me // 2

    def gather(pair):
        values = [got[2 * pair + k].astype(jnp.float32) for k in range(2)]
        for k in range(2):
            edge_rows[pl.ds((2 * pair + k) * tiles, tiles), :] = values[k][main:]
        for k in range(tiles):
            rows = slice(k * CAPS, (k + 1) * CAPS)
            both = jnp.concatenate([v[rows] for v in values], axis=0)
            x[pl.ds(pair * 2 * CAPS, 2 * CAPS), k * LANES : (k + 1) * LANES] = both.astype(
                jnp.bfloat16
            )

    each(sources // 2, gather, 16)

    for lane in range(reps):
        edge_x[lane * ranks : (lane + 1) * ranks, :] = jnp.concatenate(
            [
                edge_rows[pl.ds(lane * tiles + k, ranks, stride=reps * tiles), :]
                for k in range(tiles)
            ],
            axis=1,
        ).astype(jnp.bfloat16)

    first = (iota((8, LANES), 1) == 0).astype(jnp.bfloat16)
    contract = (((1,), (1,)), ((), ()))
    marks = lax.dot_general(first, x[:, :LANES], contract, preferred_element_type=jnp.float32)
    col_pen = jnp.where(marks[:1] > 2.0, PENALTY, 0.0)

    def put(index, value):
        owner, place = index % reps, index // reps
        slot = 2 * (my_core == owner % 2).astype(jnp.int32) + (my_y == owner // 2).astype(jnp.int32)
        hold[slot, place * LANES : place * LANES + value.shape[0], :] = value

    index = 0
    step = 2 * LANES
    for start in range(0, count, step):
        rows = x[start : start + step, :]
        gram = lax.dot_general(rows, x[start:, :], contract, preferred_element_type=jnp.float32)
        row_pen = jnp.where(rows[:, :1].astype(jnp.float32) > 2.0, PENALTY, 0.0)
        gram = gram + row_pen + col_pen[:, start:]
        shape = (LANES, LANES)
        for half in range(2):
            for tile in range(half, (count - start) // LANES):
                value = gram[
                    half * LANES : (half + 1) * LANES, tile * LANES : (tile + 1) * LANES
                ]
                if tile == half:
                    value = jnp.where(iota(shape, 0) == iota(shape, 1), PENALTY, value)
                put(index, value)
                index += 1

    near = edge_x[...]
    edge = lax.dot_general(near, x[...], contract, preferred_element_type=jnp.float32)
    edge = edge + jnp.where(near[:, :1].astype(jnp.float32) > 2.0, PENALTY, 0.0)
    lane_of = lax.rem(lax.div(iota((ranks, count), 1), CAPS), reps)
    small = edge[:ranks]
    for lane in range(1, reps):
        small = jnp.where(lane_of == lane, edge[lane * ranks : (lane + 1) * ranks], small)
    per_tile = LANES // ranks
    for first_block in range(0, blocks, per_tile):
        stop = min(blocks, first_block + per_tile)
        put(
            index,
            jnp.concatenate(
                [small[:, b * LANES : (b + 1) * LANES] for b in range(first_block, stop)], axis=0
            ),
        )
        index += 1

    copies = [
        pltpu.make_async_copy(hold.at[k], ref, sem.at[k])
        for k, ref in enumerate((send_far, send_near, keep_far, keep_near))
    ]
    for copy in copies:
        copy.start()
    for copy in copies:
        copy.wait()


def score_kernel(ranks, sources, keep, core, far, out, total):
    count = sources * CAPS
    blocks = count // LANES
    reps = 4
    me = lax.axis_index("rep")
    pairs = [(i, j) for i in range(blocks) for j in range(i, blocks)]
    total[...] = jnp.zeros_like(total)

    def value(place, size):
        at = slice(place * LANES, place * LANES + size)
        return keep[at, :] + core[at, :] + far[at, :]

    def by_rep(values):
        picked = jnp.int32(values[0])
        for k in range(1, len(values)):
            picked = jnp.where(me == k, jnp.int32(values[k]), picked)
        return picked

    def tile(place):
        options = [pairs[min(place * reps + k, len(pairs) - 1)] for k in range(reps)]
        i, j = by_rep([p[0] for p in options]), by_rep([p[1] for p in options])
        weight = jax.nn.sigmoid(slope_gain * (value(place, LANES) - inner_cut))
        total[pl.ds(i, 1), :] += jnp.sum(weight.T, axis=0, keepdims=True)
        other = (i != j).astype(jnp.float32)
        total[pl.ds(j, 1), :] += jnp.sum(weight, axis=0, keepdims=True) * other

    per_set = -(-len(pairs) // reps)
    for place in range(per_set):
        if (place + 1) * reps <= len(pairs):
            tile(place)
        else:
            pl.when(place * reps + me < len(pairs))(functools.partial(tile, place))

    per_tile = LANES // ranks
    for e, first_block in enumerate(range(0, blocks, per_tile)):
        owner, place = (len(pairs) + e) % reps, (len(pairs) + e) // reps
        stop = min(blocks, first_block + per_tile)

        @pl.when(me == owner)
        def _(place=place, first_block=first_block, stop=stop):
            edge = value(place, (stop - first_block) * ranks)
            edge = jax.nn.sigmoid(slope_gain * (edge - edge_cut))
            for b in range(first_block, stop):
                at = (b - first_block) * ranks
                total[b : b + 1, :] += jnp.sum(edge[at : at + ranks], axis=0, keepdims=True)

    result = jnp.zeros((sources, LANES), jnp.float32)
    for b in range(blocks):
        where = iota((sources, LANES), 1) + b * LANES
        mine = lax.div(where, CAPS) == iota((sources, LANES), 0)
        spread = jnp.where(mine, total[b : b + 1, :], 0.0)
        move = lax.rem(iota((LANES, LANES), 0) + b * LANES, CAPS) == iota((LANES, LANES), 1)
        result += jnp.dot(
            spread,
            move.astype(jnp.float32),
            precision=lax.Precision.HIGHEST,
            preferred_element_type=jnp.float32,
        )
    out[...] = result


def final_kernel(clusters, reps, slots, sums, out):
    slot = slots[...]
    result = jnp.ones(slot.shape, jnp.float32)
    for c in range(clusters):
        inner = jnp.sum(sums[c * reps : (c + 1) * reps, :], axis=0, keepdims=True)
        keep = jnp.broadcast_to(1.0 / (1.0 + inner), slot.shape)
        rank = slot - c * CAPS
        mine = (rank >= 0) & (rank < CAPS)
        found = jnp.take_along_axis(keep, jnp.where(mine, rank, 0), axis=1)
        result = jnp.where(mine, found, result)
    out[...] = result


def local(embeddings, assignment, block_mask, cluster_cap, adjacent):
    dp_count, reps = lax.axis_size("dp"), lax.axis_size("rep")
    devices = dp_count * reps
    rows_dev, depth = embeddings.shape
    blocks = block_mask.shape[0]
    clusters = cluster_cap.shape[0]
    quarter = depth // reps
    tiles = quarter // LANES
    chunk = tiles * CAPS + tiles
    picks = -(-(clusters * (CAPS + 1)) // 16) * 16
    params = pltpu.CompilerParams(vmem_limit_bytes=VMEM_BYTES)
    smem = pl.BlockSpec(memory_space=pltpu.SMEM)
    vmem = pl.BlockSpec(memory_space=pltpu.VMEM)
    anywhere = pl.BlockSpec(memory_space=pl.ANY)

    send, slots = pl.pallas_call(
        functools.partial(select_kernel, clusters, reps),
        grid=(depth // FEATURE_STEP,),
        in_specs=[
            smem,
            smem,
            smem,
            pl.BlockSpec((blocks, LANES), lambda i: (0, 0)),
            pl.BlockSpec((rows_dev, FEATURE_STEP), lambda i: (0, i)),
        ],
        out_specs=[
            pl.BlockSpec((devices, chunk, LANES), lambda i: (0, 0, 0)),
            pl.BlockSpec((blocks, LANES), lambda i: (0, 0)),
        ],
        out_shape=[
            jax.ShapeDtypeStruct((devices, chunk, LANES), jnp.bfloat16),
            jax.ShapeDtypeStruct((blocks, LANES), jnp.int32),
        ],
        scratch_shapes=[
            pltpu.VMEM((picks, rows_dev), jnp.bfloat16),
            pltpu.VMEM((picks, LANES), jnp.float32),
            pltpu.VMEM((picks, depth), jnp.float32),
            pltpu.VMEM((picks, LANES), jnp.float32),
        ],
        compiler_params=params,
        name="select_rows",
    )(cluster_cap, adjacent, block_mask, assignment.reshape(blocks, LANES), embeddings)

    got = lax.all_to_all(send, ALL, split_axis=0, concat_axis=0, tiled=True)

    count = devices * CAPS
    group = count // LANES
    pairs = group * (group + 1) // 2
    edge_tiles = -(-group // (LANES // dp_count))
    per_set = -(-(pairs + edge_tiles) // reps)
    part = jax.ShapeDtypeStruct((per_set * LANES, LANES), jnp.float32)
    send_far, send_near, keep_far, keep_near = pl.pallas_call(
        functools.partial(gram_kernel, dp_count, per_set),
        in_specs=[vmem],
        out_specs=[anywhere] * 4,
        out_shape=[part] * 4,
        scratch_shapes=[
            pltpu.VMEM((count, quarter), jnp.bfloat16),
            pltpu.VMEM((devices * tiles, LANES), jnp.float32),
            pltpu.VMEM((reps * dp_count, quarter), jnp.bfloat16),
            pltpu.VMEM((4, per_set * LANES, LANES), jnp.float32),
            pltpu.SemaphoreType.DMA((4,)),
        ],
        compiler_params=params,
        name="gram_tiles",
    )(got)

    cores = [(0, 1), (1, 0), (2, 3), (3, 2)]
    across = [(0, 2), (2, 0), (1, 3), (3, 1)]
    core_far = lax.ppermute(send_far, "rep", cores)
    far = lax.ppermute(keep_far + core_far, "rep", across)
    core_near = lax.ppermute(send_near, "rep", cores)

    sums = pl.pallas_call(
        functools.partial(score_kernel, dp_count, devices),
        in_specs=[vmem] * 3,
        out_specs=vmem,
        out_shape=jax.ShapeDtypeStruct((devices, LANES), jnp.float32),
        scratch_shapes=[pltpu.VMEM((-(-group // 8) * 8, LANES), jnp.float32)],
        compiler_params=params,
        name="score_tiles",
    )(keep_near, core_near, far)

    back = lax.all_to_all(sums, ALL, split_axis=0, concat_axis=0, tiled=True)
    keep = pl.pallas_call(
        functools.partial(final_kernel, clusters, reps),
        in_specs=[vmem] * 2,
        out_specs=vmem,
        out_shape=jax.ShapeDtypeStruct((blocks, LANES), jnp.float32),
        compiler_params=params,
        name="final_keep",
    )(slots, back)
    return keep.reshape(rows_dev)


def solution(mesh):
    placed = (P(ALL, None), P(ALL), P(ALL), P(), P())
    return jax.shard_map(local, mesh=mesh, in_specs=placed, out_specs=P(ALL), check_vma=False)
```

time: 155 us -> 89.9 us (0.58)
  other arithmetic: 29 us -> 1.05 us
  Pallas kernels: 0 us -> 17.4 us
  between operations: 15.9 us -> 0.02 us
  local copies, waits for them, and re-layouts: 15.1 us -> 0.76 us
  starting transfers between devices: 10.4 us -> 1.83 us
  matrix products: 7.63 us -> 0 us
  blocking collectives: 62.3 us -> 56.9 us
  waiting for transfers between devices: 14.4 us -> 11.4 us
    pallas_call x0 -> x4, Pallas kernels: none -> 17.4 us  [the longest x1 9.29 us: local(): pl.pallas_call(functools.partial(select_kernel, clusters, reps), grid=(de...]
    scatter x1 -> x0, other arithmetic: 13.4 us -> none  [send_buffers(): send_rows = send_rows.at[target_index].set(normed, mode='drop')]
    ppermute x0 -> x3, waiting for transfers between devices: none -> 11.4 us  [the longest x1 9.95 us: local(): far = lax.ppermute(keep_far + core_far, 'rep', across)]
    all_to_all x3 -> x0, waiting for transfers between devices: 11.3 us -> none  [the longest x1 5.06 us: local(): lax.all_to_all(send_flags, 'dp', split_axis=0, concat_axis=0, tiled=True)]
    all_to_all x3 -> x0, starting transfers between devices: 10.4 us -> none  [the longest x1 3.59 us: local(): lax.all_to_all(send_flags, 'dp', split_axis=0, concat_axis=0, tiled=True)]
    dot_general x2 -> x0, matrix products: 7.63 us -> none  [score_tile(): jnp.einsum('sd,kd->sk', query_rows, key_rows, preferred_element_type=jnp....]
    gather x1 -> x0, local copies, waits for them, and re-layouts: 6.86 us -> none  [local(): return jnp.where(placed, keep_got.reshape(-1)[back_index], 1.0)]
    reduce_sum x3 -> x0, other arithmetic: 6.56 us -> none  [the longest x1 5.07 us: unit_rows(): squares = jnp.sum(values * values, axis=1)]
  transfers between devices with their start and end apart: 4 -> 3, of which waited for: 4 -> 2; matrix products, arithmetic and copies ran while one was open for 7% -> 1% of each run, Pallas kernels for 0% -> 0%
where the time goes in v1:
time: 89.9 us; the launch traced here: 89.4 us
  blocking collectives  56.9 us (63%)
  Pallas kernels  17.4 us (19%)
  waiting for transfers between devices  11.4 us (13%)
  starting transfers between devices  1.83 us (2%)
  other arithmetic  1.05 us (1%)
    all_to_all x1, blocking collectives, local(): got = lax.all_to_all(send, ALL, split_axis=0, concat_axis=0, tiled=True)  46.6 us
    all_to_all x1, blocking collectives, local(): back = lax.all_to_all(sums, ALL, split_axis=0, concat_axis=0, tiled=True)  10.3 us
    ppermute x1, waiting for transfers between devices, local(): far = lax.ppermute(keep_far + core_far, 'rep', across)  9.95 us
    pallas_call x1, Pallas kernels, local(): pl.pallas_call(functools.partial(select_kernel, clusters, reps), grid=(de...  9.29 us
    pallas_call x1, Pallas kernels, local(): pl.pallas_call(functools.partial(gram_kernel, dp_count, per_set), in_spec...  4.1 us
    pallas_call x1, Pallas kernels, local(): pl.pallas_call(functools.partial(score_kernel, dp_count, devices), in_spe...  2.63 us
  transfers between devices with their start and end apart: 3, of which 2 were waited for; matrix products, arithmetic and copies ran while one was open for 1% of the time, Pallas kernels for 0%

profile of v1, /device:TPU:0, one launch (start us, length us, event | category | flops | bytes accessed | tf_op | source)
XLA Modules:
  0.0 89.4 jit_solution(6393620725284963267)
XLA Ops:
  0.0 9.3 %select_rows.1 = (bf16[32,200,128]{2,1,0:T(8,128)(2,1)}, s32[8,128]{1,0:T(8,128)}) custom-call(s32[8]{0:T(128)} %cap.1, s32[8]{0:T(128)} %adjacent.1, s32[8]{0:T(128)} %mask.1, s32[8,128]{1,0:T(8,128)} %bitcast.8, bf16[1024,4096]{1,0:T(8,128)(2,1)} %rows.1), custom_call_target="tpu_custom_call" | custom-call | tf_op jit(solution)/shard_map/select_rows/pallas_call | solution.py:314
  9.3 46.6 %all_to_all.16.got = bf16[32,200,128]{2,1,0:T(8,128)(2,1)} all-to-all(bf16[32,200,128]{2,1,0:T(8,128)(2,1)} %get-tuple-element.12), channel_id=1, replica_groups=mesh['dp'=8,'rep'=4] {'dp','rep'}, dimensions={0} | all-to-all | bytes 3276800 | tf_op jit(solution)/shard_map/all_to_all | solution.py:342
  55.9 4.1 %gram_tiles.1 = (f32[768,128]{1,0:T(8,128)}, f32[768,128]{1,0:T(8,128)}, f32[768,128]{1,0:T(8,128)}, f32[768,128]{1,0:T(8,128)}) custom-call(bf16[32,200,128]{2,1,0:T(8,128)(2,1)} %all_to_all.16.got), custom_call_target="tpu_custom_call" | custom-call | tf_op jit(solution)/shard_map/gram_tiles/pallas_call | solution.py:350
  60.0 0.1 collective-permute-start.1
  60.1 0.5 collective-permute-start
  60.6 1.4 %collective-permute-done.1 = f32[768,128]{1,0:T(8,128)S(1)} collective-permute-done((f32[768,128]{1,0:T(8,128)}, f32[768,128]{1,0:T(8,128)S(1)}, u32[]{:S(2)}, u32[]{:S(2)}) %collective-permute-start.1) | collective-permute-done | bytes 393248 | tf_op jit(solution)/shard_map/ppermute | solution.py:368
  62.0 1.1 %add.3 = f32[768,128]{1,0:T(8,128)S(1)} add(f32[768,128]{1,0:T(8,128)} %get-tuple-element.15, f32[768,128]{1,0:T(8,128)S(1)} %collective-permute-done.1) | non-fusion elementwise | flops 98304 | bytes 1179648 | tf_op jit(solution)/shard_map/add | solution.py:369
  63.1 1.3 %collective-permute-start.2 = (f32[768,128]{1,0:T(8,128)S(1)}, f32[768,128]{1,0:T(8,128)S(1)}, u32[]{:S(2)}, u32[]{:S(2)}) collective-permute-start(f32[768,128]{1,0:T(8,128)S(1)} %add.3), channel_id=1, source_target_pairs={{0,2},{2,0},{1,3},{3,1},{4,6},{6,4},{5,7},{7,5},{8,10},{10,8},{9,1... | collective-permute-start | bytes 1179656 | tf_op jit(solution)/shard_map/ppermute | solution.py:369
  64.3 0.0 collective-permute-done.core
  64.3 0.0 copy-start
  64.3 10.0 %collective-permute-done.2.far = f32[768,128]{1,0:T(8,128)S(1)} collective-permute-done((f32[768,128]{1,0:T(8,128)S(1)}, f32[768,128]{1,0:T(8,128)S(1)}, u32[]{:S(2)}, u32[]{:S(2)}) %collective-permute-start.2) | collective-permute-done | bytes 393248 | tf_op jit(solution)/shard_map/ppermute | solution.py:369
  74.3 0.0 copy-start.1
  74.3 0.0 copy-done
  74.3 0.8 copy-done.1
  75.1 2.6 %score_tiles.1 = f32[32,128]{1,0:T(8,128)} custom-call(f32[768,128]{1,0:T(8,128)} %get-tuple-element.13.keep, f32[768,128]{1,0:T(8,128)} %copy-done, f32[768,128]{1,0:T(8,128)} %copy-done.1), custom_call_target="tpu_custom_call" | custom-call | tf_op jit(solution)/shard_map/score_tiles/pallas_call | solution.py:372
  77.7 10.3 %all_to_all.17 = f32[32,1,128]{2,1,0:T(1,128)} all-to-all(f32[32,1,128]{2,1,0:T(1,128)} %bitcast.6), channel_id=1, replica_groups=mesh['dp'=8,'rep'=4] {'dp','rep'}, dimensions={0} | all-to-all | bytes 32768 | tf_op jit(solution)/shard_map/all_to_all | solution.py:382
  88.0 1.4 %final_keep.1 = f32[8,128]{1,0:T(8,128)} custom-call(s32[8,128]{1,0:T(8,128)} %get-tuple-element.11.slots, f32[32,128]{1,0:T(8,128)} %bitcast.7), custom_call_target="tpu_custom_call" | custom-call | tf_op jit(solution)/shard_map/final_keep/pallas_call | solution.py:383
Async XLA Ops:
  60.0 2.0 %collective-permute-start.1 = (f32[768,128]{1,0:T(8,128)}, f32[768,128]{1,0:T(8,128)S(1)}, u32[]{:S(2)}, u32[]{:S(2)}) collective-permute-start(f32[768,128]{1,0:T(8,128)} %get-tuple-element.16), channel_id=1, source_target_pairs={{0,1},{1,0},{2,3},{3,2},{4,5},{5,4},{6,7},{7,6},{8,9},{9,8},{10,11... | collective-permute-start | bytes 1179656 | tf_op jit(solution)/shard_map/ppermute | solution.py:368
  60.1 4.2 %collective-permute-start = (f32[768,128]{1,0:T(8,128)}, f32[768,128]{1,0:T(8,128)S(1)}, u32[]{:S(2)}, u32[]{:S(2)}) collective-permute-start(f32[768,128]{1,0:T(8,128)} %get-tuple-element.14), channel_id=1, source_target_pairs={{0,1},{1,0},{2,3},{3,2},{4,5},{5,4},{6,7},{7,6},{8,9},{9,8},{10,11... | collective-permute-start | bytes 1179656 | tf_op jit(solution)/shard_map/ppermute | solution.py:370
  63.1 11.2 %collective-permute-start.2 = (f32[768,128]{1,0:T(8,128)S(1)}, f32[768,128]{1,0:T(8,128)S(1)}, u32[]{:S(2)}, u32[]{:S(2)}) collective-permute-start(f32[768,128]{1,0:T(8,128)S(1)} %add.3), channel_id=1, source_target_pairs={{0,2},{2,0},{1,3},{3,1},{4,6},{6,4},{5,7},{7,5},{8,10},{10,8},{9,1... | collective-permute-start | bytes 1179656 | tf_op jit(solution)/shard_map/ppermute | solution.py:369
  64.3 10.0 %copy-start = (f32[768,128]{1,0:T(8,128)}, f32[768,128]{1,0:T(8,128)S(1)}, u32[]{:S(2)}) copy-start(f32[768,128]{1,0:T(8,128)S(1)} %collective-permute-done.core) | copy-start | bytes 1179652
  74.3 0.8 copy-start.1

commit v2 on v1

--- a/solution.py
+++ b/solution.py
@@ -13,7 +13,8 @@
 FEATURE_STEP = 512
 EMPTY_MARK = 4.0
 PENALTY = -1000.0
-VMEM_BYTES = 60 * 1024 * 1024
+SPARE_BYTES = 6 * 1024 * 1024
+SELECT_BYTES = 57 * 1024 * 1024
 
 slope_gain = 64.0
 inner_cut = 0.12
@@ -33,103 +34,131 @@
         lax.fori_loop(0, count, step, 0)
 
 
+def grant(size):
+    return pltpu.CompilerParams(vmem_limit_bytes=size + SPARE_BYTES)
+
+
 def iota(shape, dim):
     return lax.broadcasted_iota(jnp.int32, shape, dim)
 
 
 def select_kernel(
-    clusters, reps, cap, adjacent, mask, assign, rows, out, slots, pick, filled, chosen, squares
+    clusters,
+    reps,
+    cap,
+    adjacent,
+    mask,
+    assign,
+    rows,
+    out,
+    slots,
+    data,
+    pick,
+    filled,
+    chosen,
+    squares,
+    staged,
+    in_sem,
+    out_sem,
 ):
-    step = pl.program_id(0)
+    steps, _, wide = data.shape
+    reads = [
+        pltpu.make_async_copy(rows.at[:, i * wide : (i + 1) * wide], data.at[i], in_sem.at[i])
+        for i in range(steps)
+    ]
+    for read in reads:
+        read.start()
+
     blocks = assign.shape[0]
     depth = chosen.shape[1]
-    wide = rows.shape[1]
     count = pick.shape[0]
     base = clusters * CAPS
-
-    @pl.when(step == 0)
-    def _():
-        table = assign[...]
-        sub = iota(table.shape, 0)
-        active = jnp.zeros(table.shape, jnp.int32)
-        for block in range(blocks):
-            active = jnp.where(sub == block, mask[block], active)
-        live = jnp.where(active == 1, table, -1)
-        members = jnp.concatenate(
-            [(live == c).astype(jnp.float32) for c in range(clusters)], axis=0
-        ).astype(jnp.bfloat16)
-        total = clusters * blocks
-        earlier = (iota((LANES, LANES), 0) < iota((LANES, LANES), 1)).astype(jnp.bfloat16)
-        within = jnp.dot(members, earlier, preferred_element_type=jnp.float32)
-        left, right = iota((total, total), 0), iota((total, total), 1)
-        same = (left // blocks == right // blocks) & (right < left)
-        sums = jnp.dot(
-            same.astype(jnp.bfloat16), members, preferred_element_type=jnp.float32
-        ).astype(jnp.bfloat16)
-        before = jnp.dot(
-            sums, jnp.ones((LANES, LANES), jnp.bfloat16), preferred_element_type=jnp.float32
-        )
-        rank = (within + before).astype(jnp.int32)
-        slot = jnp.full(table.shape, -1, jnp.int32)
-        for c in range(clusters):
-            own = rank[c * blocks : (c + 1) * blocks]
-            slot = jnp.where((live == c) & (own < cap[c]), c * CAPS + own, slot)
-        slots[...] = slot
-        place = iota((count, LANES), 0)
-        target = jnp.where(place < base, place, -7)
-        for c in range(clusters):
-            target = jnp.where(place == base + c, adjacent[c] * CAPS, target)
-        seen = jnp.zeros((count, LANES), jnp.float32)
-        for block in range(blocks):
-            hit = (target == slot[block : block + 1]).astype(jnp.float32)
-            pick[:, block * LANES : (block + 1) * LANES] = hit.astype(jnp.bfloat16)
-            seen += hit
-        filled[...] = seen
-        squares[...] = jnp.zeros_like(squares)
-
-    part = jnp.dot(pick[...], rows[...], preferred_element_type=jnp.float32)
-    chosen[:, pl.ds(pl.multiple_of(step * wide, wide), wide)] = part
-    power = squares[...]
-    for k in range(wide // LANES):
-        piece = part[:, k * LANES : (k + 1) * LANES]
-        power += piece * piece
-    squares[...] = power
-
-    @pl.when(step == pl.num_programs(0) - 1)
-    def _():
-        scale = lax.rsqrt(jnp.sum(squares[...], axis=1, keepdims=True) + 1e-06)
-        squares[...] = jnp.broadcast_to(scale, squares.shape)
-        mark = jnp.sum(filled[...], axis=1, keepdims=True) < 0.5
-        mark = mark & (iota(filled.shape, 1) == 0)
-        filled[...] = jnp.where(mark, EMPTY_MARK, 0.0)
-        quarter = depth // reps
-        tiles = quarter // LANES
-        sub = iota((tiles, LANES), 0)
-
-        def eight(group):
-            near = pl.ds(pl.multiple_of(base + group * 8, 8), 8)
-            near_gain, near_flag = squares[near, :], filled[near, :]
-            for k in range(8):
-                at = pl.ds(pl.multiple_of((group * 8 + k) * CAPS, 8), CAPS)
-                gain, flag = squares[at, :], filled[at, :]
-                for q in range(reps):
-                    pieces = []
-                    edge = jnp.zeros((tiles, LANES), jnp.float32)
-                    for t in range(tiles):
-                        cols = slice(q * quarter + t * LANES, q * quarter + (t + 1) * LANES)
-                        piece = chosen[at, cols] * gain
-                        line = chosen[near, cols] * near_gain
-                        if t == 0:
-                            piece += flag
-                            line += near_flag
-                        pieces.append(piece)
-                        line = jnp.broadcast_to(line[k : k + 1], edge.shape)
-                        edge = jnp.where(sub == t, line, edge)
-                    pieces.append(edge)
-                    chunk = jnp.concatenate(pieces, axis=0).astype(jnp.bfloat16)
-                    out[(group * 8 + k) * reps + q] = chunk
-
-        each(clusters // 8, eight, 1)
+    table = assign[...]
+    sub = iota(table.shape, 0)
+    active = jnp.zeros(table.shape, jnp.int32)
+    for block in range(blocks):
+        active = jnp.where(sub == block, mask[block], active)
+    live = jnp.where(active == 1, table, -1)
+    members = jnp.concatenate(
+        [(live == c).astype(jnp.float32) for c in range(clusters)], axis=0
+    ).astype(jnp.bfloat16)
+    total = clusters * blocks
+    earlier = (iota((LANES, LANES), 0) < iota((LANES, LANES), 1)).astype(jnp.bfloat16)
+    within = jnp.dot(members, earlier, preferred_element_type=jnp.float32)
+    left, right = iota((total, total), 0), iota((total, total), 1)
+    same = (left // blocks == right // blocks) & (right < left)
+    sums = jnp.dot(
+        same.astype(jnp.bfloat16), members, preferred_element_type=jnp.float32
+    ).astype(jnp.bfloat16)
+    before = jnp.dot(
+        sums, jnp.ones((LANES, LANES), jnp.bfloat16), preferred_element_type=jnp.float32
+    )
+    rank = (within + before).astype(jnp.int32)
+    slot = jnp.full(table.shape, -1, jnp.int32)
+    for c in range(clusters):
+        own = rank[c * blocks : (c + 1) * blocks]
+        slot = jnp.where((live == c) & (own < cap[c]), c * CAPS + own, slot)
+    slots[...] = slot
+    place = iota((count, LANES), 0)
+    target = jnp.where(place < base, place, -7)
+    for c in range(clusters):
+        target = jnp.where(place == base + c, adjacent[c] * CAPS, target)
+    seen = jnp.zeros((count, LANES), jnp.float32)
+    for block in range(blocks):
+        hit = (target == slot[block : block + 1]).astype(jnp.float32)
+        pick[:, block * LANES : (block + 1) * LANES] = hit.astype(jnp.bfloat16)
+        seen += hit
+    mark = jnp.sum(seen, axis=1, keepdims=True) < 0.5
+    mark = mark & (iota(filled.shape, 1) == 0)
+    filled[...] = jnp.where(mark, EMPTY_MARK, 0.0)
+
+    power = jnp.zeros(squares.shape, jnp.float32)
+    for i, read in enumerate(reads):
+        read.wait()
+        part = jnp.dot(pick[...], data[i], preferred_element_type=jnp.float32)
+        chosen[:, i * wide : (i + 1) * wide] = part
+        for k in range(wide // LANES):
+            piece = part[:, k * LANES : (k + 1) * LANES]
+            power += piece * piece
+
+    scale = lax.rsqrt(jnp.sum(power, axis=1, keepdims=True) + 1e-06)
+    squares[...] = jnp.broadcast_to(scale, squares.shape)
+    quarter = depth // reps
+    tiles = quarter // LANES
+    sub = iota((tiles, LANES), 0)
+
+    def write(c):
+        at = pl.ds(c * reps, reps)
+        return pltpu.make_async_copy(staged.at[at], out.at[at], out_sem.at[c])
+
+    def eight(group):
+        near = pl.ds(pl.multiple_of(base + group * 8, 8), 8)
+        near_gain, near_flag = squares[near, :], filled[near, :]
+        for k in range(8):
+            c = group * 8 + k
+            at = pl.ds(pl.multiple_of(c * CAPS, 8), CAPS)
+            gain, flag = squares[at, :], filled[at, :]
+            for q in range(reps):
+                pieces = []
+                edge = jnp.zeros((tiles, LANES), jnp.float32)
+                for t in range(tiles):
+                    cols = slice(q * quarter + t * LANES, q * quarter + (t + 1) * LANES)
+                    piece = chosen[at, cols] * gain
+                    line = chosen[near, cols] * near_gain
+                    if t == 0:
+                        piece += flag
+                        line += near_flag
+                    pieces.append(piece)
+                    line = jnp.broadcast_to(line[k : k + 1], edge.shape)
+                    edge = jnp.where(sub == t, line, edge)
+                pieces.append(edge)
+                chunk = jnp.concatenate(pieces, axis=0).astype(jnp.bfloat16)
+                staged[c * reps + q] = chunk
+            write(c).start()
+
+    each(clusters // 8, eight, 1)
+    for c in range(clusters):
+        write(c).wait()
 
 
 def gram_kernel(
@@ -306,36 +335,30 @@
     tiles = quarter // LANES
     chunk = tiles * CAPS + tiles
     picks = -(-(clusters * (CAPS + 1)) // 16) * 16
-    params = pltpu.CompilerParams(vmem_limit_bytes=VMEM_BYTES)
+    steps = depth // FEATURE_STEP
     smem = pl.BlockSpec(memory_space=pltpu.SMEM)
     vmem = pl.BlockSpec(memory_space=pltpu.VMEM)
     anywhere = pl.BlockSpec(memory_space=pl.ANY)
 
     send, slots = pl.pallas_call(
         functools.partial(select_kernel, clusters, reps),
-        grid=(depth // FEATURE_STEP,),
-        in_specs=[
-            smem,
-            smem,
-            smem,
-            pl.BlockSpec((blocks, LANES), lambda i: (0, 0)),
-            pl.BlockSpec((rows_dev, FEATURE_STEP), lambda i: (0, i)),
-        ],
-        out_specs=[
-            pl.BlockSpec((devices, chunk, LANES), lambda i: (0, 0, 0)),
-            pl.BlockSpec((blocks, LANES), lambda i: (0, 0)),
-        ],
+        in_specs=[smem, smem, smem, vmem, anywhere],
+        out_specs=[anywhere, vmem],
         out_shape=[
             jax.ShapeDtypeStruct((devices, chunk, LANES), jnp.bfloat16),
             jax.ShapeDtypeStruct((blocks, LANES), jnp.int32),
         ],
         scratch_shapes=[
+            pltpu.VMEM((steps, rows_dev, FEATURE_STEP), jnp.bfloat16),
             pltpu.VMEM((picks, rows_dev), jnp.bfloat16),
             pltpu.VMEM((picks, LANES), jnp.float32),
             pltpu.VMEM((picks, depth), jnp.float32),
             pltpu.VMEM((picks, LANES), jnp.float32),
+            pltpu.VMEM((devices, chunk, LANES), jnp.bfloat16),
+            pltpu.SemaphoreType.DMA((steps,)),
+            pltpu.SemaphoreType.DMA((clusters,)),
         ],
-        compiler_params=params,
+        compiler_params=pltpu.CompilerParams(vmem_limit_bytes=SELECT_BYTES),
         name="select_rows",
     )(cluster_cap, adjacent, block_mask, assignment.reshape(blocks, LANES), embeddings)
 
@@ -359,14 +382,14 @@
             pltpu.VMEM((4, per_set * LANES, LANES), jnp.float32),
             pltpu.SemaphoreType.DMA((4,)),
         ],
-        compiler_params=params,
+        compiler_params=grant(6 * count * quarter + 4 * per_set * LANES * LANES * 4),
         name="gram_tiles",
     )(got)
 
     cores = [(0, 1), (1, 0), (2, 3), (3, 2)]
     across = [(0, 2), (2, 0), (1, 3), (3, 1)]
     core_far = lax.ppermute(send_far, "rep", cores)
-    far = lax.ppermute(keep_far + core_far, "rep", across)
+    far = lax.ppermute((keep_far + core_far).astype(jnp.float16), "rep", across)
     core_near = lax.ppermute(send_near, "rep", cores)
 
     sums = pl.pallas_call(
@@ -375,9 +398,9 @@
         out_specs=vmem,
         out_shape=jax.ShapeDtypeStruct((devices, LANES), jnp.float32),
         scratch_shapes=[pltpu.VMEM((-(-group // 8) * 8, LANES), jnp.float32)],
-        compiler_params=params,
+        compiler_params=grant(3 * per_set * LANES * LANES * 4),
         name="score_tiles",
-    )(keep_near, core_near, far)
+    )(keep_near, core_near, far.astype(jnp.float32))
 
     back = lax.all_to_all(sums, ALL, split_axis=0, concat_axis=0, tiled=True)
     keep = pl.pallas_call(
@@ -385,7 +408,7 @@
         in_specs=[vmem] * 2,
         out_specs=vmem,
         out_shape=jax.ShapeDtypeStruct((blocks, LANES), jnp.float32),
-        compiler_params=params,
+        compiler_params=grant(0),
         name="final_keep",
     )(slots, back)
     return keep.reshape(rows_dev)

time: 89.9 us -> 76.8 us (0.85)
  Pallas kernels: 17.4 us -> 11 us
  waiting for transfers between devices: 11.4 us -> 6.96 us
  other arithmetic: 1.05 us -> 0.08 us
    ppermute x1, waiting for transfers between devices: 9.95 us -> 5.74 us  [local(): far = lax.ppermute((keep_far + core_far).astype(jnp.float16), 'rep', across)]
    pallas_call x1, Pallas kernels: 9.29 us -> 7.21 us  [local(): pl.pallas_call(functools.partial(select_kernel, clusters, reps), in_specs...]
    pallas_call x1, Pallas kernels: 2.63 us -> 0.8 us  [local(): pl.pallas_call(functools.partial(score_kernel, dp_count, devices), in_spe...]
    pallas_call x1, Pallas kernels: 4.1 us -> 2.29 us  [local(): pl.pallas_call(functools.partial(gram_kernel, dp_count, per_set), in_spec...]
    add x1 -> x0, other arithmetic: 1.05 us -> none  [local(): far = lax.ppermute(keep_far + core_far, 'rep', across)]
  transfers between devices with their start and end apart: 3 -> 3, of which waited for: 2 -> 2; matrix products, arithmetic and copies ran while one was open for 1% -> 0% of each run, Pallas kernels for 0% -> 0%
where the time goes in v2:
time: 76.8 us; the launch traced here: 76.6 us
  blocking collectives  56.7 us (74%)
  Pallas kernels  11 us (14%)
  waiting for transfers between devices  6.96 us (9%)
  starting transfers between devices  1.83 us (2%)
    all_to_all x1, blocking collectives, local(): got = lax.all_to_all(send, ALL, split_axis=0, concat_axis=0, tiled=True)  46.5 us
    all_to_all x1, blocking collectives, local(): back = lax.all_to_all(sums, ALL, split_axis=0, concat_axis=0, tiled=True)  10.1 us
    pallas_call x1, Pallas kernels, local(): pl.pallas_call(functools.partial(select_kernel, clusters, reps), in_specs...  7.21 us
    ppermute x1, waiting for transfers between devices, local(): far = lax.ppermute((keep_far + core_far).astype(jnp.float16), 'rep', across)  5.74 us
    pallas_call x1, Pallas kernels, local(): pl.pallas_call(functools.partial(gram_kernel, dp_count, per_set), in_spec...  2.29 us
  transfers between devices with their start and end apart: 3, of which 2 were waited for; matrix products, arithmetic and copies ran while one was open for 0% of the time, Pallas kernels for 0%

profile of v2, /device:TPU:0, one launch (start us, length us, event | category | flops | bytes accessed | tf_op | source)
XLA Modules:
  0.0 76.6 jit_solution(4334044688629898828)
XLA Ops:
  0.0 7.2 %select_rows.1 = (bf16[32,200,128]{2,1,0:T(8,128)(2,1)}, s32[8,128]{1,0:T(8,128)}) custom-call(s32[8]{0:T(128)} %cap.1, s32[8]{0:T(128)} %adjacent.1, s32[8]{0:T(128)} %mask.1, s32[8,128]{1,0:T(8,128)} %bitcast.8, bf16[1024,4096]{1,0:T(8,128)(2,1)} %rows.1), custom_call_target="tpu_custom_call" | custom-call | tf_op jit(solution)/shard_map/select_rows/pallas_call | solution.py:343
  7.2 46.5 %all_to_all.16.got = bf16[32,200,128]{2,1,0:T(8,128)(2,1)S(1)} all-to-all(bf16[32,200,128]{2,1,0:T(8,128)(2,1)} %get-tuple-element.12), channel_id=1, replica_groups=mesh['dp'=8,'rep'=4] {'dp','rep'}, dimensions={0} | all-to-all | bytes 3276800 | tf_op jit(solution)/shard_map/all_to_all | solution.py:365
  53.7 2.3 %gram_tiles.1 = (f32[768,128]{1,0:T(8,128)S(1)}, f32[768,128]{1,0:T(8,128)S(1)}, f32[768,128]{1,0:T(8,128)S(1)}, f32[768,128]{1,0:T(8,128)S(1)}) custom-call(bf16[32,200,128]{2,1,0:T(8,128)(2,1)S(1)} %all_to_all.16.got), custom_call_target="tpu_custom_call" | custom-call | tf_op jit(solution)/shard_map/gram_tiles/pallas_call | solution.py:373
  56.0 0.0 copy-start
  56.1 0.1 collective-permute-start.1
  56.1 0.5 collective-permute-start
  56.6 1.2 %collective-permute-done.1 = f32[768,128]{1,0:T(8,128)S(1)} collective-permute-done((f32[768,128]{1,0:T(8,128)S(1)}, f32[768,128]{1,0:T(8,128)S(1)}, u32[]{:S(2)}, u32[]{:S(2)}) %collective-permute-start.1) | collective-permute-done | bytes 393248 | tf_op jit(solution)/shard_map/ppermute | solution.py:391
  57.8 0.1 add_convert_fusion
  57.9 1.3 %collective-permute-start.2 = (f16[768,128]{1,0:T(8,128)(2,1)S(1)}, f16[768,128]{1,0:T(8,128)(2,1)S(1)}, u32[]{:S(2)}, u32[]{:S(2)}) collective-permute-start(f16[768,128]{1,0:T(8,128)(2,1)S(1)} %add_convert_fusion), channel_id=1, source_target_pairs={{0,2},{2,0},{1,3},{3,1},{4,6},{6,4},{5,7},{7,5},{8,10},{10,8},{9,1... | collective-permute-start | bytes 589832 | tf_op jit(solution)/shard_map/ppermute | solution.py:392
  59.2 5.7 %collective-permute-done.2 = f16[768,128]{1,0:T(8,128)(2,1)S(1)} collective-permute-done((f16[768,128]{1,0:T(8,128)(2,1)S(1)}, f16[768,128]{1,0:T(8,128)(2,1)S(1)}, u32[]{:S(2)}, u32[]{:S(2)}) %collective-permute-start.2) | collective-permute-done | bytes 196640 | tf_op jit(solution)/shard_map/ppermute | solution.py:392
  64.9 0.0 collective-permute-done.core
  64.9 0.8 %score_tiles.1 = f32[32,128]{1,0:T(8,128)S(1)} custom-call(f32[768,128]{1,0:T(8,128)S(1)} %get-tuple-element.13.keep, f32[768,128]{1,0:T(8,128)S(1)} %collective-permute-done.core, f32[768,128]{1,0:T(8,128)S(1)} %convert_element_type.7.far), custom_call_target="tpu_custom_call" | custom-call | tf_op jit(solution)/shard_map/score_tiles/pallas_call | solution.py:395
  65.7 10.1 %all_to_all.17 = f32[32,1,128]{2,1,0:T(1,128)S(1)} all-to-all(f32[32,1,128]{2,1,0:T(1,128)S(1)} %bitcast.6), channel_id=1, replica_groups=mesh['dp'=8,'rep'=4] {'dp','rep'}, dimensions={0} | all-to-all | bytes 32768 | tf_op jit(solution)/shard_map/all_to_all | solution.py:405
  75.9 0.0 copy-done
  75.9 0.7 final_keep.1
  (1 shorter events, 0.0 us)
Async XLA Ops:
  56.0 19.8 %copy-start = (s32[8,128]{1,0:T(8,128)S(1)}, s32[8,128]{1,0:T(8,128)}, u32[]{:S(2)}) copy-start(s32[8,128]{1,0:T(8,128)} %get-tuple-element.11.slots) | copy-start | bytes 12292
  56.1 1.8 %collective-permute-start.1 = (f32[768,128]{1,0:T(8,128)S(1)}, f32[768,128]{1,0:T(8,128)S(1)}, u32[]{:S(2)}, u32[]{:S(2)}) collective-permute-start(f32[768,128]{1,0:T(8,128)S(1)} %get-tuple-element.16), channel_id=1, source_target_pairs={{0,1},{1,0},{2,3},{3,2},{4,5},{5,4},{6,7},{7,6},{8,9},{9,8},{10,11... | collective-permute-start | bytes 1179656 | tf_op jit(solution)/shard_map/ppermute | solution.py:391
  56.1 8.8 %collective-permute-start = (f32[768,128]{1,0:T(8,128)S(1)}, f32[768,128]{1,0:T(8,128)S(1)}, u32[]{:S(2)}, u32[]{:S(2)}) collective-permute-start(f32[768,128]{1,0:T(8,128)S(1)} %get-tuple-element.14), channel_id=1, source_target_pairs={{0,1},{1,0},{2,3},{3,2},{4,5},{5,4},{6,7},{7,6},{8,9},{9,8},{10,11... | collective-permute-start | bytes 1179656 | tf_op jit(solution)/shard_map/ppermute | solution.py:393
  57.9 7.0 %collective-permute-start.2 = (f16[768,128]{1,0:T(8,128)(2,1)S(1)}, f16[768,128]{1,0:T(8,128)(2,1)S(1)}, u32[]{:S(2)}, u32[]{:S(2)}) collective-permute-start(f16[768,128]{1,0:T(8,128)(2,1)S(1)} %add_convert_fusion), channel_id=1, source_target_pairs={{0,2},{2,0},{1,3},{3,1},{4,6},{6,4},{5,7},{7,5},{8,10},{10,8},{9,1... | collective-permute-start | bytes 589832 | tf_op jit(solution)/shard_map/ppermute | solution.py:392

commit v3 on v2

--- a/solution.py
+++ b/solution.py
@@ -11,10 +11,11 @@
 LANES = 128
 ALL = ("dp", "rep")
 FEATURE_STEP = 512
+ROW_STEP = 256
 EMPTY_MARK = 4.0
 PENALTY = -1000.0
 SPARE_BYTES = 6 * 1024 * 1024
-SELECT_BYTES = 57 * 1024 * 1024
+SELECT_BYTES = 48 * 1024 * 1024
 
 slope_gain = 64.0
 inner_cut = 0.12
@@ -57,13 +58,11 @@
     filled,
     chosen,
     squares,
-    staged,
     in_sem,
-    out_sem,
 ):
-    steps, _, wide = data.shape
+    steps, deep, _ = data.shape
     reads = [
-        pltpu.make_async_copy(rows.at[:, i * wide : (i + 1) * wide], data.at[i], in_sem.at[i])
+        pltpu.make_async_copy(rows.at[i * deep : (i + 1) * deep, :], data.at[i], in_sem.at[i])
         for i in range(steps)
     ]
     for read in reads:
@@ -115,21 +114,23 @@
     power = jnp.zeros(squares.shape, jnp.float32)
     for i, read in enumerate(reads):
         read.wait()
-        part = jnp.dot(pick[...], data[i], preferred_element_type=jnp.float32)
-        chosen[:, i * wide : (i + 1) * wide] = part
-        for k in range(wide // LANES):
-            piece = part[:, k * LANES : (k + 1) * LANES]
-            power += piece * piece
+        chunk_pick = pick[:, i * deep : (i + 1) * deep]
+        for start in range(0, depth, FEATURE_STEP):
+            cols = slice(start, start + FEATURE_STEP)
+            part = jnp.dot(chunk_pick, data[i, :, cols], preferred_element_type=jnp.float32)
+            if i:
+                part += chosen[:, cols]
+            chosen[:, cols] = part
+            if i == steps - 1:
+                for k in range(FEATURE_STEP // LANES):
+                    piece = part[:, k * LANES : (k + 1) * LANES]
+                    power += piece * piece
 
     scale = lax.rsqrt(jnp.sum(power, axis=1, keepdims=True) + 1e-06)
     squares[...] = jnp.broadcast_to(scale, squares.shape)
     quarter = depth // reps
     tiles = quarter // LANES
     sub = iota((tiles, LANES), 0)
-
-    def write(c):
-        at = pl.ds(c * reps, reps)
-        return pltpu.make_async_copy(staged.at[at], out.at[at], out_sem.at[c])
 
     def eight(group):
         near = pl.ds(pl.multiple_of(base + group * 8, 8), 8)
@@ -153,12 +154,9 @@
                     edge = jnp.where(sub == t, line, edge)
                 pieces.append(edge)
                 chunk = jnp.concatenate(pieces, axis=0).astype(jnp.bfloat16)
-                staged[c * reps + q] = chunk
-            write(c).start()
+                out[c * reps + q] = chunk
 
     each(clusters // 8, eight, 1)
-    for c in range(clusters):
-        write(c).wait()
 
 
 def gram_kernel(
@@ -335,32 +333,33 @@
     tiles = quarter // LANES
     chunk = tiles * CAPS + tiles
     picks = -(-(clusters * (CAPS + 1)) // 16) * 16
-    steps = depth // FEATURE_STEP
+    steps = rows_dev // ROW_STEP
     smem = pl.BlockSpec(memory_space=pltpu.SMEM)
     vmem = pl.BlockSpec(memory_space=pltpu.VMEM)
     anywhere = pl.BlockSpec(memory_space=pl.ANY)
 
+    inputs = (
+        cluster_cap, adjacent, block_mask, assignment.reshape(blocks, LANES), embeddings
+    )
     send, slots = pl.pallas_call(
         functools.partial(select_kernel, clusters, reps),
         in_specs=[smem, smem, smem, vmem, anywhere],
-        out_specs=[anywhere, vmem],
+        out_specs=[vmem, vmem],
         out_shape=[
             jax.ShapeDtypeStruct((devices, chunk, LANES), jnp.bfloat16),
             jax.ShapeDtypeStruct((blocks, LANES), jnp.int32),
         ],
         scratch_shapes=[
-            pltpu.VMEM((steps, rows_dev, FEATURE_STEP), jnp.bfloat16),
+            pltpu.VMEM((steps, ROW_STEP, depth), jnp.bfloat16),
             pltpu.VMEM((picks, rows_dev), jnp.bfloat16),
             pltpu.VMEM((picks, LANES), jnp.float32),
             pltpu.VMEM((picks, depth), jnp.float32),
             pltpu.VMEM((picks, LANES), jnp.float32),
-            pltpu.VMEM((devices, chunk, LANES), jnp.bfloat16),
             pltpu.SemaphoreType.DMA((steps,)),
-            pltpu.SemaphoreType.DMA((clusters,)),
         ],
         compiler_params=pltpu.CompilerParams(vmem_limit_bytes=SELECT_BYTES),
         name="select_rows",
-    )(cluster_cap, adjacent, block_mask, assignment.reshape(blocks, LANES), embeddings)
+    )(*[pltpu.with_memory_space_constraint(x, pltpu.HBM) for x in inputs])
 
     got = lax.all_to_all(send, ALL, split_axis=0, concat_axis=0, tiled=True)
 

time: 76.8 us -> 74.8 us (0.974)
  Pallas kernels: 11 us -> 9.18 us
    pallas_call x1, Pallas kernels: 7.21 us -> 5.39 us  [local(): pl.pallas_call(functools.partial(select_kernel, clusters, reps), in_specs...]
where the time goes in v3:
time: 74.8 us; the launch traced here: 74.5 us
  blocking collectives  56.4 us (75%)
  Pallas kernels  9.18 us (12%)
  waiting for transfers between devices  6.96 us (9%)
  starting transfers between devices  1.83 us (2%)
    all_to_all x1, blocking collectives, local(): got = lax.all_to_all(send, ALL, split_axis=0, concat_axis=0, tiled=True)  46.3 us
    all_to_all x1, blocking collectives, local(): back = lax.all_to_all(sums, ALL, split_axis=0, concat_axis=0, tiled=True)  10.1 us
    ppermute x1, waiting for transfers between devices, local(): far = lax.ppermute((keep_far + core_far).astype(jnp.float16), 'rep', across)  5.75 us
    pallas_call x1, Pallas kernels, local(): pl.pallas_call(functools.partial(select_kernel, clusters, reps), in_specs...  5.39 us
    pallas_call x1, Pallas kernels, local(): pl.pallas_call(functools.partial(gram_kernel, dp_count, per_set), in_spec...  2.3 us
  transfers between devices with their start and end apart: 3, of which 2 were waited for; matrix products, arithmetic and copies ran while one was open for 0% of the time, Pallas kernels for 0%

profile of v3, /device:TPU:0, one launch (start us, length us, event | category | flops | bytes accessed | tf_op | source)
XLA Modules:
  0.0 74.5 jit_solution(8990297648862262868)
XLA Ops:
  0.0 5.4 %select_rows.1 = (bf16[32,200,128]{2,1,0:T(8,128)(2,1)S(1)}, s32[8,128]{1,0:T(8,128)S(1)}) custom-call(s32[8]{0:T(128)} %cap.1, s32[8]{0:T(128)} %adjacent.1, s32[8]{0:T(128)} %mask.1, s32[8,128]{1,0:T(8,128)} %bitcast.8, bf16[1024,4096]{1,0:T(8,128)(2,1)} %rows.1), custom_call_target="tpu_custom_call" | custom-call | tf_op jit(solution)/shard_map/select_rows/pallas_call | solution.py:344
  5.4 46.3 %all_to_all.16.got = bf16[32,200,128]{2,1,0:T(8,128)(2,1)S(1)} all-to-all(bf16[32,200,128]{2,1,0:T(8,128)(2,1)S(1)} %get-tuple-element.12), channel_id=1, replica_groups=mesh['dp'=8,'rep'=4] {'dp','rep'}, dimensions={0} | all-to-all | bytes 3276800 | tf_op jit(solution)/shard_map/all_to_all | solution.py:364
  51.7 2.3 %gram_tiles.1 = (f32[768,128]{1,0:T(8,128)S(1)}, f32[768,128]{1,0:T(8,128)S(1)}, f32[768,128]{1,0:T(8,128)S(1)}, f32[768,128]{1,0:T(8,128)S(1)}) custom-call(bf16[32,200,128]{2,1,0:T(8,128)(2,1)S(1)} %all_to_all.16.got), custom_call_target="tpu_custom_call" | custom-call | tf_op jit(solution)/shard_map/gram_tiles/pallas_call | solution.py:372
  54.0 0.1 collective-permute-start.1
  54.1 0.5 collective-permute-start
  54.6 1.2 %collective-permute-done.1 = f32[768,128]{1,0:T(8,128)S(1)} collective-permute-done((f32[768,128]{1,0:T(8,128)S(1)}, f32[768,128]{1,0:T(8,128)S(1)}, u32[]{:S(2)}, u32[]{:S(2)}) %collective-permute-start.1) | collective-permute-done | bytes 393248 | tf_op jit(solution)/shard_map/ppermute | solution.py:390
  55.8 0.1 add_convert_fusion
  55.9 1.3 %collective-permute-start.2 = (f16[768,128]{1,0:T(8,128)(2,1)S(1)}, f16[768,128]{1,0:T(8,128)(2,1)S(1)}, u32[]{:S(2)}, u32[]{:S(2)}) collective-permute-start(f16[768,128]{1,0:T(8,128)(2,1)S(1)} %add_convert_fusion), channel_id=1, source_target_pairs={{0,2},{2,0},{1,3},{3,1},{4,6},{6,4},{5,7},{7,5},{8,10},{10,8},{9,1... | collective-permute-start | bytes 589832 | tf_op jit(solution)/shard_map/ppermute | solution.py:391
  57.1 5.7 %collective-permute-done.2 = f16[768,128]{1,0:T(8,128)(2,1)S(1)} collective-permute-done((f16[768,128]{1,0:T(8,128)(2,1)S(1)}, f16[768,128]{1,0:T(8,128)(2,1)S(1)}, u32[]{:S(2)}, u32[]{:S(2)}) %collective-permute-start.2) | collective-permute-done | bytes 196640 | tf_op jit(solution)/shard_map/ppermute | solution.py:391
  62.9 0.0 collective-permute-done.core
  62.9 0.8 %score_tiles.1 = f32[32,128]{1,0:T(8,128)S(1)} custom-call(f32[768,128]{1,0:T(8,128)S(1)} %get-tuple-element.13.keep, f32[768,128]{1,0:T(8,128)S(1)} %collective-permute-done.core, f32[768,128]{1,0:T(8,128)S(1)} %convert_element_type.7.far), custom_call_target="tpu_custom_call" | custom-call | tf_op jit(solution)/shard_map/score_tiles/pallas_call | solution.py:394
  63.7 10.1 %all_to_all.17 = f32[32,1,128]{2,1,0:T(1,128)S(1)} all-to-all(f32[32,1,128]{2,1,0:T(1,128)S(1)} %bitcast.6), channel_id=1, replica_groups=mesh['dp'=8,'rep'=4] {'dp','rep'}, dimensions={0} | all-to-all | bytes 32768 | tf_op jit(solution)/shard_map/all_to_all | solution.py:404
  73.8 0.7 final_keep.1
  (1 shorter events, 0.0 us)
Async XLA Ops:
  54.0 1.8 %collective-permute-start.1 = (f32[768,128]{1,0:T(8,128)S(1)}, f32[768,128]{1,0:T(8,128)S(1)}, u32[]{:S(2)}, u32[]{:S(2)}) collective-permute-start(f32[768,128]{1,0:T(8,128)S(1)} %get-tuple-element.16), channel_id=1, source_target_pairs={{0,1},{1,0},{2,3},{3,2},{4,5},{5,4},{6,7},{7,6},{8,9},{9,8},{10,11... | collective-permute-start | bytes 1179656 | tf_op jit(solution)/shard_map/ppermute | solution.py:390
  54.1 8.8 %collective-permute-start = (f32[768,128]{1,0:T(8,128)S(1)}, f32[768,128]{1,0:T(8,128)S(1)}, u32[]{:S(2)}, u32[]{:S(2)}) collective-permute-start(f32[768,128]{1,0:T(8,128)S(1)} %get-tuple-element.14), channel_id=1, source_target_pairs={{0,1},{1,0},{2,3},{3,2},{4,5},{5,4},{6,7},{7,6},{8,9},{9,8},{10,11... | collective-permute-start | bytes 1179656 | tf_op jit(solution)/shard_map/ppermute | solution.py:392
  55.9 7.0 %collective-permute-start.2 = (f16[768,128]{1,0:T(8,128)(2,1)S(1)}, f16[768,128]{1,0:T(8,128)(2,1)S(1)}, u32[]{:S(2)}, u32[]{:S(2)}) collective-permute-start(f16[768,128]{1,0:T(8,128)(2,1)S(1)} %add_convert_fusion), channel_id=1, source_target_pairs={{0,2},{2,0},{1,3},{3,1},{4,6},{6,4},{5,7},{7,5},{8,10},{10,8},{9,1... | collective-permute-start | bytes 589832 | tf_op jit(solution)/shard_map/ppermute | solution.py:391

commit v4 on v3

--- a/solution.py
+++ b/solution.py
@@ -159,17 +159,78 @@
     each(clusters // 8, eight, 1)
 
 
-def gram_kernel(
-    ranks, per_set, got, send_far, send_near, keep_far, keep_near, x, edge_rows, edge_x, hold, sem
-):
+def tile_sets(blocks):
+    tiles = []
+    for p in range(0, blocks, 2):
+        tiles.append((p, p + 1, True))
+        tiles += [(i, j, False) for i in (p, p + 1) for j in range(i + 1, blocks)]
+    half = len(tiles) // 2
+    return tiles[:half], tiles[half:]
+
+
+def set_rows(blocks, ranks):
+    size = len(tile_sets(blocks)[0])
+    edge = size // 2 * LANES + size % 2 * (LANES // 2)
+    return edge, edge + -(-(blocks // 2) // 2) * ranks
+
+
+def emit_tiles(y, core, ranks, x, small, out):
+    count = x.shape[0]
+    blocks = count // LANES
+    contract = (((1,), (1,)), ((), ()))
+    first = (iota((8, LANES), 1) == 0).astype(jnp.bfloat16)
+    marks = lax.dot_general(first, x[:, :LANES], contract, preferred_element_type=jnp.float32)
+    col_pen = jnp.where(marks[:1] > 2.0, PENALTY, 0.0)
+    tiles = tile_sets(blocks)[y]
+    edge_base, _ = set_rows(blocks, ranks)
+
+    def put(owner, start, value):
+        slot = (core == owner).astype(jnp.int32)
+        out[slot, start : start + value.shape[0], :] = value
+
+    for p in range(0, blocks, 2):
+        mine = [(e, t) for e, t in enumerate(tiles) if t[0] // 2 == p // 2]
+        if not mine:
+            continue
+        row0 = min(t[0] for _, t in mine)
+        row1 = max(t[1] if t[2] else t[0] for _, t in mine) + 1
+        col0 = min(t[0] if t[2] else t[1] for _, t in mine)
+        col1 = max(t[1] for _, t in mine) + 1
+        rows = x[row0 * LANES : row1 * LANES, :]
+        cols = slice(col0 * LANES, col1 * LANES)
+        gram = lax.dot_general(rows, x[cols, :], contract, preferred_element_type=jnp.float32)
+        row_pen = jnp.where(rows[:, :1].astype(jnp.float32) > 2.0, PENALTY, 0.0)
+        gram = gram + row_pen + col_pen[:, cols]
+
+        def tile(i, j, gram=gram, row0=row0, col0=col0):
+            i, j = (i - row0) * LANES, (j - col0) * LANES
+            return gram[i : i + LANES, j : j + LANES]
+
+        for e, (i, j, diagonal) in mine:
+            if diagonal:
+                upper = iota((LANES, LANES), 0) < iota((LANES, LANES), 1)
+                value = jnp.where(upper, tile(i, i), tile(j, j))
+            else:
+                value = tile(i, j)
+            if e == len(tiles) - 1 and len(tiles) % 2:
+                half = LANES // 2
+                for owner in range(2):
+                    put(owner, e // 2 * LANES, value[owner * half : (owner + 1) * half])
+            else:
+                put(e % 2, e // 2 * LANES, value)
+
+    for k in range(blocks // 2):
+        at = (y * (blocks // 2) + k) * LANES
+        put(k % 2, edge_base + k // 2 * ranks, small[:, at : at + LANES])
+
+
+def gather_kernel(ranks, got, x, small, out, edge_rows, edge_x):
     sources = got.shape[0]
     count, quarter = x.shape
     tiles = quarter // LANES
-    blocks = count // LANES
     reps = 4
     main = tiles * CAPS
     me = lax.axis_index("rep")
-    my_core, my_y = me % 2, me // 2
 
     def gather(pair):
         values = [got[2 * pair + k].astype(jnp.float32) for k in range(2)]
@@ -193,73 +254,40 @@
             axis=1,
         ).astype(jnp.bfloat16)
 
-    first = (iota((8, LANES), 1) == 0).astype(jnp.bfloat16)
+    near = edge_x[...]
     contract = (((1,), (1,)), ((), ()))
-    marks = lax.dot_general(first, x[:, :LANES], contract, preferred_element_type=jnp.float32)
-    col_pen = jnp.where(marks[:1] > 2.0, PENALTY, 0.0)
-
-    def put(index, value):
-        owner, place = index % reps, index // reps
-        slot = 2 * (my_core == owner % 2).astype(jnp.int32) + (my_y == owner // 2).astype(jnp.int32)
-        hold[slot, place * LANES : place * LANES + value.shape[0], :] = value
-
-    index = 0
-    step = 2 * LANES
-    for start in range(0, count, step):
-        rows = x[start : start + step, :]
-        gram = lax.dot_general(rows, x[start:, :], contract, preferred_element_type=jnp.float32)
-        row_pen = jnp.where(rows[:, :1].astype(jnp.float32) > 2.0, PENALTY, 0.0)
-        gram = gram + row_pen + col_pen[:, start:]
-        shape = (LANES, LANES)
-        for half in range(2):
-            for tile in range(half, (count - start) // LANES):
-                value = gram[
-                    half * LANES : (half + 1) * LANES, tile * LANES : (tile + 1) * LANES
-                ]
-                if tile == half:
-                    value = jnp.where(iota(shape, 0) == iota(shape, 1), PENALTY, value)
-                put(index, value)
-                index += 1
-
-    near = edge_x[...]
     edge = lax.dot_general(near, x[...], contract, preferred_element_type=jnp.float32)
     edge = edge + jnp.where(near[:, :1].astype(jnp.float32) > 2.0, PENALTY, 0.0)
     lane_of = lax.rem(lax.div(iota((ranks, count), 1), CAPS), reps)
-    small = edge[:ranks]
+    picked = edge[:ranks]
     for lane in range(1, reps):
-        small = jnp.where(lane_of == lane, edge[lane * ranks : (lane + 1) * ranks], small)
-    per_tile = LANES // ranks
-    for first_block in range(0, blocks, per_tile):
-        stop = min(blocks, first_block + per_tile)
-        put(
-            index,
-            jnp.concatenate(
-                [small[:, b * LANES : (b + 1) * LANES] for b in range(first_block, stop)], axis=0
-            ),
+        picked = jnp.where(lane_of == lane, edge[lane * ranks : (lane + 1) * ranks], picked)
+    small[...] = picked
+
+    for y in range(2):
+        pl.when(me // 2 != y)(
+            functools.partial(emit_tiles, y, me % 2, ranks, x, small, out)
         )
-        index += 1
-
-    copies = [
-        pltpu.make_async_copy(hold.at[k], ref, sem.at[k])
-        for k, ref in enumerate((send_far, send_near, keep_far, keep_near))
-    ]
-    for copy in copies:
-        copy.start()
-    for copy in copies:
-        copy.wait()
-
-
-def score_kernel(ranks, sources, keep, core, far, out, total):
+
+
+def near_kernel(ranks, x, small, out):
+    me = lax.axis_index("rep")
+    for y in range(2):
+        pl.when(me // 2 == y)(
+            functools.partial(emit_tiles, y, me % 2, ranks, x, small, out)
+        )
+
+
+def score_kernel(ranks, sources, sums, out, total):
     count = sources * CAPS
     blocks = count // LANES
-    reps = 4
     me = lax.axis_index("rep")
-    pairs = [(i, j) for i in range(blocks) for j in range(i, blocks)]
+    core, my_y = me % 2, me // 2
+    sets = tile_sets(blocks)
+    size = len(sets[0])
+    edge_base, _ = set_rows(blocks, ranks)
     total[...] = jnp.zeros_like(total)
-
-    def value(place, size):
-        at = slice(place * LANES, place * LANES + size)
-        return keep[at, :] + core[at, :] + far[at, :]
+    shape = (LANES, LANES)
 
     def by_rep(values):
         picked = jnp.int32(values[0])
@@ -267,33 +295,51 @@
             picked = jnp.where(me == k, jnp.int32(values[k]), picked)
         return picked
 
-    def tile(place):
-        options = [pairs[min(place * reps + k, len(pairs) - 1)] for k in range(reps)]
-        i, j = by_rep([p[0] for p in options]), by_rep([p[1] for p in options])
-        weight = jax.nn.sigmoid(slope_gain * (value(place, LANES) - inner_cut))
-        total[pl.ds(i, 1), :] += jnp.sum(weight.T, axis=0, keepdims=True)
-        other = (i != j).astype(jnp.float32)
-        total[pl.ds(j, 1), :] += jnp.sum(weight, axis=0, keepdims=True) * other
-
-    per_set = -(-len(pairs) // reps)
-    for place in range(per_set):
-        if (place + 1) * reps <= len(pairs):
-            tile(place)
+    def weigh(value, cut):
+        return jax.nn.sigmoid(slope_gain * (value - cut))
+
+    def rows_of(weight):
+        return jnp.sum(weight.T, axis=0, keepdims=True)
+
+    def cols_of(weight):
+        return jnp.sum(weight, axis=0, keepdims=True)
+
+    def plain(i, j, weight):
+        total[pl.ds(i, 1), :] += rows_of(weight)
+        total[pl.ds(j, 1), :] += cols_of(weight)
+
+    def packed(i, j, weight):
+        upper = jnp.where(iota(shape, 0) < iota(shape, 1), weight, 0.0)
+        lower = jnp.where(iota(shape, 0) > iota(shape, 1), weight, 0.0)
+        total[pl.ds(i, 1), :] += rows_of(upper) + cols_of(upper)
+        total[pl.ds(j, 1), :] += rows_of(lower) + cols_of(lower)
+
+    for place in range(size // 2):
+        options = [sets[r // 2][2 * place + r % 2] for r in range(4)]
+        i, j = by_rep([t[0] for t in options]), by_rep([t[1] for t in options])
+        kinds = [t[2] for t in options]
+        weight = weigh(sums[place * LANES : (place + 1) * LANES, :], inner_cut)
+        if not any(kinds):
+            plain(i, j, weight)
         else:
-            pl.when(place * reps + me < len(pairs))(functools.partial(tile, place))
-
-    per_tile = LANES // ranks
-    for e, first_block in enumerate(range(0, blocks, per_tile)):
-        owner, place = (len(pairs) + e) % reps, (len(pairs) + e) // reps
-        stop = min(blocks, first_block + per_tile)
-
-        @pl.when(me == owner)
-        def _(place=place, first_block=first_block, stop=stop):
-            edge = value(place, (stop - first_block) * ranks)
-            edge = jax.nn.sigmoid(slope_gain * (edge - edge_cut))
-            for b in range(first_block, stop):
-                at = (b - first_block) * ranks
-                total[b : b + 1, :] += jnp.sum(edge[at : at + ranks], axis=0, keepdims=True)
+            kind = by_rep([int(k) for k in kinds])
+            pl.when(kind == 1)(functools.partial(packed, i, j, weight))
+            pl.when(kind == 0)(functools.partial(plain, i, j, weight))
+    if size % 2:
+        options = [sets[r // 2][size - 1] for r in range(4)]
+        i, j = by_rep([t[0] for t in options]), by_rep([t[1] for t in options])
+        start = size // 2 * LANES
+        weight = weigh(sums[start : start + LANES // 2, :], inner_cut)
+        halves = [jnp.where(core == k, weight, 0.0) for k in range(2)]
+        plain(i, j, jnp.concatenate(halves, axis=0))
+
+    for k in range(blocks // 2):
+
+        @pl.when(core == k % 2)
+        def _(k=k):
+            at = edge_base + k // 2 * ranks
+            edge = weigh(sums[at : at + ranks, :], edge_cut)
+            total[pl.ds(my_y * (blocks // 2) + k, 1), :] += cols_of(edge)
 
     result = jnp.zeros((sources, LANES), jnp.float32)
     for b in range(blocks):
@@ -365,41 +411,59 @@
 
     count = devices * CAPS
     group = count // LANES
-    pairs = group * (group + 1) // 2
-    edge_tiles = -(-group // (LANES // dp_count))
-    per_set = -(-(pairs + edge_tiles) // reps)
-    part = jax.ShapeDtypeStruct((per_set * LANES, LANES), jnp.float32)
-    send_far, send_near, keep_far, keep_near = pl.pallas_call(
-        functools.partial(gram_kernel, dp_count, per_set),
+    _, part_rows = set_rows(group, dp_count)
+    part = jax.ShapeDtypeStruct((2, part_rows, LANES), jnp.float32)
+    part_bytes = 2 * part_rows * LANES * 4
+    x, small, far_parts = pl.pallas_call(
+        functools.partial(gather_kernel, dp_count),
         in_specs=[vmem],
-        out_specs=[anywhere] * 4,
-        out_shape=[part] * 4,
+        out_specs=[vmem] * 3,
+        out_shape=[
+            jax.ShapeDtypeStruct((count, quarter), jnp.bfloat16),
+            jax.ShapeDtypeStruct((dp_count, count), jnp.float32),
+            part,
+        ],
         scratch_shapes=[
-            pltpu.VMEM((count, quarter), jnp.bfloat16),
             pltpu.VMEM((devices * tiles, LANES), jnp.float32),
             pltpu.VMEM((reps * dp_count, quarter), jnp.bfloat16),
-            pltpu.VMEM((4, per_set * LANES, LANES), jnp.float32),
-            pltpu.SemaphoreType.DMA((4,)),
         ],
-        compiler_params=grant(6 * count * quarter + 4 * per_set * LANES * LANES * 4),
-        name="gram_tiles",
+        compiler_params=grant(6 * count * quarter + part_bytes),
+        name="gather_far_tiles",
     )(got)
 
+    wire = jnp.float16
     cores = [(0, 1), (1, 0), (2, 3), (3, 2)]
     across = [(0, 2), (2, 0), (1, 3), (3, 1)]
-    core_far = lax.ppermute(send_far, "rep", cores)
-    far = lax.ppermute((keep_far + core_far).astype(jnp.float16), "rep", across)
-    core_near = lax.ppermute(send_near, "rep", cores)
+    far = lax.ppermute(far_parts[0].astype(wire), "rep", cores)
+    far = (far_parts[1] + far.astype(jnp.float32)).astype(wire)
+    far, x, small = lax.optimization_barrier((far, x, small))
+    far = lax.ppermute(far, "rep", across)
+    near_parts = pl.pallas_call(
+        functools.partial(near_kernel, dp_count),
+        in_specs=[vmem] * 2,
+        out_specs=vmem,
+        out_shape=part,
+        compiler_params=grant(4 * count * quarter + part_bytes),
+        cost_estimate=pl.CostEstimate(
+            flops=count * count * quarter, bytes_accessed=2 * count * quarter, transcendentals=0
+        ),
+        name="near_tiles",
+    )(x, small)
+    near = near_parts[0].astype(wire)
+    middle = part_rows // 32 * 16
+    near = [lax.ppermute(n, "rep", cores) for n in (near[:middle], near[middle:])]
+    near = jnp.concatenate(near)
+    both = near_parts[1] + near.astype(jnp.float32) + far.astype(jnp.float32)
 
     sums = pl.pallas_call(
         functools.partial(score_kernel, dp_count, devices),
-        in_specs=[vmem] * 3,
+        in_specs=[vmem],
         out_specs=vmem,
         out_shape=jax.ShapeDtypeStruct((devices, LANES), jnp.float32),
         scratch_shapes=[pltpu.VMEM((-(-group // 8) * 8, LANES), jnp.float32)],
-        compiler_params=grant(3 * per_set * LANES * LANES * 4),
+        compiler_params=grant(part_bytes),
         name="score_tiles",
-    )(keep_near, core_near, far.astype(jnp.float32))
+    )(both)
 
     back = lax.all_to_all(sums, ALL, split_axis=0, concat_axis=0, tiled=True)
     keep = pl.pallas_call(

time: 74.8 us -> 72.9 us (0.975)
  waiting for transfers between devices: 6.96 us -> 4.81 us
    ppermute x3 -> x4, waiting for transfers between devices: 6.96 us -> 4.81 us  [the longest x1 2.53 us: local(): far = lax.ppermute(far, 'rep', across)]
    pallas_call x1 -> x2, Pallas kernels: 2.3 us -> 2.11 us  [the longest x1 1.44 us: local(): pl.pallas_call(functools.partial(gather_kernel, dp_count), in_specs=[vmem...]
    ppermute x3 -> x4, starting transfers between devices: 1.83 us -> 1.9 us  [the longest x1 1.19 us: local(): far = lax.ppermute(far, 'rep', across)]
  transfers between devices with their start and end apart: 3 -> 4, of which waited for: 2 -> 3; matrix products, arithmetic and copies ran while one was open for 0% -> 0% of each run, Pallas kernels for 0% -> 1%
where the time goes in v4:
time: 72.9 us; the launch traced here: 72.7 us
  blocking collectives  56.5 us (78%)
  Pallas kernels  9.18 us (13%)
  waiting for transfers between devices  4.81 us (7%)
  starting transfers between devices  1.9 us (3%)
    all_to_all x1, blocking collectives, local(): got = lax.all_to_all(send, ALL, split_axis=0, concat_axis=0, tiled=True)  46.3 us
    all_to_all x1, blocking collectives, local(): back = lax.all_to_all(sums, ALL, split_axis=0, concat_axis=0, tiled=True)  10.2 us
    pallas_call x1, Pallas kernels, local(): pl.pallas_call(functools.partial(select_kernel, clusters, reps), in_specs...  5.39 us
    ppermute x1, waiting for transfers between devices, local(): far = lax.ppermute(far, 'rep', across)  2.53 us
  transfers between devices with their start and end apart: 4, of which 3 were waited for; matrix products, arithmetic and copies ran while one was open for 0% of the time, Pallas kernels for 1%

profile of v4, /device:TPU:0, one launch (start us, length us, event | category | flops | bytes accessed | tf_op | source)
XLA Modules:
  0.0 72.7 jit_solution(16924906119673735243)
XLA Ops:
  0.0 5.4 %select_rows.1 = (bf16[32,200,128]{2,1,0:T(8,128)(2,1)S(1)}, s32[8,128]{1,0:T(8,128)S(1)}) custom-call(s32[8]{0:T(128)} %cap.1, s32[8]{0:T(128)} %adjacent.1, s32[8]{0:T(128)} %mask.1, s32[8,128]{1,0:T(8,128)} %bitcast.24, bf16[1024,4096]{1,0:T(8,128)(2,1)} %rows.1), custom_call_target="tpu_custom_call" | custom-call | tf_op jit(solution)/shard_map/select_rows/pallas_call | solution.py:390
  5.4 46.3 %all_to_all.16.got = bf16[32,200,128]{2,1,0:T(8,128)(2,1)S(1)} all-to-all(bf16[32,200,128]{2,1,0:T(8,128)(2,1)S(1)} %get-tuple-element.14), channel_id=1, replica_groups=mesh['dp'=8,'rep'=4] {'dp','rep'}, dimensions={0} | all-to-all | bytes 3276800 | tf_op jit(solution)/shard_map/all_to_all | solution.py:410
  51.7 1.4 %gather_far_tiles.1 = (bf16[768,1024]{1,0:T(8,128)(2,1)S(1)}, f32[8,768]{1,0:T(8,128)S(1)}, f32[2,592,128]{2,1,0:T(8,128)S(1)}) custom-call(bf16[32,200,128]{2,1,0:T(8,128)(2,1)S(1)} %all_to_all.16.got), custom_call_target="tpu_custom_call" | custom-call | tf_op jit(solution)/shard_map/gather_far_tiles/pallas_call | solution.py:417
  53.2 0.1 collective-permute-start
  53.3 1.4 %collective-permute-done = f16[592,128]{1,0:T(8,128)(2,1)S(1)} collective-permute-done((f16[592,128]{1,0:T(8,128)(2,1)S(1)}, f16[592,128]{1,0:T(8,128)(2,1)S(1)}, u32[]{:S(2)}, u32[]{:S(2)}) %collective-permute-start) | collective-permute-done | bytes 151584 | tf_op jit(solution)/shard_map/ppermute | solution.py:437
  54.6 0.1 fusion.2
  54.7 1.2 %collective-permute-start.3 = (f16[592,128]{1,0:T(8,128)(2,1)S(1)}, f16[592,128]{1,0:T(8,128)(2,1)S(1)}, u32[]{:S(2)}, u32[]{:S(2)}) collective-permute-start(f16[592,128]{1,0:T(8,128)(2,1)S(1)} %fusion.2), channel_id=1, source_target_pairs={{0,2},{2,0},{1,3},{3,1},{4,6},{6,4},{5,7},{7,5},{8,10},{10,8},{9,1... | collective-permute-start | bytes 454664 | tf_op jit(solution)/shard_map/ppermute | solution.py:440
  55.9 0.7 near_tiles.1
  56.6 0.1 collective-permute-start.2
  56.7 0.6 collective-permute-start.1
  57.3 0.9 %collective-permute-done.1 = f16[288,128]{1,0:T(8,128)(2,1)S(1)} collective-permute-done((f16[288,128]{1,0:T(8,128)(2,1)S(1)}, f16[288,128]{1,0:T(8,128)(2,1)S(1)}, u32[]{:S(2)}, u32[]{:S(2)}) %collective-permute-start.1) | collective-permute-done | bytes 73760 | tf_op jit(solution)/shard_map/ppermute | solution.py:454
  58.2 0.0 collective-permute-done.2
  58.2 2.5 %collective-permute-done.3 = f16[592,128]{1,0:T(8,128)(2,1)S(1)} collective-permute-done((f16[592,128]{1,0:T(8,128)(2,1)S(1)}, f16[592,128]{1,0:T(8,128)(2,1)S(1)}, u32[]{:S(2)}, u32[]{:S(2)}) %collective-permute-start.3) | collective-permute-done | bytes 151584 | tf_op jit(solution)/shard_map/ppermute | solution.py:440
  60.7 0.1 fusion.1.sums
  60.8 1.0 %score_tiles.1 = f32[32,128]{1,0:T(8,128)S(1)} custom-call(f32[592,128]{1,0:T(8,128)S(1)} %fusion.1.sums), custom_call_target="tpu_custom_call" | custom-call | tf_op jit(solution)/shard_map/score_tiles/pallas_call | solution.py:458
  61.8 10.2 %all_to_all.17 = f32[32,1,128]{2,1,0:T(1,128)S(1)} all-to-all(f32[32,1,128]{2,1,0:T(1,128)S(1)} %bitcast.22), channel_id=1, replica_groups=mesh['dp'=8,'rep'=4] {'dp','rep'}, dimensions={0} | all-to-all | bytes 32768 | tf_op jit(solution)/shard_map/all_to_all | solution.py:468
  72.0 0.7 final_keep.1
  (4 shorter events, 0.1 us)
Async XLA Ops:
  53.2 1.4 %collective-permute-start = (f16[592,128]{1,0:T(8,128)(2,1)S(1)}, f16[592,128]{1,0:T(8,128)(2,1)S(1)}, u32[]{:S(2)}, u32[]{:S(2)}) collective-permute-start(f16[592,128]{1,0:T(8,128)(2,1)S(1)} %fusion.3), channel_id=1, source_target_pairs={{0,1},{1,0},{2,3},{3,2},{4,5},{5,4},{6,7},{7,6},{8,9},{9,8},{10,11... | collective-permute-start | bytes 454664 | tf_op jit(solution)/shard_map/ppermute | solution.py:437
  54.7 6.1 %collective-permute-start.3 = (f16[592,128]{1,0:T(8,128)(2,1)S(1)}, f16[592,128]{1,0:T(8,128)(2,1)S(1)}, u32[]{:S(2)}, u32[]{:S(2)}) collective-permute-start(f16[592,128]{1,0:T(8,128)(2,1)S(1)} %fusion.2), channel_id=1, source_target_pairs={{0,2},{2,0},{1,3},{3,1},{4,6},{6,4},{5,7},{7,5},{8,10},{10,8},{9,1... | collective-permute-start | bytes 454664 | tf_op jit(solution)/shard_map/ppermute | solution.py:440
  56.6 1.6 %collective-permute-start.2 = (f16[304,128]{1,0:T(8,128)(2,1)S(1)}, f16[304,128]{1,0:T(8,128)(2,1)S(1)}, u32[]{:S(2)}, u32[]{:S(2)}) collective-permute-start(f16[304,128]{1,0:T(8,128)(2,1)S(1)} %slice_bitcast_fusion.1), channel_id=1, source_target_pairs={{0,1},{1,0},{2,3},{3,2},{4,5},{5,4},{6,7},{7,6},{8,9},{9,8},{10,11... | collective-permute-start | bytes 233480 | tf_op jit(solution)/shard_map/ppermute | solution.py:454
  56.7 1.5 %collective-permute-start.1 = (f16[288,128]{1,0:T(8,128)(2,1)S(1)}, f16[288,128]{1,0:T(8,128)(2,1)S(1)}, u32[]{:S(2)}, u32[]{:S(2)}) collective-permute-start(f16[288,128]{1,0:T(8,128)(2,1)S(1)} %slice_bitcast_fusion.2), channel_id=1, source_target_pairs={{0,1},{1,0},{2,3},{3,2},{4,5},{5,4},{6,7},{7,6},{8,9},{9,8},{10,11... | collective-permute-start | bytes 221192 | tf_op jit(solution)/shard_map/ppermute | solution.py:454

commit v5 on v4

--- a/solution.py
+++ b/solution.py
@@ -46,19 +46,24 @@
 def select_kernel(
     clusters,
     reps,
+    cap_in,
+    adjacent_in,
+    mask_in,
+    assign_in,
+    rows,
+    out,
+    slots,
     cap,
     adjacent,
     mask,
     assign,
-    rows,
-    out,
-    slots,
     data,
     pick,
     filled,
     chosen,
     squares,
     in_sem,
+    small_sem,
 ):
     steps, deep, _ = data.shape
     reads = [
@@ -67,6 +72,14 @@
     ]
     for read in reads:
         read.start()
+    wanted = ((assign_in, assign), (mask_in, mask), (cap_in, cap), (adjacent_in, adjacent))
+    smalls = [
+        pltpu.make_async_copy(here, there, small_sem.at[k]) for k, (here, there) in enumerate(wanted)
+    ]
+    for small in smalls:
+        small.start()
+    for small in smalls:
+        small.wait()
 
     blocks = assign.shape[0]
     depth = chosen.shape[1]
@@ -341,19 +354,17 @@
             edge = weigh(sums[at : at + ranks, :], edge_cut)
             total[pl.ds(my_y * (blocks // 2) + k, 1), :] += cols_of(edge)
 
-    result = jnp.zeros((sources, LANES), jnp.float32)
-    for b in range(blocks):
-        where = iota((sources, LANES), 1) + b * LANES
-        mine = lax.div(where, CAPS) == iota((sources, LANES), 0)
-        spread = jnp.where(mine, total[b : b + 1, :], 0.0)
-        move = lax.rem(iota((LANES, LANES), 0) + b * LANES, CAPS) == iota((LANES, LANES), 1)
-        result += jnp.dot(
-            spread,
-            move.astype(jnp.float32),
-            precision=lax.Precision.HIGHEST,
-            preferred_element_type=jnp.float32,
-        )
-    out[...] = result
+    board = total[...]
+    lane = iota((1, LANES), 1)
+    for shift in range(0, LANES, 8):
+        turned = pltpu.roll(board, (LANES - shift) % LANES, 1)
+        for source in range(sources):
+            block, offset = divmod(source * CAPS, LANES)
+            if offset == shift:
+                line = turned[block : block + 1, :]
+                if offset + CAPS > LANES:
+                    line = jnp.where(lane < LANES - offset, line, turned[block + 1 : block + 2, :])
+                out[source : source + 1, :] = line
 
 
 def final_kernel(clusters, reps, slots, sums, out):
@@ -389,19 +400,24 @@
     )
     send, slots = pl.pallas_call(
         functools.partial(select_kernel, clusters, reps),
-        in_specs=[smem, smem, smem, vmem, anywhere],
+        in_specs=[anywhere] * 5,
         out_specs=[vmem, vmem],
         out_shape=[
             jax.ShapeDtypeStruct((devices, chunk, LANES), jnp.bfloat16),
             jax.ShapeDtypeStruct((blocks, LANES), jnp.int32),
         ],
         scratch_shapes=[
+            pltpu.SMEM((clusters,), jnp.int32),
+            pltpu.SMEM((clusters,), jnp.int32),
+            pltpu.SMEM((blocks,), jnp.int32),
+            pltpu.VMEM((blocks, LANES), jnp.int32),
             pltpu.VMEM((steps, ROW_STEP, depth), jnp.bfloat16),
             pltpu.VMEM((picks, rows_dev), jnp.bfloat16),
             pltpu.VMEM((picks, LANES), jnp.float32),
             pltpu.VMEM((picks, depth), jnp.float32),
             pltpu.VMEM((picks, LANES), jnp.float32),
             pltpu.SemaphoreType.DMA((steps,)),
+            pltpu.SemaphoreType.DMA((4,)),
         ],
         compiler_params=pltpu.CompilerParams(vmem_limit_bytes=SELECT_BYTES),
         name="select_rows",

time: 72.9 us -> 71.9 us (0.986)
  Pallas kernels: 9.18 us -> 8.18 us
where the time goes in v5:
time: 71.9 us; the launch traced here: 71.7 us
  blocking collectives  56.5 us (79%)
  Pallas kernels  8.18 us (11%)
  waiting for transfers between devices  4.8 us (7%)
  starting transfers between devices  1.9 us (3%)
    all_to_all x1, blocking collectives, local(): got = lax.all_to_all(send, ALL, split_axis=0, concat_axis=0, tiled=True)  46.3 us
    all_to_all x1, blocking collectives, local(): back = lax.all_to_all(sums, ALL, split_axis=0, concat_axis=0, tiled=True)  10.2 us
    pallas_call x1, Pallas kernels, local(): pl.pallas_call(functools.partial(select_kernel, clusters, reps), in_specs...  4.79 us
    ppermute x1, waiting for transfers between devices, local(): far = lax.ppermute(far, 'rep', across)  2.52 us
  transfers between devices with their start and end apart: 4, of which 3 were waited for; matrix products, arithmetic and copies ran while one was open for 0% of the time, Pallas kernels for 1%

profile of v5, /device:TPU:0, one launch (start us, length us, event | category | flops | bytes accessed | tf_op | source)
XLA Modules:
  0.0 71.7 jit_solution(14665798631274021832)
XLA Ops:
  0.0 4.8 %select_rows.1 = (bf16[32,200,128]{2,1,0:T(8,128)(2,1)S(1)}, s32[8,128]{1,0:T(8,128)S(1)}) custom-call(s32[8]{0:T(128)} %cap_in.1, s32[8]{0:T(128)} %adjacent_in.1, s32[8]{0:T(128)} %mask_in.1, s32[8,128]{1,0:T(8,128)} %bitcast.24, bf16[1024,4096]{1,0:T(8,128)(2,1)} %rows.1), custom_call_target="tpu_custom_call" | custom-call | tf_op jit(solution)/shard_map/select_rows/pallas_call | solution.py:401
  4.8 46.3 %all_to_all.16.got = bf16[32,200,128]{2,1,0:T(8,128)(2,1)S(1)} all-to-all(bf16[32,200,128]{2,1,0:T(8,128)(2,1)S(1)} %get-tuple-element.14), channel_id=1, replica_groups=mesh['dp'=8,'rep'=4] {'dp','rep'}, dimensions={0} | all-to-all | bytes 3276800 | tf_op jit(solution)/shard_map/all_to_all | solution.py:426
  51.1 1.4 %gather_far_tiles.1 = (bf16[768,1024]{1,0:T(8,128)(2,1)S(1)}, f32[8,768]{1,0:T(8,128)S(1)}, f32[2,592,128]{2,1,0:T(8,128)S(1)}) custom-call(bf16[32,200,128]{2,1,0:T(8,128)(2,1)S(1)} %all_to_all.16.got), custom_call_target="tpu_custom_call" | custom-call | tf_op jit(solution)/shard_map/gather_far_tiles/pallas_call | solution.py:433
  52.6 0.1 collective-permute-start
  52.7 1.4 %collective-permute-done = f16[592,128]{1,0:T(8,128)(2,1)S(1)} collective-permute-done((f16[592,128]{1,0:T(8,128)(2,1)S(1)}, f16[592,128]{1,0:T(8,128)(2,1)S(1)}, u32[]{:S(2)}, u32[]{:S(2)}) %collective-permute-start) | collective-permute-done | bytes 151584 | tf_op jit(solution)/shard_map/ppermute | solution.py:453
  54.0 0.1 fusion.2
  54.1 1.2 %collective-permute-start.3 = (f16[592,128]{1,0:T(8,128)(2,1)S(1)}, f16[592,128]{1,0:T(8,128)(2,1)S(1)}, u32[]{:S(2)}, u32[]{:S(2)}) collective-permute-start(f16[592,128]{1,0:T(8,128)(2,1)S(1)} %fusion.2), channel_id=1, source_target_pairs={{0,2},{2,0},{1,3},{3,1},{4,6},{6,4},{5,7},{7,5},{8,10},{10,8},{9,1... | collective-permute-start | bytes 454664 | tf_op jit(solution)/shard_map/ppermute | solution.py:456
  55.3 0.7 near_tiles.1
  56.0 0.1 collective-permute-start.2
  56.1 0.6 collective-permute-start.1
  56.7 0.9 %collective-permute-done.1 = f16[288,128]{1,0:T(8,128)(2,1)S(1)} collective-permute-done((f16[288,128]{1,0:T(8,128)(2,1)S(1)}, f16[288,128]{1,0:T(8,128)(2,1)S(1)}, u32[]{:S(2)}, u32[]{:S(2)}) %collective-permute-start.1) | collective-permute-done | bytes 73760 | tf_op jit(solution)/shard_map/ppermute | solution.py:470
  57.6 0.0 collective-permute-done.2
  57.6 2.5 %collective-permute-done.3 = f16[592,128]{1,0:T(8,128)(2,1)S(1)} collective-permute-done((f16[592,128]{1,0:T(8,128)(2,1)S(1)}, f16[592,128]{1,0:T(8,128)(2,1)S(1)}, u32[]{:S(2)}, u32[]{:S(2)}) %collective-permute-start.3) | collective-permute-done | bytes 151584 | tf_op jit(solution)/shard_map/ppermute | solution.py:456
  60.1 0.1 fusion.1.sums
  60.2 0.6 score_tiles.1
  60.8 10.2 %all_to_all.17 = f32[32,1,128]{2,1,0:T(1,128)S(1)} all-to-all(f32[32,1,128]{2,1,0:T(1,128)S(1)} %bitcast.22), channel_id=1, replica_groups=mesh['dp'=8,'rep'=4] {'dp','rep'}, dimensions={0} | all-to-all | bytes 32768 | tf_op jit(solution)/shard_map/all_to_all | solution.py:484
  71.0 0.7 final_keep.1
  (4 shorter events, 0.1 us)
Async XLA Ops:
  52.6 1.4 %collective-permute-start = (f16[592,128]{1,0:T(8,128)(2,1)S(1)}, f16[592,128]{1,0:T(8,128)(2,1)S(1)}, u32[]{:S(2)}, u32[]{:S(2)}) collective-permute-start(f16[592,128]{1,0:T(8,128)(2,1)S(1)} %fusion.3), channel_id=1, source_target_pairs={{0,1},{1,0},{2,3},{3,2},{4,5},{5,4},{6,7},{7,6},{8,9},{9,8},{10,11... | collective-permute-start | bytes 454664 | tf_op jit(solution)/shard_map/ppermute | solution.py:453
  54.1 6.1 %collective-permute-start.3 = (f16[592,128]{1,0:T(8,128)(2,1)S(1)}, f16[592,128]{1,0:T(8,128)(2,1)S(1)}, u32[]{:S(2)}, u32[]{:S(2)}) collective-permute-start(f16[592,128]{1,0:T(8,128)(2,1)S(1)} %fusion.2), channel_id=1, source_target_pairs={{0,2},{2,0},{1,3},{3,1},{4,6},{6,4},{5,7},{7,5},{8,10},{10,8},{9,1... | collective-permute-start | bytes 454664 | tf_op jit(solution)/shard_map/ppermute | solution.py:456
  56.0 1.6 %collective-permute-start.2 = (f16[304,128]{1,0:T(8,128)(2,1)S(1)}, f16[304,128]{1,0:T(8,128)(2,1)S(1)}, u32[]{:S(2)}, u32[]{:S(2)}) collective-permute-start(f16[304,128]{1,0:T(8,128)(2,1)S(1)} %slice_bitcast_fusion.1), channel_id=1, source_target_pairs={{0,1},{1,0},{2,3},{3,2},{4,5},{5,4},{6,7},{7,6},{8,9},{9,8},{10,11... | collective-permute-start | bytes 233480 | tf_op jit(solution)/shard_map/ppermute | solution.py:470
  56.1 1.5 %collective-permute-start.1 = (f16[288,128]{1,0:T(8,128)(2,1)S(1)}, f16[288,128]{1,0:T(8,128)(2,1)S(1)}, u32[]{:S(2)}, u32[]{:S(2)}) collective-permute-start(f16[288,128]{1,0:T(8,128)(2,1)S(1)} %slice_bitcast_fusion.2), channel_id=1, source_target_pairs={{0,1},{1,0},{2,3},{3,2},{4,5},{5,4},{6,7},{7,6},{8,9},{9,8},{10,11... | collective-permute-start | bytes 221192 | tf_op jit(solution)/shard_map/ppermute | solution.py:470

commit v6 on v5

--- a/solution.py
+++ b/solution.py
@@ -187,19 +187,23 @@
     return edge, edge + -(-(blocks // 2) // 2) * ranks
 
 
-def emit_tiles(y, core, ranks, x, small, out):
-    count = x.shape[0]
+def emit_tiles(y, core, ranks, x, edge_x, out):
+    count, quarter = x.shape
     blocks = count // LANES
+    half = blocks // 2
+    reps = edge_x.shape[0] // ranks
     contract = (((1,), (1,)), ((), ()))
-    first = (iota((8, LANES), 1) == 0).astype(jnp.bfloat16)
-    marks = lax.dot_general(first, x[:, :LANES], contract, preferred_element_type=jnp.float32)
-    col_pen = jnp.where(marks[:1] > 2.0, PENALTY, 0.0)
     tiles = tile_sets(blocks)[y]
     edge_base, _ = set_rows(blocks, ranks)
+    marker = (iota((16, quarter), 1) == 0).astype(jnp.bfloat16)
+    edges_left = True
 
     def put(owner, start, value):
         slot = (core == owner).astype(jnp.int32)
         out[slot, start : start + value.shape[0], :] = value
+
+    def penalty(marks):
+        return jnp.where(marks > 2.0, PENALTY, 0.0)
 
     for p in range(0, blocks, 2):
         mine = [(e, t) for e, t in enumerate(tiles) if t[0] // 2 == p // 2]
@@ -210,14 +214,18 @@
         col0 = min(t[0] if t[2] else t[1] for _, t in mine)
         col1 = max(t[1] for _, t in mine) + 1
         rows = x[row0 * LANES : row1 * LANES, :]
-        cols = slice(col0 * LANES, col1 * LANES)
-        gram = lax.dot_general(rows, x[cols, :], contract, preferred_element_type=jnp.float32)
-        row_pen = jnp.where(rows[:, :1].astype(jnp.float32) > 2.0, PENALTY, 0.0)
-        gram = gram + row_pen + col_pen[:, cols]
-
-        def tile(i, j, gram=gram, row0=row0, col0=col0):
+        edges_here = edges_left and col0 <= y * half and col1 >= (y + 1) * half
+        near = [edge_x[...]] if edges_here else []
+        left = jnp.concatenate([rows, *near, marker], axis=0)
+        right = x[col0 * LANES : col1 * LANES, :]
+        gram = lax.dot_general(left, right, contract, preferred_element_type=jnp.float32)
+        col_pen = penalty(gram[left.shape[0] - 16 : left.shape[0] - 15])
+        main = rows.shape[0]
+        pairs = gram[:main] + penalty(rows[:, :1].astype(jnp.float32)) + col_pen
+
+        def tile(i, j, pairs=pairs, row0=row0, col0=col0):
             i, j = (i - row0) * LANES, (j - col0) * LANES
-            return gram[i : i + LANES, j : j + LANES]
+            return pairs[i : i + LANES, j : j + LANES]
 
         for e, (i, j, diagonal) in mine:
             if diagonal:
@@ -226,22 +234,34 @@
             else:
                 value = tile(i, j)
             if e == len(tiles) - 1 and len(tiles) % 2:
-                half = LANES // 2
+                cut = LANES // 2
                 for owner in range(2):
-                    put(owner, e // 2 * LANES, value[owner * half : (owner + 1) * half])
+                    put(owner, e // 2 * LANES, value[owner * cut : (owner + 1) * cut])
             else:
                 put(e % 2, e // 2 * LANES, value)
 
-    for k in range(blocks // 2):
-        at = (y * (blocks // 2) + k) * LANES
-        put(k % 2, edge_base + k // 2 * ranks, small[:, at : at + LANES])
-
-
-def gather_kernel(ranks, got, x, small, out, edge_rows, edge_x):
+        if edges_here:
+            edges_left = False
+            edge = gram[main : main + reps * ranks] + penalty(near[0][:, :1].astype(jnp.float32))
+            shape = (ranks, LANES)
+            for k in range(half):
+                block = y * half + k
+                at = (block - col0) * LANES
+                spot = iota(shape, 1) + block * LANES
+                lane_of = lax.rem(lax.div(spot, CAPS), reps)
+                value = edge[:ranks, at : at + LANES]
+                for lane in range(1, reps):
+                    other = edge[lane * ranks : (lane + 1) * ranks, at : at + LANES]
+                    value = jnp.where(lane_of == lane, other, value)
+                put(k % 2, edge_base + k // 2 * ranks, value)
+    assert not edges_left
+
+
+def gather_kernel(ranks, got, x, edge_x, out, edge_rows):
     sources = got.shape[0]
-    count, quarter = x.shape
+    quarter = x.shape[1]
     tiles = quarter // LANES
-    reps = 4
+    reps = edge_x.shape[0] // ranks
     main = tiles * CAPS
     me = lax.axis_index("rep")
 
@@ -258,36 +278,24 @@
 
     each(sources // 2, gather, 16)
 
-    for lane in range(reps):
-        edge_x[lane * ranks : (lane + 1) * ranks, :] = jnp.concatenate(
-            [
-                edge_rows[pl.ds(lane * tiles + k, ranks, stride=reps * tiles), :]
-                for k in range(tiles)
-            ],
-            axis=1,
-        ).astype(jnp.bfloat16)
-
-    near = edge_x[...]
-    contract = (((1,), (1,)), ((), ()))
-    edge = lax.dot_general(near, x[...], contract, preferred_element_type=jnp.float32)
-    edge = edge + jnp.where(near[:, :1].astype(jnp.float32) > 2.0, PENALTY, 0.0)
-    lane_of = lax.rem(lax.div(iota((ranks, count), 1), CAPS), reps)
-    picked = edge[:ranks]
-    for lane in range(1, reps):
-        picked = jnp.where(lane_of == lane, edge[lane * ranks : (lane + 1) * ranks], picked)
-    small[...] = picked
+    for k in range(tiles):
+        lines = [
+            edge_rows[pl.ds(lane * tiles + k, ranks, stride=reps * tiles), :]
+            for lane in range(reps)
+        ]
+        edge_x[:, k * LANES : (k + 1) * LANES] = jnp.concatenate(lines, axis=0).astype(jnp.bfloat16)
 
     for y in range(2):
         pl.when(me // 2 != y)(
-            functools.partial(emit_tiles, y, me % 2, ranks, x, small, out)
+            functools.partial(emit_tiles, y, me % 2, ranks, x, edge_x, out)
         )
 
 
-def near_kernel(ranks, x, small, out):
+def near_kernel(ranks, x, edge_x, out):
     me = lax.axis_index("rep")
     for y in range(2):
         pl.when(me // 2 == y)(
-            functools.partial(emit_tiles, y, me % 2, ranks, x, small, out)
+            functools.partial(emit_tiles, y, me % 2, ranks, x, edge_x, out)
         )
 
 
@@ -430,18 +438,17 @@
     _, part_rows = set_rows(group, dp_count)
     part = jax.ShapeDtypeStruct((2, part_rows, LANES), jnp.float32)
     part_bytes = 2 * part_rows * LANES * 4
-    x, small, far_parts = pl.pallas_call(
+    x, edge_x, far_parts = pl.pallas_call(
         functools.partial(gather_kernel, dp_count),
         in_specs=[vmem],
         out_specs=[vmem] * 3,
         out_shape=[
             jax.ShapeDtypeStruct((count, quarter), jnp.bfloat16),
-            jax.ShapeDtypeStruct((dp_count, count), jnp.float32),
+            jax.ShapeDtypeStruct((reps * dp_count, quarter), jnp.bfloat16),
             part,
         ],
         scratch_shapes=[
             pltpu.VMEM((devices * tiles, LANES), jnp.float32),
-            pltpu.VMEM((reps * dp_count, quarter), jnp.bfloat16),
         ],
         compiler_params=grant(6 * count * quarter + part_bytes),
         name="gather_far_tiles",
@@ -452,7 +459,7 @@
     across = [(0, 2), (2, 0), (1, 3), (3, 1)]
     far = lax.ppermute(far_parts[0].astype(wire), "rep", cores)
     far = (far_parts[1] + far.astype(jnp.float32)).astype(wire)
-    far, x, small = lax.optimization_barrier((far, x, small))
+    far, x, edge_x = lax.optimization_barrier((far, x, edge_x))
     far = lax.ppermute(far, "rep", across)
     near_parts = pl.pallas_call(
         functools.partial(near_kernel, dp_count),
@@ -464,7 +471,7 @@
             flops=count * count * quarter, bytes_accessed=2 * count * quarter, transcendentals=0
         ),
         name="near_tiles",
-    )(x, small)
+    )(x, edge_x)
     near = near_parts[0].astype(wire)
     middle = part_rows // 32 * 16
     near = [lax.ppermute(n, "rep", cores) for n in (near[:middle], near[middle:])]

time: 71.9 us -> 71.6 us (level)
  no operation moved by 1% of the time
where the time goes in v6:
time: 71.6 us; the launch traced here: 71.4 us
  blocking collectives  56.5 us (79%)
  Pallas kernels  7.95 us (11%)
  waiting for transfers between devices  4.67 us (7%)
  starting transfers between devices  1.96 us (3%)
    all_to_all x1, blocking collectives, local(): got = lax.all_to_all(send, ALL, split_axis=0, concat_axis=0, tiled=True)  46.3 us
    all_to_all x1, blocking collectives, local(): back = lax.all_to_all(sums, ALL, split_axis=0, concat_axis=0, tiled=True)  10.2 us
    pallas_call x1, Pallas kernels, local(): pl.pallas_call(functools.partial(select_kernel, clusters, reps), in_specs...  4.79 us
    ppermute x1, waiting for transfers between devices, local(): far = lax.ppermute(far, 'rep', across)  2.39 us
  transfers between devices with their start and end apart: 4, of which 3 were waited for; matrix products, arithmetic and copies ran while one was open for 0% of the time, Pallas kernels for 1%

profile of v6, /device:TPU:0, one launch (start us, length us, event | category | flops | bytes accessed | tf_op | source)
XLA Modules:
  0.0 71.4 jit_solution(6089257833241499226)
XLA Ops:
  0.0 4.8 %select_rows.1 = (bf16[32,200,128]{2,1,0:T(8,128)(2,1)S(1)}, s32[8,128]{1,0:T(8,128)S(1)}) custom-call(s32[8]{0:T(128)} %cap_in.1, s32[8]{0:T(128)} %adjacent_in.1, s32[8]{0:T(128)} %mask_in.1, s32[8,128]{1,0:T(8,128)} %bitcast.24, bf16[1024,4096]{1,0:T(8,128)(2,1)} %rows.1), custom_call_target="tpu_custom_call" | custom-call | tf_op jit(solution)/shard_map/select_rows/pallas_call | solution.py:409
  4.8 46.3 %all_to_all.16.got = bf16[32,200,128]{2,1,0:T(8,128)(2,1)S(1)} all-to-all(bf16[32,200,128]{2,1,0:T(8,128)(2,1)S(1)} %get-tuple-element.14), channel_id=1, replica_groups=mesh['dp'=8,'rep'=4] {'dp','rep'}, dimensions={0} | all-to-all | bytes 3276800 | tf_op jit(solution)/shard_map/all_to_all | solution.py:434
  51.1 1.1 %gather_far_tiles.1 = (bf16[768,1024]{1,0:T(8,128)(2,1)S(1)}, bf16[32,1024]{1,0:T(8,128)(2,1)S(1)}, f32[2,592,128]{2,1,0:T(8,128)S(1)}) custom-call(bf16[32,200,128]{2,1,0:T(8,128)(2,1)S(1)} %all_to_all.16.got), custom_call_target="tpu_custom_call" | custom-call | tf_op jit(solution)/shard_map/gather_far_tiles/pallas_call | solution.py:441
  52.3 0.1 collective-permute-start
  52.3 1.4 %collective-permute-done = f16[592,128]{1,0:T(8,128)(2,1)S(1)} collective-permute-done((f16[592,128]{1,0:T(8,128)(2,1)S(1)}, f16[592,128]{1,0:T(8,128)(2,1)S(1)}, u32[]{:S(2)}, u32[]{:S(2)}) %collective-permute-start) | collective-permute-done | bytes 151584 | tf_op jit(solution)/shard_map/ppermute | solution.py:460
  53.7 0.1 fusion.2
  53.8 1.2 %collective-permute-start.3 = (f16[592,128]{1,0:T(8,128)(2,1)S(1)}, f16[592,128]{1,0:T(8,128)(2,1)S(1)}, u32[]{:S(2)}, u32[]{:S(2)}) collective-permute-start(f16[592,128]{1,0:T(8,128)(2,1)S(1)} %fusion.2), channel_id=1, source_target_pairs={{0,2},{2,0},{1,3},{3,1},{4,6},{6,4},{5,7},{7,5},{8,10},{10,8},{9,1... | collective-permute-start | bytes 454664 | tf_op jit(solution)/shard_map/ppermute | solution.py:463
  55.0 0.8 %near_tiles.1 = f32[2,592,128]{2,1,0:T(8,128)S(1)} custom-call(bf16[768,1024]{1,0:T(8,128)(2,1)S(1)} %get-tuple-element.18.x, bf16[32,1024]{1,0:T(8,128)(2,1)S(1)} %get-tuple-element.19.edge_x), custom_call_target="tpu_custom_call" | custom-call | flops 603979776 | bytes 1572864 | tf_op jit(solution)/shard_map/near_tiles/pallas_call | solution.py:464
  55.9 0.1 collective-permute-start.2
  56.0 0.6 collective-permute-start.1
  56.5 0.9 %collective-permute-done.1 = f16[288,128]{1,0:T(8,128)(2,1)S(1)} collective-permute-done((f16[288,128]{1,0:T(8,128)(2,1)S(1)}, f16[288,128]{1,0:T(8,128)(2,1)S(1)}, u32[]{:S(2)}, u32[]{:S(2)}) %collective-permute-start.1) | collective-permute-done | bytes 73760 | tf_op jit(solution)/shard_map/ppermute | solution.py:477
  57.4 0.0 collective-permute-done.2
  57.4 2.4 %collective-permute-done.3 = f16[592,128]{1,0:T(8,128)(2,1)S(1)} collective-permute-done((f16[592,128]{1,0:T(8,128)(2,1)S(1)}, f16[592,128]{1,0:T(8,128)(2,1)S(1)}, u32[]{:S(2)}, u32[]{:S(2)}) %collective-permute-start.3) | collective-permute-done | bytes 151584 | tf_op jit(solution)/shard_map/ppermute | solution.py:463
  59.8 0.1 fusion.1.sums
  59.9 0.6 score_tiles.1
  60.5 10.2 %all_to_all.17 = f32[32,1,128]{2,1,0:T(1,128)S(1)} all-to-all(f32[32,1,128]{2,1,0:T(1,128)S(1)} %bitcast.22), channel_id=1, replica_groups=mesh['dp'=8,'rep'=4] {'dp','rep'}, dimensions={0} | all-to-all | bytes 32768 | tf_op jit(solution)/shard_map/all_to_all | solution.py:491
  70.7 0.7 final_keep.1
  (4 shorter events, 0.1 us)
Async XLA Ops:
  52.3 1.4 %collective-permute-start = (f16[592,128]{1,0:T(8,128)(2,1)S(1)}, f16[592,128]{1,0:T(8,128)(2,1)S(1)}, u32[]{:S(2)}, u32[]{:S(2)}) collective-permute-start(f16[592,128]{1,0:T(8,128)(2,1)S(1)} %fusion.3), channel_id=1, source_target_pairs={{0,1},{1,0},{2,3},{3,2},{4,5},{5,4},{6,7},{7,6},{8,9},{9,8},{10,11... | collective-permute-start | bytes 454664 | tf_op jit(solution)/shard_map/ppermute | solution.py:460
  53.8 6.1 %collective-permute-start.3 = (f16[592,128]{1,0:T(8,128)(2,1)S(1)}, f16[592,128]{1,0:T(8,128)(2,1)S(1)}, u32[]{:S(2)}, u32[]{:S(2)}) collective-permute-start(f16[592,128]{1,0:T(8,128)(2,1)S(1)} %fusion.2), channel_id=1, source_target_pairs={{0,2},{2,0},{1,3},{3,1},{4,6},{6,4},{5,7},{7,5},{8,10},{10,8},{9,1... | collective-permute-start | bytes 454664 | tf_op jit(solution)/shard_map/ppermute | solution.py:463
  55.9 1.6 %collective-permute-start.2 = (f16[304,128]{1,0:T(8,128)(2,1)S(1)}, f16[304,128]{1,0:T(8,128)(2,1)S(1)}, u32[]{:S(2)}, u32[]{:S(2)}) collective-permute-start(f16[304,128]{1,0:T(8,128)(2,1)S(1)} %slice_bitcast_fusion.1), channel_id=1, source_target_pairs={{0,1},{1,0},{2,3},{3,2},{4,5},{5,4},{6,7},{7,6},{8,9},{9,8},{10,11... | collective-permute-start | bytes 233480 | tf_op jit(solution)/shard_map/ppermute | solution.py:477
  56.0 1.5 %collective-permute-start.1 = (f16[288,128]{1,0:T(8,128)(2,1)S(1)}, f16[288,128]{1,0:T(8,128)(2,1)S(1)}, u32[]{:S(2)}, u32[]{:S(2)}) collective-permute-start(f16[288,128]{1,0:T(8,128)(2,1)S(1)} %slice_bitcast_fusion.2), channel_id=1, source_target_pairs={{0,1},{1,0},{2,3},{3,2},{4,5},{5,4},{6,7},{7,6},{8,9},{9,8},{10,11... | collective-permute-start | bytes 221192 | tf_op jit(solution)/shard_map/ppermute | solution.py:477

commit v7 on v6

--- a/solution.py
+++ b/solution.py
@@ -62,6 +62,7 @@
     filled,
     chosen,
     squares,
+    edges,
     in_sem,
     small_sem,
 ):
@@ -143,31 +144,29 @@
     squares[...] = jnp.broadcast_to(scale, squares.shape)
     quarter = depth // reps
     tiles = quarter // LANES
-    sub = iota((tiles, LANES), 0)
 
     def eight(group):
         near = pl.ds(pl.multiple_of(base + group * 8, 8), 8)
         near_gain, near_flag = squares[near, :], filled[near, :]
+        for q in range(reps):
+            for t in range(tiles):
+                col = q * quarter + t * LANES
+                line = chosen[near, col : col + LANES] * near_gain
+                if t == 0:
+                    line += near_flag
+                edges[pl.ds(q * 8 * tiles + t, 8, stride=tiles), :] = line
         for k in range(8):
-            c = group * 8 + k
-            at = pl.ds(pl.multiple_of(c * CAPS, 8), CAPS)
+            at = pl.ds(pl.multiple_of((group * 8 + k) * CAPS, 8), CAPS)
             gain, flag = squares[at, :], filled[at, :]
             for q in range(reps):
                 pieces = []
-                edge = jnp.zeros((tiles, LANES), jnp.float32)
                 for t in range(tiles):
                     cols = slice(q * quarter + t * LANES, q * quarter + (t + 1) * LANES)
-                    piece = chosen[at, cols] * gain
-                    line = chosen[near, cols] * near_gain
-                    if t == 0:
-                        piece += flag
-                        line += near_flag
-                    pieces.append(piece)
-                    line = jnp.broadcast_to(line[k : k + 1], edge.shape)
-                    edge = jnp.where(sub == t, line, edge)
-                pieces.append(edge)
+                    pieces.append(chosen[at, cols] * gain)
+                pieces[0] += flag
+                pieces.append(edges[(q * 8 + k) * tiles : (q * 8 + k + 1) * tiles, :])
                 chunk = jnp.concatenate(pieces, axis=0).astype(jnp.bfloat16)
-                out[c * reps + q] = chunk
+                out[(group * 8 + k) * reps + q] = chunk
 
     each(clusters // 8, eight, 1)
 
@@ -424,6 +423,7 @@
             pltpu.VMEM((picks, LANES), jnp.float32),
             pltpu.VMEM((picks, depth), jnp.float32),
             pltpu.VMEM((picks, LANES), jnp.float32),
+            pltpu.VMEM((8 * reps * tiles, LANES), jnp.float32),
             pltpu.SemaphoreType.DMA((steps,)),
             pltpu.SemaphoreType.DMA((4,)),
         ],
@@ -472,11 +472,9 @@
         ),
         name="near_tiles",
     )(x, edge_x)
-    near = near_parts[0].astype(wire)
-    middle = part_rows // 32 * 16
-    near = [lax.ppermute(n, "rep", cores) for n in (near[:middle], near[middle:])]
-    near = jnp.concatenate(near)
-    both = near_parts[1] + near.astype(jnp.float32) + far.astype(jnp.float32)
+    near = lax.ppermute(near_parts[0].astype(wire), "rep", cores)
+    both = near_parts[1] + far.astype(jnp.float32)
+    both = lax.optimization_barrier(both) + near.astype(jnp.float32)
 
     sums = pl.pallas_call(
         functools.partial(score_kernel, dp_count, devices),

time: 71.6 us -> 71.6 us (level)
    ppermute x1, waiting for transfers between devices: 2.39 us -> 3.93 us  [local(): far = lax.ppermute(far, 'rep', across)]
    ppermute x2 -> x1, waiting for transfers between devices: 0.92 us -> 0.01 us  [local(): near = lax.ppermute(near_parts[0].astype(wire), 'rep', cores)]
  transfers between devices with their start and end apart: 4 -> 3, of which waited for: 3 -> 2; matrix products, arithmetic and copies ran while one was open for 0% -> 0% of each run, Pallas kernels for 1% -> 1%
where the time goes in v7:
time: 71.6 us; the launch traced here: 71.4 us
  blocking collectives  56.5 us (79%)
  Pallas kernels  7.88 us (11%)
  waiting for transfers between devices  5.29 us (7%)
  starting transfers between devices  1.4 us (2%)
    all_to_all x1, blocking collectives, local(): got = lax.all_to_all(send, ALL, split_axis=0, concat_axis=0, tiled=True)  46.3 us
    all_to_all x1, blocking collectives, local(): back = lax.all_to_all(sums, ALL, split_axis=0, concat_axis=0, tiled=True)  10.2 us
    pallas_call x1, Pallas kernels, local(): pl.pallas_call(functools.partial(select_kernel, clusters, reps), in_specs...  4.73 us
    ppermute x1, waiting for transfers between devices, local(): far = lax.ppermute(far, 'rep', across)  3.93 us
  transfers between devices with their start and end apart: 3, of which 2 were waited for; matrix products, arithmetic and copies ran while one was open for 0% of the time, Pallas kernels for 1%

profile of v7, /device:TPU:0, one launch (start us, length us, event | category | flops | bytes accessed | tf_op | source)
XLA Modules:
  0.0 71.4 jit_solution(12730675313791287326)
XLA Ops:
  0.0 4.7 %select_rows.1 = (bf16[32,200,128]{2,1,0:T(8,128)(2,1)S(1)}, s32[8,128]{1,0:T(8,128)S(1)}) custom-call(s32[8]{0:T(128)} %cap_in.1, s32[8]{0:T(128)} %adjacent_in.1, s32[8]{0:T(128)} %mask_in.1, s32[8,128]{1,0:T(8,128)} %bitcast.20, bf16[1024,4096]{1,0:T(8,128)(2,1)} %rows.1), custom_call_target="tpu_custom_call" | custom-call | tf_op jit(solution)/shard_map/select_rows/pallas_call | solution.py:408
  4.7 46.3 %all_to_all.16.got = bf16[32,200,128]{2,1,0:T(8,128)(2,1)S(1)} all-to-all(bf16[32,200,128]{2,1,0:T(8,128)(2,1)S(1)} %get-tuple-element.14), channel_id=1, replica_groups=mesh['dp'=8,'rep'=4] {'dp','rep'}, dimensions={0} | all-to-all | bytes 3276800 | tf_op jit(solution)/shard_map/all_to_all | solution.py:434
  51.0 1.1 %gather_far_tiles.1 = (bf16[768,1024]{1,0:T(8,128)(2,1)S(1)}, bf16[32,1024]{1,0:T(8,128)(2,1)S(1)}, f32[2,592,128]{2,1,0:T(8,128)S(1)}) custom-call(bf16[32,200,128]{2,1,0:T(8,128)(2,1)S(1)} %all_to_all.16.got), custom_call_target="tpu_custom_call" | custom-call | tf_op jit(solution)/shard_map/gather_far_tiles/pallas_call | solution.py:441
  52.2 0.1 collective-permute-start
  52.3 1.4 %collective-permute-done = f16[592,128]{1,0:T(8,128)(2,1)S(1)} collective-permute-done((f16[592,128]{1,0:T(8,128)(2,1)S(1)}, f16[592,128]{1,0:T(8,128)(2,1)S(1)}, u32[]{:S(2)}, u32[]{:S(2)}) %collective-permute-start) | collective-permute-done | bytes 151584 | tf_op jit(solution)/shard_map/ppermute | solution.py:460
  53.7 0.1 fusion.1
  53.7 1.3 %collective-permute-start.1 = (f16[592,128]{1,0:T(8,128)(2,1)S(1)}, f16[592,128]{1,0:T(8,128)(2,1)S(1)}, u32[]{:S(2)}, u32[]{:S(2)}) collective-permute-start(f16[592,128]{1,0:T(8,128)(2,1)S(1)} %fusion.1), channel_id=1, source_target_pairs={{0,2},{2,0},{1,3},{3,1},{4,6},{6,4},{5,7},{7,5},{8,10},{10,8},{9,1... | collective-permute-start | bytes 454664 | tf_op jit(solution)/shard_map/ppermute | solution.py:463
  55.0 0.7 %near_tiles.1 = f32[2,592,128]{2,1,0:T(8,128)S(1)} custom-call(bf16[768,1024]{1,0:T(8,128)(2,1)S(1)} %get-tuple-element.18.x, bf16[32,1024]{1,0:T(8,128)(2,1)S(1)} %get-tuple-element.19.edge_x), custom_call_target="tpu_custom_call" | custom-call | flops 603979776 | bytes 1572864 | tf_op jit(solution)/shard_map/near_tiles/pallas_call | solution.py:464
  55.7 0.1 collective-permute-start.2
  55.8 3.9 %collective-permute-done.1 = f16[592,128]{1,0:T(8,128)(2,1)S(1)} collective-permute-done((f16[592,128]{1,0:T(8,128)(2,1)S(1)}, f16[592,128]{1,0:T(8,128)(2,1)S(1)}, u32[]{:S(2)}, u32[]{:S(2)}) %collective-permute-start.1) | collective-permute-done | bytes 151584 | tf_op jit(solution)/shard_map/ppermute | solution.py:463
  59.8 0.0 collective-permute-done.2
  59.8 0.1 convert_add_fusion.sums
  59.9 0.6 score_tiles.1
  60.5 10.2 %all_to_all.17 = f32[32,1,128]{2,1,0:T(1,128)S(1)} all-to-all(f32[32,1,128]{2,1,0:T(1,128)S(1)} %bitcast.18), channel_id=1, replica_groups=mesh['dp'=8,'rep'=4] {'dp','rep'}, dimensions={0} | all-to-all | bytes 32768 | tf_op jit(solution)/shard_map/all_to_all | solution.py:489
  70.7 0.7 final_keep.1
  (3 shorter events, 0.1 us)
Async XLA Ops:
  52.2 1.4 %collective-permute-start = (f16[592,128]{1,0:T(8,128)(2,1)S(1)}, f16[592,128]{1,0:T(8,128)(2,1)S(1)}, u32[]{:S(2)}, u32[]{:S(2)}) collective-permute-start(f16[592,128]{1,0:T(8,128)(2,1)S(1)} %fusion.2), channel_id=1, source_target_pairs={{0,1},{1,0},{2,3},{3,2},{4,5},{5,4},{6,7},{7,6},{8,9},{9,8},{10,11... | collective-permute-start | bytes 454664 | tf_op jit(solution)/shard_map/ppermute | solution.py:460
  53.7 6.1 %collective-permute-start.1 = (f16[592,128]{1,0:T(8,128)(2,1)S(1)}, f16[592,128]{1,0:T(8,128)(2,1)S(1)}, u32[]{:S(2)}, u32[]{:S(2)}) collective-permute-start(f16[592,128]{1,0:T(8,128)(2,1)S(1)} %fusion.1), channel_id=1, source_target_pairs={{0,2},{2,0},{1,3},{3,1},{4,6},{6,4},{5,7},{7,5},{8,10},{10,8},{9,1... | collective-permute-start | bytes 454664 | tf_op jit(solution)/shard_map/ppermute | solution.py:463
  55.7 4.1 %collective-permute-start.2 = (f16[592,128]{1,0:T(8,128)(2,1)S(1)}, f16[592,128]{1,0:T(8,128)(2,1)S(1)}, u32[]{:S(2)}, u32[]{:S(2)}) collective-permute-start(f16[592,128]{1,0:T(8,128)(2,1)S(1)} %fusion.3), channel_id=1, source_target_pairs={{0,1},{1,0},{2,3},{3,2},{4,5},{5,4},{6,7},{7,6},{8,9},{9,8},{10,11... | collective-permute-start | bytes 454664 | tf_op jit(solution)/shard_map/ppermute | solution.py:475

commit v8 on v7

--- a/solution.py
+++ b/solution.py
@@ -9,6 +9,7 @@
 
 CAPS = 24
 LANES = 128
+GROUPS = LANES // CAPS
 ALL = ("dp", "rep")
 FEATURE_STEP = 512
 ROW_STEP = 256
@@ -41,6 +42,10 @@
 
 def iota(shape, dim):
     return lax.broadcasted_iota(jnp.int32, shape, dim)
+
+
+def ring(count):
+    return [*range(0, count, 2), *range(count - 1, 0, -2)]
 
 
 def select_kernel(
@@ -62,7 +67,6 @@
     filled,
     chosen,
     squares,
-    edges,
     in_sem,
     small_sem,
 ):
@@ -85,13 +89,19 @@
     blocks = assign.shape[0]
     depth = chosen.shape[1]
     count = pick.shape[0]
-    base = clusters * CAPS
     table = assign[...]
     sub = iota(table.shape, 0)
     active = jnp.zeros(table.shape, jnp.int32)
     for block in range(blocks):
         active = jnp.where(sub == block, mask[block], active)
-    live = jnp.where(active == 1, table, -1)
+    owner = jnp.full(table.shape, -1, jnp.int32)
+    caps = [None] * clusters
+    current = jnp.int32(0)
+    for place in ring(clusters):
+        owner = jnp.where(table == current, place, owner)
+        caps[place] = cap[current]
+        current = adjacent[current]
+    live = jnp.where(active == 1, owner, -1)
     members = jnp.concatenate(
         [(live == c).astype(jnp.float32) for c in range(clusters)], axis=0
     ).astype(jnp.bfloat16)
@@ -110,12 +120,9 @@
     slot = jnp.full(table.shape, -1, jnp.int32)
     for c in range(clusters):
         own = rank[c * blocks : (c + 1) * blocks]
-        slot = jnp.where((live == c) & (own < cap[c]), c * CAPS + own, slot)
+        slot = jnp.where((live == c) & (own < caps[c]), c * CAPS + own, slot)
     slots[...] = slot
-    place = iota((count, LANES), 0)
-    target = jnp.where(place < base, place, -7)
-    for c in range(clusters):
-        target = jnp.where(place == base + c, adjacent[c] * CAPS, target)
+    target = iota((count, LANES), 0)
     seen = jnp.zeros((count, LANES), jnp.float32)
     for block in range(blocks):
         hit = (target == slot[block : block + 1]).astype(jnp.float32)
@@ -146,15 +153,6 @@
     tiles = quarter // LANES
 
     def eight(group):
-        near = pl.ds(pl.multiple_of(base + group * 8, 8), 8)
-        near_gain, near_flag = squares[near, :], filled[near, :]
-        for q in range(reps):
-            for t in range(tiles):
-                col = q * quarter + t * LANES
-                line = chosen[near, col : col + LANES] * near_gain
-                if t == 0:
-                    line += near_flag
-                edges[pl.ds(q * 8 * tiles + t, 8, stride=tiles), :] = line
         for k in range(8):
             at = pl.ds(pl.multiple_of((group * 8 + k) * CAPS, 8), CAPS)
             gain, flag = squares[at, :], filled[at, :]
@@ -164,7 +162,6 @@
                     cols = slice(q * quarter + t * LANES, q * quarter + (t + 1) * LANES)
                     pieces.append(chosen[at, cols] * gain)
                 pieces[0] += flag
-                pieces.append(edges[(q * 8 + k) * tiles : (q * 8 + k + 1) * tiles, :])
                 chunk = jnp.concatenate(pieces, axis=0).astype(jnp.bfloat16)
                 out[(group * 8 + k) * reps + q] = chunk
 
@@ -180,22 +177,24 @@
     return tiles[:half], tiles[half:]
 
 
-def set_rows(blocks, ranks):
+def set_rows(blocks):
     size = len(tile_sets(blocks)[0])
-    edge = size // 2 * LANES + size % 2 * (LANES // 2)
-    return edge, edge + -(-(blocks // 2) // 2) * ranks
-
-
-def emit_tiles(y, core, ranks, x, edge_x, out):
+    return size // 2 * LANES + size % 2 * (LANES // 2)
+
+
+def back_rows(ranks):
+    return -(-(1 + ranks) // GROUPS)
+
+
+def emit_tiles(y, core, x, edge_x, out, packed):
     count, quarter = x.shape
     blocks = count // LANES
-    half = blocks // 2
-    reps = edge_x.shape[0] // ranks
     contract = (((1,), (1,)), ((), ()))
     tiles = tile_sets(blocks)[y]
-    edge_base, _ = set_rows(blocks, ranks)
     marker = (iota((16, quarter), 1) == 0).astype(jnp.bfloat16)
-    edges_left = True
+    extra = [marker] if edge_x is None else [edge_x[...], marker]
+    size = sum(e.shape[0] for e in extra)
+    edges = {}
 
     def put(owner, start, value):
         slot = (core == owner).astype(jnp.int32)
@@ -203,6 +202,10 @@
 
     def penalty(marks):
         return jnp.where(marks > 2.0, PENALTY, 0.0)
+
+    def note(gram, main, col0):
+        for k in range(gram.shape[1] // LANES):
+            edges.setdefault(col0 + k, gram[main : main + size - 16, k * LANES : (k + 1) * LANES])
 
     for p in range(0, blocks, 2):
         mine = [(e, t) for e, t in enumerate(tiles) if t[0] // 2 == p // 2]
@@ -213,14 +216,13 @@
         col0 = min(t[0] if t[2] else t[1] for _, t in mine)
         col1 = max(t[1] for _, t in mine) + 1
         rows = x[row0 * LANES : row1 * LANES, :]
-        edges_here = edges_left and col0 <= y * half and col1 >= (y + 1) * half
-        near = [edge_x[...]] if edges_here else []
-        left = jnp.concatenate([rows, *near, marker], axis=0)
+        left = jnp.concatenate([rows, *extra], axis=0)
         right = x[col0 * LANES : col1 * LANES, :]
         gram = lax.dot_general(left, right, contract, preferred_element_type=jnp.float32)
-        col_pen = penalty(gram[left.shape[0] - 16 : left.shape[0] - 15])
         main = rows.shape[0]
+        col_pen = penalty(gram[main + size - 16 : main + size - 15])
         pairs = gram[:main] + penalty(rows[:, :1].astype(jnp.float32)) + col_pen
+        note(gram, main, col0)
 
         def tile(i, j, pairs=pairs, row0=row0, col0=col0):
             i, j = (i - row0) * LANES, (j - col0) * LANES
@@ -239,21 +241,47 @@
             else:
                 put(e % 2, e // 2 * LANES, value)
 
-        if edges_here:
-            edges_left = False
-            edge = gram[main : main + reps * ranks] + penalty(near[0][:, :1].astype(jnp.float32))
-            shape = (ranks, LANES)
-            for k in range(half):
-                block = y * half + k
-                at = (block - col0) * LANES
-                spot = iota(shape, 1) + block * LANES
-                lane_of = lax.rem(lax.div(spot, CAPS), reps)
-                value = edge[:ranks, at : at + LANES]
-                for lane in range(1, reps):
-                    other = edge[lane * ranks : (lane + 1) * ranks, at : at + LANES]
-                    value = jnp.where(lane_of == lane, other, value)
-                put(k % 2, edge_base + k // 2 * ranks, value)
-    assert not edges_left
+    if edge_x is None:
+        return
+    first = min(edges)
+    if first:
+        near = edge_x[...]
+        note(
+            lax.dot_general(
+                near, x[: first * LANES, :], contract, preferred_element_type=jnp.float32
+            ),
+            0,
+            0,
+        )
+    reps = 4
+    ranks = edge_x.shape[0] // reps
+    row_pen = penalty(edge_x[:, :1].astype(jnp.float32))
+    shape = (ranks, LANES)
+    lines = []
+    for block in range(blocks):
+        edge = edges[block] + row_pen
+        lane_of = lax.rem(lax.div(iota(shape, 1) + block * LANES, CAPS), reps)
+        value = edge[:ranks]
+        for lane in range(1, reps):
+            value = jnp.where(lane_of == lane, edge[lane * ranks : (lane + 1) * ranks], value)
+        lines.append(value)
+
+    height = back_rows(ranks)
+    spot = iota((1, LANES), 1)
+    for source in range(count // CAPS):
+        block, offset = divmod(source * CAPS, LANES)
+        value = lines[block]
+        if offset + CAPS > LANES:
+            value = jnp.where(iota(shape, 1) >= offset, value, lines[block + 1])
+        turned = [pltpu.roll(value, (k * CAPS - offset) % LANES, 1) for k in range(GROUPS)]
+        for row in range(height):
+            line = jnp.zeros((1, LANES), jnp.float32)
+            for k in range(GROUPS):
+                j = row * GROUPS + k - 1
+                if 0 <= j < ranks:
+                    line = jnp.where(spot >= k * CAPS, turned[k][j : j + 1, :], line)
+            at = source * height + row
+            packed[at : at + 1, :] = line
 
 
 def gather_kernel(ranks, got, x, edge_x, out, edge_rows):
@@ -261,17 +289,21 @@
     quarter = x.shape[1]
     tiles = quarter // LANES
     reps = edge_x.shape[0] // ranks
-    main = tiles * CAPS
     me = lax.axis_index("rep")
+    sub = iota((tiles, LANES), 0)
 
     def gather(pair):
         values = [got[2 * pair + k].astype(jnp.float32) for k in range(2)]
         for k in range(2):
-            edge_rows[pl.ds((2 * pair + k) * tiles, tiles), :] = values[k][main:]
-        for k in range(tiles):
-            rows = slice(k * CAPS, (k + 1) * CAPS)
+            lines = jnp.zeros((tiles, LANES), jnp.float32)
+            for t in range(tiles):
+                line = jnp.broadcast_to(values[k][t * CAPS : t * CAPS + 1], lines.shape)
+                lines = jnp.where(sub == t, line, lines)
+            edge_rows[pl.ds((2 * pair + k) * tiles, tiles), :] = lines
+        for t in range(tiles):
+            rows = slice(t * CAPS, (t + 1) * CAPS)
             both = jnp.concatenate([v[rows] for v in values], axis=0)
-            x[pl.ds(pair * 2 * CAPS, 2 * CAPS), k * LANES : (k + 1) * LANES] = both.astype(
+            x[pl.ds(pair * 2 * CAPS, 2 * CAPS), t * LANES : (t + 1) * LANES] = both.astype(
                 jnp.bfloat16
             )
 
@@ -285,27 +317,22 @@
         edge_x[:, k * LANES : (k + 1) * LANES] = jnp.concatenate(lines, axis=0).astype(jnp.bfloat16)
 
     for y in range(2):
-        pl.when(me // 2 != y)(
-            functools.partial(emit_tiles, y, me % 2, ranks, x, edge_x, out)
-        )
-
-
-def near_kernel(ranks, x, edge_x, out):
+        pl.when(me // 2 != y)(functools.partial(emit_tiles, y, me % 2, x, None, out, None))
+
+
+def near_kernel(x, edge_x, out, packed):
     me = lax.axis_index("rep")
     for y in range(2):
-        pl.when(me // 2 == y)(
-            functools.partial(emit_tiles, y, me % 2, ranks, x, edge_x, out)
-        )
-
-
-def score_kernel(ranks, sources, sums, out, total):
+        pl.when(me // 2 == y)(functools.partial(emit_tiles, y, me % 2, x, edge_x, out, packed))
+
+
+def score_kernel(sources, sums, logits, out, total):
     count = sources * CAPS
     blocks = count // LANES
     me = lax.axis_index("rep")
-    core, my_y = me % 2, me // 2
+    core = me % 2
     sets = tile_sets(blocks)
     size = len(sets[0])
-    edge_base, _ = set_rows(blocks, ranks)
     total[...] = jnp.zeros_like(total)
     shape = (LANES, LANES)
 
@@ -353,14 +380,8 @@
         halves = [jnp.where(core == k, weight, 0.0) for k in range(2)]
         plain(i, j, jnp.concatenate(halves, axis=0))
 
-    for k in range(blocks // 2):
-
-        @pl.when(core == k % 2)
-        def _(k=k):
-            at = edge_base + k // 2 * ranks
-            edge = weigh(sums[at : at + ranks, :], edge_cut)
-            total[pl.ds(my_y * (blocks // 2) + k, 1), :] += cols_of(edge)
-
+    height = logits.shape[0] // sources
+    out[...] = logits[...]
     board = total[...]
     lane = iota((1, LANES), 1)
     for shift in range(0, LANES, 8):
@@ -371,15 +392,32 @@
                 line = turned[block : block + 1, :]
                 if offset + CAPS > LANES:
                     line = jnp.where(lane < LANES - offset, line, turned[block + 1 : block + 2, :])
-                out[source : source + 1, :] = line
+                at = slice(source * height, source * height + 1)
+                out[at, :] = jnp.where(lane < CAPS, line, logits[at, :])
 
 
 def final_kernel(clusters, reps, slots, sums, out):
+    height = sums.shape[0] // (clusters * reps)
+    ranks = clusters
     slot = slots[...]
+
+    def gathered(row):
+        lines = []
+        for c in range(clusters):
+            starts = [(c * reps + q) * height + row for q in range(reps)]
+            lines.append(sum(sums[at : at + 1, :] for at in starts))
+        return jnp.concatenate(lines, axis=0)
+
+    rows = [gathered(row) for row in range(height)]
+    edges = [jax.nn.sigmoid(slope_gain * (r - edge_cut)) for r in rows]
+    inner = rows[0]
+    for k in range(GROUPS):
+        mine = [r for r in range(height) if 1 <= r * GROUPS + k <= ranks]
+        inner += pltpu.roll(sum(edges[r] for r in mine), (-k * CAPS) % LANES, 1)
+    board = 1.0 / (1.0 + inner)
     result = jnp.ones(slot.shape, jnp.float32)
     for c in range(clusters):
-        inner = jnp.sum(sums[c * reps : (c + 1) * reps, :], axis=0, keepdims=True)
-        keep = jnp.broadcast_to(1.0 / (1.0 + inner), slot.shape)
+        keep = jnp.broadcast_to(board[c : c + 1, :], slot.shape)
         rank = slot - c * CAPS
         mine = (rank >= 0) & (rank < CAPS)
         found = jnp.take_along_axis(keep, jnp.where(mine, rank, 0), axis=1)
@@ -395,8 +433,8 @@
     clusters = cluster_cap.shape[0]
     quarter = depth // reps
     tiles = quarter // LANES
-    chunk = tiles * CAPS + tiles
-    picks = -(-(clusters * (CAPS + 1)) // 16) * 16
+    chunk = tiles * CAPS
+    picks = clusters * CAPS
     steps = rows_dev // ROW_STEP
     smem = pl.BlockSpec(memory_space=pltpu.SMEM)
     vmem = pl.BlockSpec(memory_space=pltpu.VMEM)
@@ -423,7 +461,6 @@
             pltpu.VMEM((picks, LANES), jnp.float32),
             pltpu.VMEM((picks, depth), jnp.float32),
             pltpu.VMEM((picks, LANES), jnp.float32),
-            pltpu.VMEM((8 * reps * tiles, LANES), jnp.float32),
             pltpu.SemaphoreType.DMA((steps,)),
             pltpu.SemaphoreType.DMA((4,)),
         ],
@@ -435,9 +472,9 @@
 
     count = devices * CAPS
     group = count // LANES
-    _, part_rows = set_rows(group, dp_count)
-    part = jax.ShapeDtypeStruct((2, part_rows, LANES), jnp.float32)
-    part_bytes = 2 * part_rows * LANES * 4
+    part_rows = set_rows(group)
+    height = back_rows(dp_count)
+    near_bytes = (2 * part_rows + devices * height) * LANES * 4
     x, edge_x, far_parts = pl.pallas_call(
         functools.partial(gather_kernel, dp_count),
         in_specs=[vmem],
@@ -445,28 +482,32 @@
         out_shape=[
             jax.ShapeDtypeStruct((count, quarter), jnp.bfloat16),
             jax.ShapeDtypeStruct((reps * dp_count, quarter), jnp.bfloat16),
-            part,
+            jax.ShapeDtypeStruct((2, part_rows, LANES), jnp.float32),
         ],
-        scratch_shapes=[
-            pltpu.VMEM((devices * tiles, LANES), jnp.float32),
-        ],
-        compiler_params=grant(6 * count * quarter + part_bytes),
+        scratch_shapes=[pltpu.VMEM((devices * tiles, LANES), jnp.float32)],
+        compiler_params=grant(6 * count * quarter + near_bytes),
         name="gather_far_tiles",
     )(got)
 
     wire = jnp.float16
     cores = [(0, 1), (1, 0), (2, 3), (3, 2)]
     across = [(0, 2), (2, 0), (1, 3), (3, 1)]
+    order = ring(dp_count)
+    back_one = [(order[(p + 1) % dp_count], order[p]) for p in range(dp_count)]
     far = lax.ppermute(far_parts[0].astype(wire), "rep", cores)
+    edge_x = lax.ppermute(edge_x, "dp", back_one)
     far = (far_parts[1] + far.astype(jnp.float32)).astype(wire)
-    far, x, edge_x = lax.optimization_barrier((far, x, edge_x))
+    far, x = lax.optimization_barrier((far, x))
     far = lax.ppermute(far, "rep", across)
-    near_parts = pl.pallas_call(
-        functools.partial(near_kernel, dp_count),
+    near_parts, packed = pl.pallas_call(
+        near_kernel,
         in_specs=[vmem] * 2,
-        out_specs=vmem,
-        out_shape=part,
-        compiler_params=grant(4 * count * quarter + part_bytes),
+        out_specs=[vmem] * 2,
+        out_shape=[
+            jax.ShapeDtypeStruct((2, part_rows, LANES), jnp.float32),
+            jax.ShapeDtypeStruct((devices * height, LANES), jnp.float32),
+        ],
+        compiler_params=grant(4 * count * quarter + near_bytes),
         cost_estimate=pl.CostEstimate(
             flops=count * count * quarter, bytes_accessed=2 * count * quarter, transcendentals=0
         ),
@@ -477,14 +518,14 @@
     both = lax.optimization_barrier(both) + near.astype(jnp.float32)
 
     sums = pl.pallas_call(
-        functools.partial(score_kernel, dp_count, devices),
-        in_specs=[vmem],
+        functools.partial(score_kernel, devices),
+        in_specs=[vmem] * 2,
         out_specs=vmem,
-        out_shape=jax.ShapeDtypeStruct((devices, LANES), jnp.float32),
+        out_shape=jax.ShapeDtypeStruct((devices * height, LANES), jnp.float32),
         scratch_shapes=[pltpu.VMEM((-(-group // 8) * 8, LANES), jnp.float32)],
-        compiler_params=grant(part_bytes),
+        compiler_params=grant(near_bytes),
         name="score_tiles",
-    )(both)
+    )(both, packed).reshape(devices, height, LANES)
 
     back = lax.all_to_all(sums, ALL, split_axis=0, concat_axis=0, tiled=True)
     keep = pl.pallas_call(
@@ -494,7 +535,7 @@
         out_shape=jax.ShapeDtypeStruct((blocks, LANES), jnp.float32),
         compiler_params=grant(0),
         name="final_keep",
-    )(slots, back)
+    )(slots, back.reshape(devices * height, LANES))
     return keep.reshape(rows_dev)
 
 

time: 71.6 us -> 70 us (0.978)
  waiting for transfers between devices: 5.29 us -> 3.91 us
  blocking collectives: 56.5 us -> 55.2 us
  starting transfers between devices: 1.4 us -> 2.61 us
    ppermute x1, waiting for transfers between devices: 3.93 us -> 1.94 us  [local(): far = lax.ppermute(far, 'rep', across)]
    ppermute x0 -> x1, waiting for transfers between devices: none -> 1.96 us  [local(): edge_x = lax.ppermute(edge_x, 'dp', back_one)]
    ppermute x1, waiting for transfers between devices: 1.36 us -> 0.01 us  [local(): far = lax.ppermute(far_parts[0].astype(wire), 'rep', cores)]
    ppermute x0 -> x1, starting transfers between devices: none -> 1.35 us  [local(): edge_x = lax.ppermute(edge_x, 'dp', back_one)]
    all_to_all x1, blocking collectives: 46.3 us -> 45.1 us  [local(): got = lax.all_to_all(send, ALL, split_axis=0, concat_axis=0, tiled=True)]
  transfers between devices with their start and end apart: 3 -> 4, of which waited for: 2 -> 2; matrix products, arithmetic and copies ran while one was open for 0% -> 0% of each run, Pallas kernels for 1% -> 1%
where the time goes in v8:
time: 70 us; the launch traced here: 69.8 us
  blocking collectives  55.2 us (79%)
  Pallas kernels  7.88 us (11%)
  waiting for transfers between devices  3.91 us (6%)
  starting transfers between devices  2.61 us (4%)
    all_to_all x1, blocking collectives, local(): got = lax.all_to_all(send, ALL, split_axis=0, concat_axis=0, tiled=True)  45.1 us
    all_to_all x1, blocking collectives, local(): back = lax.all_to_all(sums, ALL, split_axis=0, concat_axis=0, tiled=True)  10.1 us
    pallas_call x1, Pallas kernels, local(): pl.pallas_call(functools.partial(select_kernel, clusters, reps), in_specs...  4.51 us
    ppermute x1, waiting for transfers between devices, local(): edge_x = lax.ppermute(edge_x, 'dp', back_one)  1.96 us
    ppermute x1, waiting for transfers between devices, local(): far = lax.ppermute(far, 'rep', across)  1.94 us
  transfers between devices with their start and end apart: 4, of which 2 were waited for; matrix products, arithmetic and copies ran while one was open for 0% of the time, Pallas kernels for 1%

profile of v8, /device:TPU:0, one launch (start us, length us, event | category | flops | bytes accessed | tf_op | source)
XLA Modules:
  0.0 69.8 jit_solution(593446796500881022)
XLA Ops:
  0.0 4.5 %select_rows.1 = (bf16[32,192,128]{2,1,0:T(8,128)(2,1)S(1)}, s32[8,128]{1,0:T(8,128)S(1)}) custom-call(s32[8]{0:T(128)} %cap_in.1, s32[8]{0:T(128)} %adjacent_in.1, s32[8]{0:T(128)} %mask_in.1, s32[8,128]{1,0:T(8,128)} %bitcast.16, bf16[1024,4096]{1,0:T(8,128)(2,1)} %rows.1), custom_call_target="tpu_custom_call" | custom-call | tf_op jit(solution)/shard_map/select_rows/pallas_call | solution.py:446
  4.5 45.1 %all_to_all.10.got = bf16[32,192,128]{2,1,0:T(8,128)(2,1)S(1)} all-to-all(bf16[32,192,128]{2,1,0:T(8,128)(2,1)S(1)} %get-tuple-element.15), channel_id=1, replica_groups=mesh['dp'=8,'rep'=4] {'dp','rep'}, dimensions={0} | all-to-all | bytes 3145728 | tf_op jit(solution)/shard_map/all_to_all | solution.py:471
  49.6 1.2 %gather_far_tiles.1 = (bf16[768,1024]{1,0:T(8,128)(2,1)S(1)}, bf16[32,1024]{1,0:T(8,128)(2,1)S(1)}, f32[2,576,128]{2,1,0:T(8,128)S(1)}) custom-call(bf16[32,192,128]{2,1,0:T(8,128)(2,1)S(1)} %all_to_all.10.got), custom_call_target="tpu_custom_call" | custom-call | tf_op jit(solution)/shard_map/gather_far_tiles/pallas_call | solution.py:478
  50.8 0.1 collective-permute-start
  50.9 1.3 %collective-permute-start.1 = (bf16[32,1024]{1,0:T(8,128)(2,1)S(1)}, bf16[32,1024]{1,0:T(8,128)(2,1)S(1)}, u32[]{:S(2)}, u32[]{:S(2)}) collective-permute-start(bf16[32,1024]{1,0:T(8,128)(2,1)S(1)} %get-tuple-element.19), channel_id=1, source_target_pairs={{8,0},{16,8},{24,16},{28,24},{20,28},{12,20},{4,12},{0,4},{9,1},{1... | collective-permute-start | bytes 196616 | tf_op jit(solution)/shard_map/ppermute | solution.py:498
  52.3 0.0 collective-permute-done
  52.3 1.1 %collective-permute-start.2 = (f16[576,128]{1,0:T(8,128)(2,1)S(1)}, f16[576,128]{1,0:T(8,128)(2,1)S(1)}, u32[]{:S(2)}, u32[]{:S(2)}) collective-permute-start(f16[576,128]{1,0:T(8,128)(2,1)S(1)} %fusion), channel_id=1, source_target_pairs={{0,2},{2,0},{1,3},{3,1},{4,6},{6,4},{5,7},{7,5},{8,10},{10,8},{9,1... | collective-permute-start | bytes 442376 | tf_op jit(solution)/shard_map/ppermute | solution.py:501
  53.5 2.0 %collective-permute-done.1.edge_x = bf16[32,1024]{1,0:T(8,128)(2,1)S(1)} collective-permute-done((bf16[32,1024]{1,0:T(8,128)(2,1)S(1)}, bf16[32,1024]{1,0:T(8,128)(2,1)S(1)}, u32[]{:S(2)}, u32[]{:S(2)}) %collective-permute-start.1) | collective-permute-done | bytes 65568 | tf_op jit(solution)/shard_map/ppermute | solution.py:498
  55.4 0.8 %near_tiles.1 = (f32[2,576,128]{2,1,0:T(8,128)S(1)}, f32[64,128]{1,0:T(8,128)S(1)}) custom-call(bf16[768,1024]{1,0:T(8,128)(2,1)S(1)} %get-tuple-element.18.x, bf16[32,1024]{1,0:T(8,128)(2,1)S(1)} %collective-permute-done.1.edge_x), custom_call_target="tpu_custom_call" | custom-call | flops 603979776 | bytes 1572864 | tf_op jit(solution)/shard_map/near_tiles/pallas_call | solution.py:502
  56.3 0.1 collective-permute-start.3
  56.4 1.9 %collective-permute-done.2 = f16[576,128]{1,0:T(8,128)(2,1)S(1)} collective-permute-done((f16[576,128]{1,0:T(8,128)(2,1)S(1)}, f16[576,128]{1,0:T(8,128)(2,1)S(1)}, u32[]{:S(2)}, u32[]{:S(2)}) %collective-permute-start.2) | collective-permute-done | bytes 147488 | tf_op jit(solution)/shard_map/ppermute | solution.py:501
  58.3 0.0 collective-permute-done.3
  58.4 0.6 score_tiles.1
  59.0 10.1 %all_to_all.11 = f32[32,2,128]{2,1,0:T(2,128)S(1)} all-to-all(f32[32,2,128]{2,1,0:T(2,128)S(1)} %bitcast.15), channel_id=1, replica_groups=mesh['dp'=8,'rep'=4] {'dp','rep'}, dimensions={0} | all-to-all | bytes 65536 | tf_op jit(solution)/shard_map/all_to_all | solution.py:530
  69.1 0.8 %final_keep.1 = f32[8,128]{1,0:T(8,128)} custom-call(s32[8,128]{1,0:T(8,128)S(1)} %get-tuple-element.14.slots, f32[64,128]{1,0:T(8,128)S(1)} %bitcast.14), custom_call_target="tpu_custom_call" | custom-call | tf_op jit(solution)/shard_map/final_keep/pallas_call | solution.py:531
  (5 shorter events, 0.2 us)
Async XLA Ops:
  50.8 1.4 %collective-permute-start = (f16[576,128]{1,0:T(8,128)(2,1)S(1)}, f16[576,128]{1,0:T(8,128)(2,1)S(1)}, u32[]{:S(2)}, u32[]{:S(2)}) collective-permute-start(f16[576,128]{1,0:T(8,128)(2,1)S(1)} %fusion.1), channel_id=1, source_target_pairs={{0,1},{1,0},{2,3},{3,2},{4,5},{5,4},{6,7},{7,6},{8,9},{9,8},{10,11... | collective-permute-start | bytes 442376 | tf_op jit(solution)/shard_map/ppermute | solution.py:497
  50.9 4.5 %collective-permute-start.1 = (bf16[32,1024]{1,0:T(8,128)(2,1)S(1)}, bf16[32,1024]{1,0:T(8,128)(2,1)S(1)}, u32[]{:S(2)}, u32[]{:S(2)}) collective-permute-start(bf16[32,1024]{1,0:T(8,128)(2,1)S(1)} %get-tuple-element.19), channel_id=1, source_target_pairs={{8,0},{16,8},{24,16},{28,24},{20,28},{12,20},{4,12},{0,4},{9,1},{1... | collective-permute-start | bytes 196616 | tf_op jit(solution)/shard_map/ppermute | solution.py:498
  52.3 6.0 %collective-permute-start.2 = (f16[576,128]{1,0:T(8,128)(2,1)S(1)}, f16[576,128]{1,0:T(8,128)(2,1)S(1)}, u32[]{:S(2)}, u32[]{:S(2)}) collective-permute-start(f16[576,128]{1,0:T(8,128)(2,1)S(1)} %fusion), channel_id=1, source_target_pairs={{0,2},{2,0},{1,3},{3,1},{4,6},{6,4},{5,7},{7,5},{8,10},{10,8},{9,1... | collective-permute-start | bytes 442376 | tf_op jit(solution)/shard_map/ppermute | solution.py:501
  56.3 2.1 %collective-permute-start.3 = (f16[576,128]{1,0:T(8,128)(2,1)S(1)}, f16[576,128]{1,0:T(8,128)(2,1)S(1)}, u32[]{:S(2)}, u32[]{:S(2)}) collective-permute-start(f16[576,128]{1,0:T(8,128)(2,1)S(1)} %fusion.2), channel_id=1, source_target_pairs={{0,1},{1,0},{2,3},{3,2},{4,5},{5,4},{6,7},{7,6},{8,9},{9,8},{10,11... | collective-permute-start | bytes 442376 | tf_op jit(solution)/shard_map/ppermute | solution.py:516

commit v9 on v8

--- a/solution.py
+++ b/solution.py
@@ -186,26 +186,20 @@
     return -(-(1 + ranks) // GROUPS)
 
 
-def emit_tiles(y, core, x, edge_x, out, packed):
+def penalty(marks):
+    return jnp.where(marks > 2.0, PENALTY, 0.0)
+
+
+def emit_tiles(y, core, x, out):
     count, quarter = x.shape
     blocks = count // LANES
     contract = (((1,), (1,)), ((), ()))
     tiles = tile_sets(blocks)[y]
     marker = (iota((16, quarter), 1) == 0).astype(jnp.bfloat16)
-    extra = [marker] if edge_x is None else [edge_x[...], marker]
-    size = sum(e.shape[0] for e in extra)
-    edges = {}
 
     def put(owner, start, value):
         slot = (core == owner).astype(jnp.int32)
         out[slot, start : start + value.shape[0], :] = value
-
-    def penalty(marks):
-        return jnp.where(marks > 2.0, PENALTY, 0.0)
-
-    def note(gram, main, col0):
-        for k in range(gram.shape[1] // LANES):
-            edges.setdefault(col0 + k, gram[main : main + size - 16, k * LANES : (k + 1) * LANES])
 
     for p in range(0, blocks, 2):
         mine = [(e, t) for e, t in enumerate(tiles) if t[0] // 2 == p // 2]
@@ -216,13 +210,12 @@
         col0 = min(t[0] if t[2] else t[1] for _, t in mine)
         col1 = max(t[1] for _, t in mine) + 1
         rows = x[row0 * LANES : row1 * LANES, :]
-        left = jnp.concatenate([rows, *extra], axis=0)
+        left = jnp.concatenate([rows, marker], axis=0)
         right = x[col0 * LANES : col1 * LANES, :]
         gram = lax.dot_general(left, right, contract, preferred_element_type=jnp.float32)
         main = rows.shape[0]
-        col_pen = penalty(gram[main + size - 16 : main + size - 15])
+        col_pen = penalty(gram[main : main + 1])
         pairs = gram[:main] + penalty(rows[:, :1].astype(jnp.float32)) + col_pen
-        note(gram, main, col0)
 
         def tile(i, j, pairs=pairs, row0=row0, col0=col0):
             i, j = (i - row0) * LANES, (j - col0) * LANES
@@ -241,25 +234,18 @@
             else:
                 put(e % 2, e // 2 * LANES, value)
 
-    if edge_x is None:
-        return
-    first = min(edges)
-    if first:
-        near = edge_x[...]
-        note(
-            lax.dot_general(
-                near, x[: first * LANES, :], contract, preferred_element_type=jnp.float32
-            ),
-            0,
-            0,
-        )
-    reps = 4
+
+def edge_kernel(reps, x, edge_x, packed):
+    count = x.shape[0]
     ranks = edge_x.shape[0] // reps
-    row_pen = penalty(edge_x[:, :1].astype(jnp.float32))
+    contract = (((1,), (1,)), ((), ()))
+    near = edge_x[...]
+    edges = lax.dot_general(near, x[...], contract, preferred_element_type=jnp.float32)
+    edges = edges + penalty(near[:, :1].astype(jnp.float32))
     shape = (ranks, LANES)
     lines = []
-    for block in range(blocks):
-        edge = edges[block] + row_pen
+    for block in range(count // LANES):
+        edge = edges[:, block * LANES : (block + 1) * LANES]
         lane_of = lax.rem(lax.div(iota(shape, 1) + block * LANES, CAPS), reps)
         value = edge[:ranks]
         for lane in range(1, reps):
@@ -284,22 +270,13 @@
             packed[at : at + 1, :] = line
 
 
-def gather_kernel(ranks, got, x, edge_x, out, edge_rows):
+def gather_kernel(got, x, out):
     sources = got.shape[0]
-    quarter = x.shape[1]
-    tiles = quarter // LANES
-    reps = edge_x.shape[0] // ranks
+    tiles = x.shape[1] // LANES
     me = lax.axis_index("rep")
-    sub = iota((tiles, LANES), 0)
 
     def gather(pair):
         values = [got[2 * pair + k].astype(jnp.float32) for k in range(2)]
-        for k in range(2):
-            lines = jnp.zeros((tiles, LANES), jnp.float32)
-            for t in range(tiles):
-                line = jnp.broadcast_to(values[k][t * CAPS : t * CAPS + 1], lines.shape)
-                lines = jnp.where(sub == t, line, lines)
-            edge_rows[pl.ds((2 * pair + k) * tiles, tiles), :] = lines
         for t in range(tiles):
             rows = slice(t * CAPS, (t + 1) * CAPS)
             both = jnp.concatenate([v[rows] for v in values], axis=0)
@@ -309,21 +286,32 @@
 
     each(sources // 2, gather, 16)
 
-    for k in range(tiles):
-        lines = [
-            edge_rows[pl.ds(lane * tiles + k, ranks, stride=reps * tiles), :]
-            for lane in range(reps)
-        ]
-        edge_x[:, k * LANES : (k + 1) * LANES] = jnp.concatenate(lines, axis=0).astype(jnp.bfloat16)
-
     for y in range(2):
-        pl.when(me // 2 != y)(functools.partial(emit_tiles, y, me % 2, x, None, out, None))
-
-
-def near_kernel(x, edge_x, out, packed):
+        pl.when(me // 2 != y)(functools.partial(emit_tiles, y, me % 2, x, out))
+
+
+def first_rows_kernel(reps, x, edge_x):
+    ranks = edge_x.shape[0] // reps
+    shape = (8, x.shape[1])
+    sub = iota(shape, 0)
+    for first in range(0, edge_x.shape[0], 16):
+        halves = []
+        for start in (first, first + 8):
+            lines = jnp.zeros(shape, jnp.float32)
+            for k in range(8):
+                lane, rank = divmod(start + k, ranks)
+                at = (rank * reps + lane) * CAPS
+                rows = x[at // 16 * 16 : at // 16 * 16 + 16, :].astype(jnp.float32)
+                line = jnp.broadcast_to(rows[at % 16 : at % 16 + 1], shape)
+                lines = jnp.where(sub == k, line, lines)
+            halves.append(lines)
+        edge_x[first : first + 16, :] = jnp.concatenate(halves, axis=0).astype(jnp.bfloat16)
+
+
+def near_kernel(x, out):
     me = lax.axis_index("rep")
     for y in range(2):
-        pl.when(me // 2 == y)(functools.partial(emit_tiles, y, me % 2, x, edge_x, out, packed))
+        pl.when(me // 2 == y)(functools.partial(emit_tiles, y, me % 2, x, out))
 
 
 def score_kernel(sources, sums, logits, out, total):
@@ -475,19 +463,25 @@
     part_rows = set_rows(group)
     height = back_rows(dp_count)
     near_bytes = (2 * part_rows + devices * height) * LANES * 4
-    x, edge_x, far_parts = pl.pallas_call(
-        functools.partial(gather_kernel, dp_count),
+    x, far_parts = pl.pallas_call(
+        gather_kernel,
         in_specs=[vmem],
-        out_specs=[vmem] * 3,
+        out_specs=[vmem] * 2,
         out_shape=[
             jax.ShapeDtypeStruct((count, quarter), jnp.bfloat16),
-            jax.ShapeDtypeStruct((reps * dp_count, quarter), jnp.bfloat16),
             jax.ShapeDtypeStruct((2, part_rows, LANES), jnp.float32),
         ],
-        scratch_shapes=[pltpu.VMEM((devices * tiles, LANES), jnp.float32)],
         compiler_params=grant(6 * count * quarter + near_bytes),
         name="gather_far_tiles",
     )(got)
+    edge_x = pl.pallas_call(
+        functools.partial(first_rows_kernel, reps),
+        in_specs=[vmem],
+        out_specs=vmem,
+        out_shape=jax.ShapeDtypeStruct((reps * dp_count, quarter), jnp.bfloat16),
+        compiler_params=grant(4 * count * quarter),
+        name="first_rows",
+    )(x)
 
     wire = jnp.float16
     cores = [(0, 1), (1, 0), (2, 3), (3, 2)]
@@ -499,22 +493,31 @@
     far = (far_parts[1] + far.astype(jnp.float32)).astype(wire)
     far, x = lax.optimization_barrier((far, x))
     far = lax.ppermute(far, "rep", across)
-    near_parts, packed = pl.pallas_call(
+    near_parts = pl.pallas_call(
         near_kernel,
-        in_specs=[vmem] * 2,
-        out_specs=[vmem] * 2,
-        out_shape=[
-            jax.ShapeDtypeStruct((2, part_rows, LANES), jnp.float32),
-            jax.ShapeDtypeStruct((devices * height, LANES), jnp.float32),
-        ],
+        in_specs=[vmem],
+        out_specs=vmem,
+        out_shape=jax.ShapeDtypeStruct((2, part_rows, LANES), jnp.float32),
         compiler_params=grant(4 * count * quarter + near_bytes),
         cost_estimate=pl.CostEstimate(
             flops=count * count * quarter, bytes_accessed=2 * count * quarter, transcendentals=0
         ),
         name="near_tiles",
+    )(x)
+    packed = pl.pallas_call(
+        functools.partial(edge_kernel, reps),
+        in_specs=[vmem] * 2,
+        out_specs=vmem,
+        out_shape=jax.ShapeDtypeStruct((devices * height, LANES), jnp.float32),
+        compiler_params=grant(4 * count * quarter + near_bytes),
+        cost_estimate=pl.CostEstimate(
+            flops=count * count * quarter, bytes_accessed=2 * count * quarter, transcendentals=0
+        ),
+        name="edge_logits",
     )(x, edge_x)
     near = lax.ppermute(near_parts[0].astype(wire), "rep", cores)
-    both = near_parts[1] + far.astype(jnp.float32)
+    near_kept, packed = lax.optimization_barrier((near_parts[1], packed))
+    both = near_kept + far.astype(jnp.float32)
     both = lax.optimization_barrier(both) + near.astype(jnp.float32)
 
     sums = pl.pallas_call(

time: 70 us -> 69.9 us (level)
    pallas_call x2 -> x4, Pallas kernels: 2 us -> 2.52 us  [the longest x1 1.03 us: local(): pl.pallas_call(gather_kernel, in_specs=[vmem], out_specs=[vmem] * 2, out_...]
  transfers between devices with their start and end apart: 4 -> 4, of which waited for: 2 -> 2; matrix products, arithmetic and copies ran while one was open for 0% -> 0% of each run, Pallas kernels for 1% -> 2%
where the time goes in v9:
time: 69.9 us; the launch traced here: 69.7 us
  blocking collectives  55 us (79%)
  Pallas kernels  8.4 us (12%)
  waiting for transfers between devices  3.39 us (5%)
  starting transfers between devices  2.61 us (4%)
    all_to_all x1, blocking collectives, local(): got = lax.all_to_all(send, ALL, split_axis=0, concat_axis=0, tiled=True)  45.1 us
    all_to_all x1, blocking collectives, local(): back = lax.all_to_all(sums, ALL, split_axis=0, concat_axis=0, tiled=True)  9.9 us
    pallas_call x1, Pallas kernels, local(): pl.pallas_call(functools.partial(select_kernel, clusters, reps), in_specs...  4.51 us
    ppermute x1, waiting for transfers between devices, local(): far = lax.ppermute(far, 'rep', across)  2.12 us
  transfers between devices with their start and end apart: 4, of which 2 were waited for; matrix products, arithmetic and copies ran while one was open for 0% of the time, Pallas kernels for 2%

profile of v9, /device:TPU:0, one launch (start us, length us, event | category | flops | bytes accessed | tf_op | source)
XLA Modules:
  0.0 69.7 jit_solution(1177953171987417404)
XLA Ops:
  0.0 4.5 %select_rows.1 = (bf16[32,192,128]{2,1,0:T(8,128)(2,1)S(1)}, s32[8,128]{1,0:T(8,128)S(1)}) custom-call(s32[8]{0:T(128)} %cap_in.1, s32[8]{0:T(128)} %adjacent_in.1, s32[8]{0:T(128)} %mask_in.1, s32[8,128]{1,0:T(8,128)} %bitcast.16, bf16[1024,4096]{1,0:T(8,128)(2,1)} %rows.1), custom_call_target="tpu_custom_call" | custom-call | tf_op jit(solution)/shard_map/select_rows/pallas_call | solution.py:434
  4.5 45.1 %all_to_all.10.got = bf16[32,192,128]{2,1,0:T(8,128)(2,1)S(1)} all-to-all(bf16[32,192,128]{2,1,0:T(8,128)(2,1)S(1)} %get-tuple-element.14), channel_id=1, replica_groups=mesh['dp'=8,'rep'=4] {'dp','rep'}, dimensions={0} | all-to-all | bytes 3145728 | tf_op jit(solution)/shard_map/all_to_all | solution.py:459
  49.6 1.0 %gather_far_tiles.1 = (bf16[768,1024]{1,0:T(8,128)(2,1)S(1)}, f32[2,576,128]{2,1,0:T(8,128)S(1)}) custom-call(bf16[32,192,128]{2,1,0:T(8,128)(2,1)S(1)} %all_to_all.10.got), custom_call_target="tpu_custom_call" | custom-call | tf_op jit(solution)/shard_map/gather_far_tiles/pallas_call | solution.py:466
  50.7 0.1 collective-permute-start
  50.8 0.1 first_rows.1
  50.9 1.3 %collective-permute-start.1 = (bf16[32,1024]{1,0:T(8,128)(2,1)S(1)}, bf16[32,1024]{1,0:T(8,128)(2,1)S(1)}, u32[]{:S(2)}, u32[]{:S(2)}) collective-permute-start(bf16[32,1024]{1,0:T(8,128)(2,1)S(1)} %first_rows.1), channel_id=1, source_target_pairs={{8,0},{16,8},{24,16},{28,24},{20,28},{12,20},{4,12},{0,4},{9,1},{1... | collective-permute-start | bytes 196616 | tf_op jit(solution)/shard_map/ppermute | solution.py:492
  52.2 0.0 collective-permute-done
  52.3 1.1 %collective-permute-start.2 = (f16[576,128]{1,0:T(8,128)(2,1)S(1)}, f16[576,128]{1,0:T(8,128)(2,1)S(1)}, u32[]{:S(2)}, u32[]{:S(2)}) collective-permute-start(f16[576,128]{1,0:T(8,128)(2,1)S(1)} %fusion), channel_id=1, source_target_pairs={{0,2},{2,0},{1,3},{3,1},{4,6},{6,4},{5,7},{7,5},{8,10},{10,8},{9,1... | collective-permute-start | bytes 442376 | tf_op jit(solution)/shard_map/ppermute | solution.py:495
  53.4 0.7 near_tiles.1
  54.2 1.3 %collective-permute-done.1.edge_x = bf16[32,1024]{1,0:T(8,128)(2,1)S(1)} collective-permute-done((bf16[32,1024]{1,0:T(8,128)(2,1)S(1)}, bf16[32,1024]{1,0:T(8,128)(2,1)S(1)}, u32[]{:S(2)}, u32[]{:S(2)}) %collective-permute-start.1) | collective-permute-done | bytes 65568 | tf_op jit(solution)/shard_map/ppermute | solution.py:492
  55.4 0.7 edge_logits.1.logits
  56.1 0.1 collective-permute-start.3
  56.2 2.1 %collective-permute-done.2 = f16[576,128]{1,0:T(8,128)(2,1)S(1)} collective-permute-done((f16[576,128]{1,0:T(8,128)(2,1)S(1)}, f16[576,128]{1,0:T(8,128)(2,1)S(1)}, u32[]{:S(2)}, u32[]{:S(2)}) %collective-permute-start.2) | collective-permute-done | bytes 147488 | tf_op jit(solution)/shard_map/ppermute | solution.py:495
  58.4 0.0 collective-permute-done.3
  58.4 0.6 score_tiles.1
  59.0 9.9 %all_to_all.11 = f32[32,2,128]{2,1,0:T(2,128)S(1)} all-to-all(f32[32,2,128]{2,1,0:T(2,128)S(1)} %bitcast.15), channel_id=1, replica_groups=mesh['dp'=8,'rep'=4] {'dp','rep'}, dimensions={0} | all-to-all | bytes 65536 | tf_op jit(solution)/shard_map/all_to_all | solution.py:533
  68.9 0.8 %final_keep.1 = f32[8,128]{1,0:T(8,128)} custom-call(s32[8,128]{1,0:T(8,128)S(1)} %get-tuple-element.13.slots, f32[64,128]{1,0:T(8,128)S(1)} %bitcast.14), custom_call_target="tpu_custom_call" | custom-call | tf_op jit(solution)/shard_map/final_keep/pallas_call | solution.py:534
  (5 shorter events, 0.2 us)
Async XLA Ops:
  50.7 1.5 %collective-permute-start = (f16[576,128]{1,0:T(8,128)(2,1)S(1)}, f16[576,128]{1,0:T(8,128)(2,1)S(1)}, u32[]{:S(2)}, u32[]{:S(2)}) collective-permute-start(f16[576,128]{1,0:T(8,128)(2,1)S(1)} %fusion.1), channel_id=1, source_target_pairs={{0,1},{1,0},{2,3},{3,2},{4,5},{5,4},{6,7},{7,6},{8,9},{9,8},{10,11... | collective-permute-start | bytes 442376 | tf_op jit(solution)/shard_map/ppermute | solution.py:491
  50.9 4.5 %collective-permute-start.1 = (bf16[32,1024]{1,0:T(8,128)(2,1)S(1)}, bf16[32,1024]{1,0:T(8,128)(2,1)S(1)}, u32[]{:S(2)}, u32[]{:S(2)}) collective-permute-start(bf16[32,1024]{1,0:T(8,128)(2,1)S(1)} %first_rows.1), channel_id=1, source_target_pairs={{8,0},{16,8},{24,16},{28,24},{20,28},{12,20},{4,12},{0,4},{9,1},{1... | collective-permute-start | bytes 196616 | tf_op jit(solution)/shard_map/ppermute | solution.py:492
  52.3 6.0 %collective-permute-start.2 = (f16[576,128]{1,0:T(8,128)(2,1)S(1)}, f16[576,128]{1,0:T(8,128)(2,1)S(1)}, u32[]{:S(2)}, u32[]{:S(2)}) collective-permute-start(f16[576,128]{1,0:T(8,128)(2,1)S(1)} %fusion), channel_id=1, source_target_pairs={{0,2},{2,0},{1,3},{3,1},{4,6},{6,4},{5,7},{7,5},{8,10},{10,8},{9,1... | collective-permute-start | bytes 442376 | tf_op jit(solution)/shard_map/ppermute | solution.py:495
  56.1 2.2 %collective-permute-start.3 = (f16[576,128]{1,0:T(8,128)(2,1)S(1)}, f16[576,128]{1,0:T(8,128)(2,1)S(1)}, u32[]{:S(2)}, u32[]{:S(2)}) collective-permute-start(f16[576,128]{1,0:T(8,128)(2,1)S(1)} %get-tuple-element.21), channel_id=1, source_target_pairs={{0,1},{1,0},{2,3},{3,2},{4,5},{5,4},{6,7},{7,6},{8,9},{9,8},{10,11... | collective-permute-start | bytes 442376 | tf_op jit(solution)/shard_map/ppermute | solution.py:518

commit v10 on v9

--- a/solution.py
+++ b/solution.py
@@ -252,22 +252,27 @@
             value = jnp.where(lane_of == lane, edge[lane * ranks : (lane + 1) * ranks], value)
         lines.append(value)
 
-    height = back_rows(ranks)
+    half = ranks // 2
+    height = back_rows(half)
     spot = iota((1, LANES), 1)
+    me = lax.axis_index("rep")
     for source in range(count // CAPS):
         block, offset = divmod(source * CAPS, LANES)
         value = lines[block]
         if offset + CAPS > LANES:
             value = jnp.where(iota(shape, 1) >= offset, value, lines[block + 1])
         turned = [pltpu.roll(value, (k * CAPS - offset) % LANES, 1) for k in range(GROUPS)]
-        for row in range(height):
-            line = jnp.zeros((1, LANES), jnp.float32)
-            for k in range(GROUPS):
-                j = row * GROUPS + k - 1
-                if 0 <= j < ranks:
-                    line = jnp.where(spot >= k * CAPS, turned[k][j : j + 1, :], line)
-            at = source * height + row
-            packed[at : at + 1, :] = line
+        for core in range(2):
+            slot = (me % 2 == core).astype(jnp.int32)
+            for row in range(height):
+                line = jnp.zeros((1, LANES), jnp.float32)
+                for k in range(GROUPS):
+                    j = row * GROUPS + k - 1
+                    if 0 <= j < half:
+                        picked = turned[k][core * half + j : core * half + j + 1, :]
+                        line = jnp.where(spot >= k * CAPS, picked, line)
+                at = source * height + row
+                packed[slot, at : at + 1, :] = line
 
 
 def gather_kernel(got, x, out):
@@ -386,22 +391,21 @@
 
 def final_kernel(clusters, reps, slots, sums, out):
     height = sums.shape[0] // (clusters * reps)
-    ranks = clusters
+    half = clusters // 2
     slot = slots[...]
 
-    def gathered(row):
-        lines = []
-        for c in range(clusters):
-            starts = [(c * reps + q) * height + row for q in range(reps)]
-            lines.append(sum(sums[at : at + 1, :] for at in starts))
-        return jnp.concatenate(lines, axis=0)
-
-    rows = [gathered(row) for row in range(height)]
-    edges = [jax.nn.sigmoid(slope_gain * (r - edge_cut)) for r in rows]
-    inner = rows[0]
+    def part(q, row):
+        return sums[pl.ds(q * height + row, clusters, stride=reps * height), :]
+
+    inner = sum(part(q, 0) for q in range(reps))
+    edges = []
+    for row in range(height):
+        logits = [part(core, row) + part(core + 2, row) for core in range(2)]
+        edges.append(sum(jax.nn.sigmoid(slope_gain * (x - edge_cut)) for x in logits))
     for k in range(GROUPS):
-        mine = [r for r in range(height) if 1 <= r * GROUPS + k <= ranks]
-        inner += pltpu.roll(sum(edges[r] for r in mine), (-k * CAPS) % LANES, 1)
+        mine = [edges[r] for r in range(height) if 1 <= r * GROUPS + k <= half]
+        if mine:
+            inner += pltpu.roll(sum(mine), (-k * CAPS) % LANES, 1)
     board = 1.0 / (1.0 + inner)
     result = jnp.ones(slot.shape, jnp.float32)
     for c in range(clusters):
@@ -461,8 +465,8 @@
     count = devices * CAPS
     group = count // LANES
     part_rows = set_rows(group)
-    height = back_rows(dp_count)
-    near_bytes = (2 * part_rows + devices * height) * LANES * 4
+    height = back_rows(dp_count // 2)
+    near_bytes = (2 * part_rows + 2 * devices * height) * LANES * 4
     x, far_parts = pl.pallas_call(
         gather_kernel,
         in_specs=[vmem],
@@ -508,17 +512,18 @@
         functools.partial(edge_kernel, reps),
         in_specs=[vmem] * 2,
         out_specs=vmem,
-        out_shape=jax.ShapeDtypeStruct((devices * height, LANES), jnp.float32),
+        out_shape=jax.ShapeDtypeStruct((2, devices * height, LANES), jnp.float32),
         compiler_params=grant(4 * count * quarter + near_bytes),
         cost_estimate=pl.CostEstimate(
             flops=count * count * quarter, bytes_accessed=2 * count * quarter, transcendentals=0
         ),
         name="edge_logits",
     )(x, edge_x)
-    near = lax.ppermute(near_parts[0].astype(wire), "rep", cores)
-    near_kept, packed = lax.optimization_barrier((near_parts[1], packed))
-    both = near_kept + far.astype(jnp.float32)
-    both = lax.optimization_barrier(both) + near.astype(jnp.float32)
+    near = jnp.concatenate([near_parts[0], packed[0]]).astype(wire)
+    near = lax.ppermute(near, "rep", cores)
+    both = near_parts[1] + far.astype(jnp.float32)
+    both = lax.optimization_barrier(both) + near[:part_rows].astype(jnp.float32)
+    logits = packed[1] + near[part_rows:].astype(jnp.float32)
 
     sums = pl.pallas_call(
         functools.partial(score_kernel, devices),
@@ -528,7 +533,7 @@
         scratch_shapes=[pltpu.VMEM((-(-group // 8) * 8, LANES), jnp.float32)],
         compiler_params=grant(near_bytes),
         name="score_tiles",
-    )(both, packed).reshape(devices, height, LANES)
+    )(both, logits).reshape(devices, height, LANES)
 
     back = lax.all_to_all(sums, ALL, split_axis=0, concat_axis=0, tiled=True)
     keep = pl.pallas_call(

time: 69.9 us -> 69.8 us (level)
  no operation moved by 1% of the time
where the time goes in v10:
time: 69.8 us; the launch traced here: 69.6 us
  blocking collectives  54.9 us (79%)
  Pallas kernels  8.38 us (12%)
  waiting for transfers between devices  3.35 us (5%)
  starting transfers between devices  2.61 us (4%)
    all_to_all x1, blocking collectives, local(): got = lax.all_to_all(send, ALL, split_axis=0, concat_axis=0, tiled=True)  45.1 us
    all_to_all x1, blocking collectives, local(): back = lax.all_to_all(sums, ALL, split_axis=0, concat_axis=0, tiled=True)  9.8 us
    pallas_call x1, Pallas kernels, local(): pl.pallas_call(functools.partial(select_kernel, clusters, reps), in_specs...  4.51 us
    ppermute x1, waiting for transfers between devices, local(): far = lax.ppermute(far, 'rep', across)  2.06 us
  transfers between devices with their start and end apart: 4, of which 2 were waited for; matrix products, arithmetic and copies ran while one was open for 0% of the time, Pallas kernels for 2%

profile of v10, /device:TPU:0, one launch (start us, length us, event | category | flops | bytes accessed | tf_op | source)
XLA Modules:
  0.0 69.6 jit_solution(16012744871342775222)
XLA Ops:
  0.0 4.5 %select_rows.1 = (bf16[32,192,128]{2,1,0:T(8,128)(2,1)S(1)}, s32[8,128]{1,0:T(8,128)S(1)}) custom-call(s32[8]{0:T(128)} %cap_in.1, s32[8]{0:T(128)} %adjacent_in.1, s32[8]{0:T(128)} %mask_in.1, s32[8,128]{1,0:T(8,128)} %bitcast.26, bf16[1024,4096]{1,0:T(8,128)(2,1)} %rows.1), custom_call_target="tpu_custom_call" | custom-call | tf_op jit(solution)/shard_map/select_rows/pallas_call | solution.py:438
  4.5 45.1 %all_to_all.10.got = bf16[32,192,128]{2,1,0:T(8,128)(2,1)S(1)} all-to-all(bf16[32,192,128]{2,1,0:T(8,128)(2,1)S(1)} %get-tuple-element.12), channel_id=1, replica_groups=mesh['dp'=8,'rep'=4] {'dp','rep'}, dimensions={0} | all-to-all | bytes 3145728 | tf_op jit(solution)/shard_map/all_to_all | solution.py:463
  49.6 1.0 %gather_far_tiles.1 = (bf16[768,1024]{1,0:T(8,128)(2,1)S(1)}, f32[2,576,128]{2,1,0:T(8,128)S(1)}) custom-call(bf16[32,192,128]{2,1,0:T(8,128)(2,1)S(1)} %all_to_all.10.got), custom_call_target="tpu_custom_call" | custom-call | tf_op jit(solution)/shard_map/gather_far_tiles/pallas_call | solution.py:470
  50.7 0.1 collective-permute-start
  50.8 0.1 first_rows.1
  50.9 1.3 %collective-permute-start.2 = (bf16[32,1024]{1,0:T(8,128)(2,1)S(1)}, bf16[32,1024]{1,0:T(8,128)(2,1)S(1)}, u32[]{:S(2)}, u32[]{:S(2)}) collective-permute-start(bf16[32,1024]{1,0:T(8,128)(2,1)S(1)} %first_rows.1), channel_id=1, source_target_pairs={{8,0},{16,8},{24,16},{28,24},{20,28},{12,20},{4,12},{0,4},{9,1},{1... | collective-permute-start | bytes 196616 | tf_op jit(solution)/shard_map/ppermute | solution.py:496
  52.2 0.0 collective-permute-done
  52.3 1.1 %collective-permute-start.1 = (f16[576,128]{1,0:T(8,128)(2,1)S(1)}, f16[576,128]{1,0:T(8,128)(2,1)S(1)}, u32[]{:S(2)}, u32[]{:S(2)}) collective-permute-start(f16[576,128]{1,0:T(8,128)(2,1)S(1)} %fusion.1), channel_id=1, source_target_pairs={{0,2},{2,0},{1,3},{3,1},{4,6},{6,4},{5,7},{7,5},{8,10},{10,8},{9,1... | collective-permute-start | bytes 442376 | tf_op jit(solution)/shard_map/ppermute | solution.py:499
  53.4 0.7 near_tiles.1
  54.2 1.3 %collective-permute-done.2.edge_x = bf16[32,1024]{1,0:T(8,128)(2,1)S(1)} collective-permute-done((bf16[32,1024]{1,0:T(8,128)(2,1)S(1)}, bf16[32,1024]{1,0:T(8,128)(2,1)S(1)}, u32[]{:S(2)}, u32[]{:S(2)}) %collective-permute-start.2) | collective-permute-done | bytes 65568 | tf_op jit(solution)/shard_map/ppermute | solution.py:496
  55.4 0.7 edge_logits.1
  56.2 0.1 collective-permute-start.3
  56.3 2.1 %collective-permute-done.1 = f16[576,128]{1,0:T(8,128)(2,1)S(1)} collective-permute-done((f16[576,128]{1,0:T(8,128)(2,1)S(1)}, f16[576,128]{1,0:T(8,128)(2,1)S(1)}, u32[]{:S(2)}, u32[]{:S(2)}) %collective-permute-start.1) | collective-permute-done | bytes 147488 | tf_op jit(solution)/shard_map/ppermute | solution.py:499
  58.4 0.0 collective-permute-done.3
  58.4 0.6 score_tiles.1
  59.0 9.8 %all_to_all.11 = f32[32,1,128]{2,1,0:T(1,128)S(1)} all-to-all(f32[32,1,128]{2,1,0:T(1,128)S(1)} %bitcast.24), channel_id=1, replica_groups=mesh['dp'=8,'rep'=4] {'dp','rep'}, dimensions={0} | all-to-all | bytes 32768 | tf_op jit(solution)/shard_map/all_to_all | solution.py:538
  68.8 0.8 %final_keep.1 = f32[8,128]{1,0:T(8,128)} custom-call(s32[8,128]{1,0:T(8,128)S(1)} %get-tuple-element.11.slots, f32[32,128]{1,0:T(8,128)S(1)} %bitcast.25), custom_call_target="tpu_custom_call" | custom-call | tf_op jit(solution)/shard_map/final_keep/pallas_call | solution.py:539
  (8 shorter events, 0.2 us)
Async XLA Ops:
  50.7 1.5 %collective-permute-start = (f16[576,128]{1,0:T(8,128)(2,1)S(1)}, f16[576,128]{1,0:T(8,128)(2,1)S(1)}, u32[]{:S(2)}, u32[]{:S(2)}) collective-permute-start(f16[576,128]{1,0:T(8,128)(2,1)S(1)} %fusion.2), channel_id=1, source_target_pairs={{0,1},{1,0},{2,3},{3,2},{4,5},{5,4},{6,7},{7,6},{8,9},{9,8},{10,11... | collective-permute-start | bytes 442376 | tf_op jit(solution)/shard_map/ppermute | solution.py:495
  50.9 4.5 %collective-permute-start.2 = (bf16[32,1024]{1,0:T(8,128)(2,1)S(1)}, bf16[32,1024]{1,0:T(8,128)(2,1)S(1)}, u32[]{:S(2)}, u32[]{:S(2)}) collective-permute-start(bf16[32,1024]{1,0:T(8,128)(2,1)S(1)} %first_rows.1), channel_id=1, source_target_pairs={{8,0},{16,8},{24,16},{28,24},{20,28},{12,20},{4,12},{0,4},{9,1},{1... | collective-permute-start | bytes 196616 | tf_op jit(solution)/shard_map/ppermute | solution.py:496
  52.3 6.0 %collective-permute-start.1 = (f16[576,128]{1,0:T(8,128)(2,1)S(1)}, f16[576,128]{1,0:T(8,128)(2,1)S(1)}, u32[]{:S(2)}, u32[]{:S(2)}) collective-permute-start(f16[576,128]{1,0:T(8,128)(2,1)S(1)} %fusion.1), channel_id=1, source_target_pairs={{0,2},{2,0},{1,3},{3,1},{4,6},{6,4},{5,7},{7,5},{8,10},{10,8},{9,1... | collective-permute-start | bytes 442376 | tf_op jit(solution)/shard_map/ppermute | solution.py:499
  56.2 2.2 %collective-permute-start.3 = (f16[608,128]{1,0:T(8,128)(2,1)S(1)}, f16[608,128]{1,0:T(8,128)(2,1)S(1)}, u32[]{:S(2)}, u32[]{:S(2)}) collective-permute-start(f16[608,128]{1,0:T(8,128)(2,1)S(1)} %pad_maximum_fusion), channel_id=1, source_target_pairs={{0,1},{1,0},{2,3},{3,2},{4,5},{5,4},{6,7},{7,6},{8,9},{9,8},{10,11... | collective-permute-start | bytes 466952 | tf_op jit(solution)/shard_map/ppermute | solution.py:523

commit v11 on v10

--- a/solution.py
+++ b/solution.py
@@ -75,14 +75,14 @@
         pltpu.make_async_copy(rows.at[i * deep : (i + 1) * deep, :], data.at[i], in_sem.at[i])
         for i in range(steps)
     ]
-    for read in reads:
-        read.start()
     wanted = ((assign_in, assign), (mask_in, mask), (cap_in, cap), (adjacent_in, adjacent))
     smalls = [
         pltpu.make_async_copy(here, there, small_sem.at[k]) for k, (here, there) in enumerate(wanted)
     ]
     for small in smalls:
         small.start()
+    for read in reads:
+        read.start()
     for small in smalls:
         small.wait()
 

time: 69.8 us -> 69.8 us (level)
  no operation moved by 1% of the time
where the time goes in v11:
time: 69.8 us; the launch traced here: 69.6 us
  blocking collectives  54.9 us (79%)
  Pallas kernels  8.37 us (12%)
  waiting for transfers between devices  3.35 us (5%)
  starting transfers between devices  2.61 us (4%)
    all_to_all x1, blocking collectives, local(): got = lax.all_to_all(send, ALL, split_axis=0, concat_axis=0, tiled=True)  45.1 us
    all_to_all x1, blocking collectives, local(): back = lax.all_to_all(sums, ALL, split_axis=0, concat_axis=0, tiled=True)  9.8 us
    pallas_call x1, Pallas kernels, local(): pl.pallas_call(functools.partial(select_kernel, clusters, reps), in_specs...  4.5 us
    ppermute x1, waiting for transfers between devices, local(): far = lax.ppermute(far, 'rep', across)  2.06 us
  transfers between devices with their start and end apart: 4, of which 2 were waited for; matrix products, arithmetic and copies ran while one was open for 0% of the time, Pallas kernels for 2%

profile of v11, /device:TPU:0, one launch (start us, length us, event | category | flops | bytes accessed | tf_op | source)
XLA Modules:
  0.0 69.6 jit_solution(17057462739059446685)
XLA Ops:
  0.0 4.5 %select_rows.1 = (bf16[32,192,128]{2,1,0:T(8,128)(2,1)S(1)}, s32[8,128]{1,0:T(8,128)S(1)}) custom-call(s32[8]{0:T(128)} %cap_in.1, s32[8]{0:T(128)} %adjacent_in.1, s32[8]{0:T(128)} %mask_in.1, s32[8,128]{1,0:T(8,128)} %bitcast.26, bf16[1024,4096]{1,0:T(8,128)(2,1)} %rows.1), custom_call_target="tpu_custom_call" | custom-call | tf_op jit(solution)/shard_map/select_rows/pallas_call | solution.py:438
  4.5 45.1 %all_to_all.10.got = bf16[32,192,128]{2,1,0:T(8,128)(2,1)S(1)} all-to-all(bf16[32,192,128]{2,1,0:T(8,128)(2,1)S(1)} %get-tuple-element.12), channel_id=1, replica_groups=mesh['dp'=8,'rep'=4] {'dp','rep'}, dimensions={0} | all-to-all | bytes 3145728 | tf_op jit(solution)/shard_map/all_to_all | solution.py:463
  49.6 1.0 %gather_far_tiles.1 = (bf16[768,1024]{1,0:T(8,128)(2,1)S(1)}, f32[2,576,128]{2,1,0:T(8,128)S(1)}) custom-call(bf16[32,192,128]{2,1,0:T(8,128)(2,1)S(1)} %all_to_all.10.got), custom_call_target="tpu_custom_call" | custom-call | tf_op jit(solution)/shard_map/gather_far_tiles/pallas_call | solution.py:470
  50.7 0.1 collective-permute-start
  50.8 0.1 first_rows.1
  50.9 1.3 %collective-permute-start.2 = (bf16[32,1024]{1,0:T(8,128)(2,1)S(1)}, bf16[32,1024]{1,0:T(8,128)(2,1)S(1)}, u32[]{:S(2)}, u32[]{:S(2)}) collective-permute-start(bf16[32,1024]{1,0:T(8,128)(2,1)S(1)} %first_rows.1), channel_id=1, source_target_pairs={{8,0},{16,8},{24,16},{28,24},{20,28},{12,20},{4,12},{0,4},{9,1},{1... | collective-permute-start | bytes 196616 | tf_op jit(solution)/shard_map/ppermute | solution.py:496
  52.2 0.0 collective-permute-done
  52.3 1.1 %collective-permute-start.1 = (f16[576,128]{1,0:T(8,128)(2,1)S(1)}, f16[576,128]{1,0:T(8,128)(2,1)S(1)}, u32[]{:S(2)}, u32[]{:S(2)}) collective-permute-start(f16[576,128]{1,0:T(8,128)(2,1)S(1)} %fusion.1), channel_id=1, source_target_pairs={{0,2},{2,0},{1,3},{3,1},{4,6},{6,4},{5,7},{7,5},{8,10},{10,8},{9,1... | collective-permute-start | bytes 442376 | tf_op jit(solution)/shard_map/ppermute | solution.py:499
  53.4 0.7 near_tiles.1
  54.2 1.3 %collective-permute-done.2.edge_x = bf16[32,1024]{1,0:T(8,128)(2,1)S(1)} collective-permute-done((bf16[32,1024]{1,0:T(8,128)(2,1)S(1)}, bf16[32,1024]{1,0:T(8,128)(2,1)S(1)}, u32[]{:S(2)}, u32[]{:S(2)}) %collective-permute-start.2) | collective-permute-done | bytes 65568 | tf_op jit(solution)/shard_map/ppermute | solution.py:496
  55.4 0.7 edge_logits.1
  56.2 0.1 collective-permute-start.3
  56.3 2.1 %collective-permute-done.1 = f16[576,128]{1,0:T(8,128)(2,1)S(1)} collective-permute-done((f16[576,128]{1,0:T(8,128)(2,1)S(1)}, f16[576,128]{1,0:T(8,128)(2,1)S(1)}, u32[]{:S(2)}, u32[]{:S(2)}) %collective-permute-start.1) | collective-permute-done | bytes 147488 | tf_op jit(solution)/shard_map/ppermute | solution.py:499
  58.4 0.0 collective-permute-done.3
  58.4 0.6 score_tiles.1
  59.0 9.8 %all_to_all.11 = f32[32,1,128]{2,1,0:T(1,128)S(1)} all-to-all(f32[32,1,128]{2,1,0:T(1,128)S(1)} %bitcast.24), channel_id=1, replica_groups=mesh['dp'=8,'rep'=4] {'dp','rep'}, dimensions={0} | all-to-all | bytes 32768 | tf_op jit(solution)/shard_map/all_to_all | solution.py:538
  68.8 0.8 %final_keep.1 = f32[8,128]{1,0:T(8,128)} custom-call(s32[8,128]{1,0:T(8,128)S(1)} %get-tuple-element.11.slots, f32[32,128]{1,0:T(8,128)S(1)} %bitcast.25), custom_call_target="tpu_custom_call" | custom-call | tf_op jit(solution)/shard_map/final_keep/pallas_call | solution.py:539
  (8 shorter events, 0.2 us)
Async XLA Ops:
  50.7 1.5 %collective-permute-start = (f16[576,128]{1,0:T(8,128)(2,1)S(1)}, f16[576,128]{1,0:T(8,128)(2,1)S(1)}, u32[]{:S(2)}, u32[]{:S(2)}) collective-permute-start(f16[576,128]{1,0:T(8,128)(2,1)S(1)} %fusion.2), channel_id=1, source_target_pairs={{0,1},{1,0},{2,3},{3,2},{4,5},{5,4},{6,7},{7,6},{8,9},{9,8},{10,11... | collective-permute-start | bytes 442376 | tf_op jit(solution)/shard_map/ppermute | solution.py:495
  50.9 4.5 %collective-permute-start.2 = (bf16[32,1024]{1,0:T(8,128)(2,1)S(1)}, bf16[32,1024]{1,0:T(8,128)(2,1)S(1)}, u32[]{:S(2)}, u32[]{:S(2)}) collective-permute-start(bf16[32,1024]{1,0:T(8,128)(2,1)S(1)} %first_rows.1), channel_id=1, source_target_pairs={{8,0},{16,8},{24,16},{28,24},{20,28},{12,20},{4,12},{0,4},{9,1},{1... | collective-permute-start | bytes 196616 | tf_op jit(solution)/shard_map/ppermute | solution.py:496
  52.3 6.0 %collective-permute-start.1 = (f16[576,128]{1,0:T(8,128)(2,1)S(1)}, f16[576,128]{1,0:T(8,128)(2,1)S(1)}, u32[]{:S(2)}, u32[]{:S(2)}) collective-permute-start(f16[576,128]{1,0:T(8,128)(2,1)S(1)} %fusion.1), channel_id=1, source_target_pairs={{0,2},{2,0},{1,3},{3,1},{4,6},{6,4},{5,7},{7,5},{8,10},{10,8},{9,1... | collective-permute-start | bytes 442376 | tf_op jit(solution)/shard_map/ppermute | solution.py:499
  56.2 2.2 %collective-permute-start.3 = (f16[608,128]{1,0:T(8,128)(2,1)S(1)}, f16[608,128]{1,0:T(8,128)(2,1)S(1)}, u32[]{:S(2)}, u32[]{:S(2)}) collective-permute-start(f16[608,128]{1,0:T(8,128)(2,1)S(1)} %pad_maximum_fusion), channel_id=1, source_target_pairs={{0,1},{1,0},{2,3},{3,2},{4,5},{5,4},{6,7},{7,6},{8,9},{9,8},{10,11... | collective-permute-start | bytes 466952 | tf_op jit(solution)/shard_map/ppermute | solution.py:523

commit v12 on v10

--- a/solution.py
+++ b/solution.py
@@ -11,7 +11,7 @@
 LANES = 128
 GROUPS = LANES // CAPS
 ALL = ("dp", "rep")
-FEATURE_STEP = 512
+FEATURE_STEP = 1024
 ROW_STEP = 256
 EMPTY_MARK = 4.0
 PENALTY = -1000.0

time: 69.8 us -> 69.8 us (level)
  no operation moved by 1% of the time
where the time goes in v12:
time: 69.8 us; the launch traced here: 69.6 us
  blocking collectives  54.9 us (79%)
  Pallas kernels  8.38 us (12%)
  waiting for transfers between devices  3.35 us (5%)
  starting transfers between devices  2.61 us (4%)
    all_to_all x1, blocking collectives, local(): got = lax.all_to_all(send, ALL, split_axis=0, concat_axis=0, tiled=True)  45.1 us
    all_to_all x1, blocking collectives, local(): back = lax.all_to_all(sums, ALL, split_axis=0, concat_axis=0, tiled=True)  9.8 us
    pallas_call x1, Pallas kernels, local(): pl.pallas_call(functools.partial(select_kernel, clusters, reps), in_specs...  4.51 us
    ppermute x1, waiting for transfers between devices, local(): far = lax.ppermute(far, 'rep', across)  2.06 us
  transfers between devices with their start and end apart: 4, of which 2 were waited for; matrix products, arithmetic and copies ran while one was open for 0% of the time, Pallas kernels for 2%

profile of v12, /device:TPU:0, one launch (start us, length us, event | category | flops | bytes accessed | tf_op | source)
XLA Modules:
  0.0 69.6 jit_solution(16012744871342775222)
XLA Ops:
  0.0 4.5 %select_rows.1 = (bf16[32,192,128]{2,1,0:T(8,128)(2,1)S(1)}, s32[8,128]{1,0:T(8,128)S(1)}) custom-call(s32[8]{0:T(128)} %cap_in.1, s32[8]{0:T(128)} %adjacent_in.1, s32[8]{0:T(128)} %mask_in.1, s32[8,128]{1,0:T(8,128)} %bitcast.26, bf16[1024,4096]{1,0:T(8,128)(2,1)} %rows.1), custom_call_target="tpu_custom_call" | custom-call | tf_op jit(solution)/shard_map/select_rows/pallas_call | solution.py:438
  4.5 45.1 %all_to_all.10.got = bf16[32,192,128]{2,1,0:T(8,128)(2,1)S(1)} all-to-all(bf16[32,192,128]{2,1,0:T(8,128)(2,1)S(1)} %get-tuple-element.12), channel_id=1, replica_groups=mesh['dp'=8,'rep'=4] {'dp','rep'}, dimensions={0} | all-to-all | bytes 3145728 | tf_op jit(solution)/shard_map/all_to_all | solution.py:463
  49.6 1.0 %gather_far_tiles.1 = (bf16[768,1024]{1,0:T(8,128)(2,1)S(1)}, f32[2,576,128]{2,1,0:T(8,128)S(1)}) custom-call(bf16[32,192,128]{2,1,0:T(8,128)(2,1)S(1)} %all_to_all.10.got), custom_call_target="tpu_custom_call" | custom-call | tf_op jit(solution)/shard_map/gather_far_tiles/pallas_call | solution.py:470
  50.7 0.1 collective-permute-start
  50.8 0.1 first_rows.1
  50.9 1.3 %collective-permute-start.2 = (bf16[32,1024]{1,0:T(8,128)(2,1)S(1)}, bf16[32,1024]{1,0:T(8,128)(2,1)S(1)}, u32[]{:S(2)}, u32[]{:S(2)}) collective-permute-start(bf16[32,1024]{1,0:T(8,128)(2,1)S(1)} %first_rows.1), channel_id=1, source_target_pairs={{8,0},{16,8},{24,16},{28,24},{20,28},{12,20},{4,12},{0,4},{9,1},{1... | collective-permute-start | bytes 196616 | tf_op jit(solution)/shard_map/ppermute | solution.py:496
  52.2 0.0 collective-permute-done
  52.3 1.1 %collective-permute-start.1 = (f16[576,128]{1,0:T(8,128)(2,1)S(1)}, f16[576,128]{1,0:T(8,128)(2,1)S(1)}, u32[]{:S(2)}, u32[]{:S(2)}) collective-permute-start(f16[576,128]{1,0:T(8,128)(2,1)S(1)} %fusion.1), channel_id=1, source_target_pairs={{0,2},{2,0},{1,3},{3,1},{4,6},{6,4},{5,7},{7,5},{8,10},{10,8},{9,1... | collective-permute-start | bytes 442376 | tf_op jit(solution)/shard_map/ppermute | solution.py:499
  53.4 0.7 near_tiles.1
  54.2 1.3 %collective-permute-done.2.edge_x = bf16[32,1024]{1,0:T(8,128)(2,1)S(1)} collective-permute-done((bf16[32,1024]{1,0:T(8,128)(2,1)S(1)}, bf16[32,1024]{1,0:T(8,128)(2,1)S(1)}, u32[]{:S(2)}, u32[]{:S(2)}) %collective-permute-start.2) | collective-permute-done | bytes 65568 | tf_op jit(solution)/shard_map/ppermute | solution.py:496
  55.4 0.7 edge_logits.1
  56.2 0.1 collective-permute-start.3
  56.3 2.1 %collective-permute-done.1 = f16[576,128]{1,0:T(8,128)(2,1)S(1)} collective-permute-done((f16[576,128]{1,0:T(8,128)(2,1)S(1)}, f16[576,128]{1,0:T(8,128)(2,1)S(1)}, u32[]{:S(2)}, u32[]{:S(2)}) %collective-permute-start.1) | collective-permute-done | bytes 147488 | tf_op jit(solution)/shard_map/ppermute | solution.py:499
  58.4 0.0 collective-permute-done.3
  58.4 0.6 score_tiles.1
  59.0 9.8 %all_to_all.11 = f32[32,1,128]{2,1,0:T(1,128)S(1)} all-to-all(f32[32,1,128]{2,1,0:T(1,128)S(1)} %bitcast.24), channel_id=1, replica_groups=mesh['dp'=8,'rep'=4] {'dp','rep'}, dimensions={0} | all-to-all | bytes 32768 | tf_op jit(solution)/shard_map/all_to_all | solution.py:538
  68.8 0.8 %final_keep.1 = f32[8,128]{1,0:T(8,128)} custom-call(s32[8,128]{1,0:T(8,128)S(1)} %get-tuple-element.11.slots, f32[32,128]{1,0:T(8,128)S(1)} %bitcast.25), custom_call_target="tpu_custom_call" | custom-call | tf_op jit(solution)/shard_map/final_keep/pallas_call | solution.py:539
  (8 shorter events, 0.2 us)
Async XLA Ops:
  50.7 1.5 %collective-permute-start = (f16[576,128]{1,0:T(8,128)(2,1)S(1)}, f16[576,128]{1,0:T(8,128)(2,1)S(1)}, u32[]{:S(2)}, u32[]{:S(2)}) collective-permute-start(f16[576,128]{1,0:T(8,128)(2,1)S(1)} %fusion.2), channel_id=1, source_target_pairs={{0,1},{1,0},{2,3},{3,2},{4,5},{5,4},{6,7},{7,6},{8,9},{9,8},{10,11... | collective-permute-start | bytes 442376 | tf_op jit(solution)/shard_map/ppermute | solution.py:495
  50.9 4.5 %collective-permute-start.2 = (bf16[32,1024]{1,0:T(8,128)(2,1)S(1)}, bf16[32,1024]{1,0:T(8,128)(2,1)S(1)}, u32[]{:S(2)}, u32[]{:S(2)}) collective-permute-start(bf16[32,1024]{1,0:T(8,128)(2,1)S(1)} %first_rows.1), channel_id=1, source_target_pairs={{8,0},{16,8},{24,16},{28,24},{20,28},{12,20},{4,12},{0,4},{9,1},{1... | collective-permute-start | bytes 196616 | tf_op jit(solution)/shard_map/ppermute | solution.py:496
  52.3 6.0 %collective-permute-start.1 = (f16[576,128]{1,0:T(8,128)(2,1)S(1)}, f16[576,128]{1,0:T(8,128)(2,1)S(1)}, u32[]{:S(2)}, u32[]{:S(2)}) collective-permute-start(f16[576,128]{1,0:T(8,128)(2,1)S(1)} %fusion.1), channel_id=1, source_target_pairs={{0,2},{2,0},{1,3},{3,1},{4,6},{6,4},{5,7},{7,5},{8,10},{10,8},{9,1... | collective-permute-start | bytes 442376 | tf_op jit(solution)/shard_map/ppermute | solution.py:499
  56.2 2.2 %collective-permute-start.3 = (f16[608,128]{1,0:T(8,128)(2,1)S(1)}, f16[608,128]{1,0:T(8,128)(2,1)S(1)}, u32[]{:S(2)}, u32[]{:S(2)}) collective-permute-start(f16[608,128]{1,0:T(8,128)(2,1)S(1)} %pad_maximum_fusion), channel_id=1, source_target_pairs={{0,1},{1,0},{2,3},{3,2},{4,5},{5,4},{6,7},{7,6},{8,9},{9,8},{10,11... | collective-permute-start | bytes 466952 | tf_op jit(solution)/shard_map/ppermute | solution.py:523
